TPU v7x, 32 devices: a whole 2x2x4 slice. The times are simulated.
32 devices in a mesh: blk: 8 (over z, core), group: 4 (over y, x).
Axes of the slice: x: 2, y: 2, z: 4, core: 2. Of those that a mesh axis runs over, the one named last changes fastest.
Arguments:
- img_feat: bfloat16 [4096, 3072], P(('blk', 'group')), may hold values from -0.375 to 0.375
- head_weight: bfloat16 [3072, 512], replicated, may hold values from -1 to 3
- text_emb: bfloat16 [4096, 512], P(('blk', 'group')), may hold values from -0.375 to 0.375
- natural_exponent_factor: float32 [1], replicated, may hold values from 1.6 to 2
- bias: float32 [1], replicated, may hold values from -3.5 to -2.5
Outputs:
- d_feat: float32 [4096, 3072], P(('blk', 'group'))
- d_text: float32 [4096, 512], P(('blk', 'group'))
All inputs are finite; a program needn't handle non-finite values.
Results may differ from a plain program's by a relative error of at most 0.005.
Values may be sent and summed in bfloat16 or wider, within the bound.
No kernel may reach another device: no remote copies, remote signals or barrier semaphores. Data moves between devices by JAX's collectives and lax.ppermute only.
A program may use at most 64 MiB of HBM per device.

v0:
```python
import jax
import jax.numpy as jnp
from jax import lax
from jax.sharding import PartitionSpec as P

STEPS = 2


EPS = 1e-06


def passed_along(block, axis, distance):
    devices = range(lax.axis_size(axis))
    route = [((i - distance) % len(devices), i) for i in devices]
    return lax.ppermute(block, axis, route)


def to_unit(values):
    inverse = lax.rsqrt(jnp.sum(values * values, axis=-1, keepdims=True) + EPS)
    return (values * inverse, inverse)


def unit_back(grad_in, unit_rows, inverse):
    return (grad_in - unit_rows * jnp.sum(unit_rows * grad_in, axis=-1, keepdims=True)) * inverse


def body(img_feat, head_weight, text_emb, natural_exponent_factor, bias):
    similarity_multiplier = jnp.exp(natural_exponent_factor[0])
    partner_offset = bias[0]
    projected = jnp.dot(img_feat, head_weight, preferred_element_type=jnp.float32)
    img_unit, img_inv = to_unit(projected)
    img_low = img_unit.astype(jnp.bfloat16)
    txt_unit, txt_inv = to_unit(text_emb.astype(jnp.float32))
    text_piece = txt_unit.astype(jnp.bfloat16)
    row_count = img_feat.shape[0]
    emb_width = text_emb.shape[1]
    panel_rows = row_count * lax.axis_size("group")
    own_slot = lax.axis_index("group") * row_count
    row_ids = lax.broadcasted_iota(jnp.int32, (row_count, 1), 0)
    contract_last = (((1,), (1,)), ((), ()))
    contract_first = (((0,), (0,)), ((), ()))
    images = lax.all_gather(img_low, "group", axis=0, tiled=True)
    image_ids = lax.broadcasted_iota(jnp.int32, (panel_rows, 1), 0)
    piece_ids = lax.broadcasted_iota(jnp.int32, (1, row_count), 1)
    grad_img = jnp.zeros((row_count, emb_width), jnp.float32)
    grad_txt = jnp.zeros((row_count, emb_width), jnp.float32)
    for loop_step in range(STEPS):
        pos_weight = 1.0 if loop_step == 0 else 0.0
        block_rows = lax.all_gather(text_piece, "group", axis=0, tiled=True)
        block_size = block_rows.shape[0]
        matched_similarity_matrix = (
            similarity_multiplier
            * lax.dot_general(
                img_low, block_rows, contract_last, preferred_element_type=jnp.float32
            )
            + partner_offset
        )
        col_ids = lax.broadcasted_iota(jnp.int32, (1, block_size), 1)
        positive = jnp.where(col_ids == own_slot + row_ids, pos_weight, 0.0)
        weights_low = (jax.nn.sigmoid(matched_similarity_matrix) - positive).astype(jnp.bfloat16)
        round_derivative_part = similarity_multiplier * jnp.dot(
            weights_low, block_rows, preferred_element_type=jnp.float32
        )
        own_rows = text_piece
        grad_img = grad_img + round_derivative_part
        matched_similarity_matrix = (
            similarity_multiplier
            * lax.dot_general(images, own_rows, contract_last, preferred_element_type=jnp.float32)
            + partner_offset
        )
        positive = jnp.where(image_ids == own_slot + piece_ids, pos_weight, 0.0)
        weights_low = (jax.nn.sigmoid(matched_similarity_matrix) - positive).astype(jnp.bfloat16)
        caption_share = similarity_multiplier * lax.dot_general(
            weights_low, images, contract_first, preferred_element_type=jnp.float32
        )
        if loop_step > 0:
            caption_share = passed_along(
                caption_share.astype(jnp.bfloat16), "blk", -loop_step
            ).astype(caption_share.dtype)
        grad_txt = grad_txt + caption_share
        if loop_step + 1 < STEPS:
            text_piece = passed_along(text_piece, "blk", 1)
    img_back = unit_back(grad_img, img_unit, img_inv).astype(jnp.bfloat16)
    d_feat = lax.dot_general(
        img_back, head_weight, contract_last, preferred_element_type=jnp.float32
    )
    d_text = unit_back(grad_txt, txt_unit, txt_inv)
    return (d_feat, d_text)


def solution(mesh):
    return jax.shard_map(
        body,
        mesh=mesh,
        in_specs=(P(("blk", "group"), None), P(), P(("blk", "group"), None), P(), P()),
        out_specs=(P(("blk", "group"), None), P(("blk", "group"), None)),
        check_vma=False,
    )
```

profile of v0, /device:TPU:0, one launch (start us, length us, event | category | flops | bytes accessed | tf_op | source)
XLA Modules:
  0.0 57.9 jit_solution(11161386973851490509)
XLA Ops:
  0.6 0.0 copy-start
  0.6 1.2 %fusion.35 = f32[128]{0:T(128)S(1)} fusion(bf16[128,512]{1,0:T(8,128)(2,1)} %param.7), kind=kLoop, calls=%fused_computation.44 | loop fusion | flops 196480 | bytes 131584 | tf_op jit(solution)/shard_map/reduce_sum | solution.py:19
  1.8 1.0 %fusion.31 = bf16[128,512]{1,0:T(8,128)(2,1)S(1)} fusion(bf16[128,512]{1,0:T(8,128)(2,1)} %param.7, f32[128]{0:T(128)S(1)} %add_rsqrt_fusion), kind=kLoop, calls=%fused_computation.40 | loop fusion | flops 196608 | bytes 262656 | tf_op jit(solution)/shard_map/convert_element_type | solution.py:34
  2.8 0.5 collective-permute-start
  3.3 13.1 %all_gather.9 = bf16[512,512]{1,0:T(8,128)(2,1)} all-gather(bf16[128,512]{1,0:T(8,128)(2,1)S(1)} %fusion.31), channel_id=1, replica_groups=mesh['blk'=8,'group'=4] {'group'}, dimensions={0}, use_global_device_ids=true | all-gather | bytes 655360 | tf_op jit(solution)/shard_map/all_gather | solution.py:49
  17.8 0.0 copy-done
  17.8 1.8 %multiply_reduce_fusion.1 = (f32[128]{0:T(128)S(1)}, f32[128,512]{1,0:T(8,128)S(1)}) fusion(bf16[128,3072]{1,0:T(8,128)(2,1)} %param.5, bf16[3072,512]{1,0:T(8,128)(2,1)S(1)} %copy-done), kind=kOutput, calls=%fused_computation.52 | convolution fusion | flops 402784128 | bytes 4194816 | tf_op jit(solution)/shard_map/dot_general | solution.py:30
  19.6 0.8 %multiply_convert_fusion.1 = bf16[128,512]{1,0:T(8,128)(2,1)} fusion(f32[128,512]{1,0:T(8,128)S(1)} %get-tuple-element.3, f32[128]{0:T(128)S(1)} %add_rsqrt_fusion.1), kind=kLoop, calls=%fused_computation.53 | loop fusion | flops 131072 | bytes 393728 | tf_op jit(solution)/shard_map/convert_element_type | solution.py:32
  20.3 2.5 %fusion.28 = f32[128,512]{1,0:T(8,128)} fusion(bf16[512,512]{1,0:T(8,128)(2,1)} %all_gather.9, bf16[128,512]{1,0:T(8,128)(2,1)} %multiply_convert_fusion.1, s32[128]{0:T(128)S(1)} %iota_add_fusion, f32[]{:T(128)} %bitcast.16, f32[]{:T(128)} %bitcast), kind=kOutput, calls=%fused_computation.35 | convolution fusion | flops 134807552 | bytes 918024 | tf_op jit(solution)/shard_map/dot_general | solution.py:61
  22.8 11.1 %all_gather.11 = bf16[512,512]{1,0:T(8,128)(2,1)} all-gather(bf16[128,512]{1,0:T(8,128)(2,1)} %multiply_convert_fusion.1), channel_id=1, replica_groups=mesh['blk'=8,'group'=4] {'group'}, dimensions={0}, use_global_device_ids=true | all-gather | bytes 655360 | tf_op jit(solution)/shard_map/all_gather | solution.py:42
  33.9 0.0 collective-permute-done
  34.0 2.5 %fusion.23 = bf16[128,512]{1,0:T(8,128)(2,1)} fusion(bf16[512,512]{1,0:T(8,128)(2,1)} %all_gather.11, bf16[128,512]{1,0:T(8,128)(2,1)} %collective-permute-done, f32[]{:T(128)} %bitcast.18, f32[]{:T(128)} %bitcast), kind=kOutput, calls=%fused_computation.30 | convolution fusion | flops 134742016 | bytes 786440 | tf_op jit(solution)/shard_map/dot_general | solution.py:73
  36.5 0.0 collective-permute-start.1
  36.5 11.9 %all_gather.10 = bf16[512,512]{1,0:T(8,128)(2,1)} all-gather(bf16[128,512]{1,0:T(8,128)(2,1)} %collective-permute-done), channel_id=1, replica_groups=mesh['blk'=8,'group'=4] {'group'}, dimensions={0}, use_global_device_ids=true | all-gather | bytes 655360 | tf_op jit(solution)/shard_map/all_gather | solution.py:49
  48.4 2.6 %multiply_reduce_fusion = (f32[128]{0:T(128)S(1)}, f32[128,512]{1,0:T(8,128)}) fusion(f32[128,512]{1,0:T(8,128)S(1)} %get-tuple-element.3, f32[128]{0:T(128)S(1)} %add_rsqrt_fusion.1, f32[]{:T(128)} %bitcast, f32[128,512]{1,0:T(8,128)} %fusion.28, bf16[512,512]{1,0:T(8,128)(2,1)} %all_gather.10, bf16[128,512]{1,0:T(8,128)(2,1)} %multiply_convert_fusion.1, ...), kind=kOutput, calls=%fused_computation.49 | convolution fusion | flops 134938496 | bytes 1442824 | tf_op jit(solution)/shard_map/dot_general | solution.py:61
  50.9 0.0 copy-start.1
  50.9 3.3 %fusion.38 = f32[128,3072]{1,0:T(8,128)} fusion(bf16[3072,512]{1,0:T(8,128)(2,1)S(1)} %copy-done, f32[128,512]{1,0:T(8,128)} %get-tuple-element.5, f32[128,512]{1,0:T(8,128)S(1)} %get-tuple-element.3, f32[128]{0:T(128)S(1)} %get-tuple-element.4, f32[128]{0:T(128)S(1)} %add_rsqrt_fusion.1), kind=kOutput, calls=%fused_computation.54 | convolution fusion | flops 402980864 | bytes 5243904 | tf_op jit(solution)/shard_map/dot_general | solution.py:84
  54.2 0.0 collective-permute-done.1
  54.2 0.0 copy-done.1
  54.2 2.0 %fusion.32 = (f32[128]{0:T(128)S(1)}, f32[128,512]{1,0:T(8,128)S(1)}) fusion(bf16[128,512]{1,0:T(8,128)(2,1)S(1)} %copy-done.1, bf16[128,512]{1,0:T(8,128)(2,1)} %collective-permute-done.1, f32[128]{0:T(128)S(1)} %add_rsqrt_fusion, bf16[512,512]{1,0:T(8,128)(2,1)} %all_gather.11, s32[128]{0:T(128)S(1)} %iota_add_fusion, f32[]{:T(128)} %bitcast.17, f32[]{:T(128)} %bitcast), kind=kOutput, calls=%fused_computation.41 | convolution fusion | flops 135462784 | bytes 1050120 | tf_op jit(solution)/shard_map/dot_general | solution.py:73
  56.2 1.7 %fusion.34 = f32[128,512]{1,0:T(8,128)} fusion(bf16[128,512]{1,0:T(8,128)(2,1)S(1)} %copy-done.1, f32[128,512]{1,0:T(8,128)S(1)} %get-tuple-element.7, bf16[128,512]{1,0:T(8,128)(2,1)} %collective-permute-done.1, f32[128]{0:T(128)S(1)} %get-tuple-element.6, f32[128]{0:T(128)S(1)} %add_rsqrt_fusion), kind=kLoop, calls=%fused_computation.43 | loop fusion | flops 458752 | bytes 787456 | tf_op jit(solution)/shard_map/mul | solution.py:24
  (3 shorter events, 0.0 us)
Async XLA Ops:
  0.6 17.1 %copy-start = (bf16[3072,512]{1,0:T(8,128)(2,1)S(1)}, bf16[3072,512]{1,0:T(8,128)(2,1)}, u32[]{:S(2)}) copy-start(bf16[3072,512]{1,0:T(8,128)(2,1)} %param.6) | copy-start | bytes 9437188
  2.8 31.1 %collective-permute-start = (bf16[128,512]{1,0:T(8,128)(2,1)S(1)}, bf16[128,512]{1,0:T(8,128)(2,1)}, u32[]{:S(2)}, u32[]{:S(2)}) collective-permute-start(bf16[128,512]{1,0:T(8,128)(2,1)S(1)} %fusion.31), channel_id=1, source_target_pairs={{28,0},{0,4},{4,8},{8,12},{12,16},{16,20},{20,24},{24,28},{29,1},{... | collective-permute-start | bytes 393224 | tf_op jit(solution)/shard_map/ppermute | solution.py:15
  36.5 17.7 %collective-permute-start.1 = (bf16[128,512]{1,0:T(8,128)(2,1)}, bf16[128,512]{1,0:T(8,128)(2,1)}, u32[]{:S(2)}, u32[]{:S(2)}) collective-permute-start(bf16[128,512]{1,0:T(8,128)(2,1)} %fusion.23), channel_id=1, source_target_pairs={{4,0},{8,4},{12,8},{16,12},{20,16},{24,20},{28,24},{0,28},{5,1},{9... | collective-permute-start | bytes 393224 | tf_op jit(solution)/shard_map/ppermute | solution.py:15
  50.9 3.3 %copy-start.1 = (bf16[128,512]{1,0:T(8,128)(2,1)S(1)}, bf16[128,512]{1,0:T(8,128)(2,1)}, u32[]{:S(2)}) copy-start(bf16[128,512]{1,0:T(8,128)(2,1)} %param.7) | copy-start | bytes 393220
where the time goes:
time: 58.3 us; the launch traced here: 57.9 us
  blocking collectives  36.1 us (62%)
  matrix products  14.6 us (25%)
  other arithmetic  4.67 us (8%)
  between operations  2.03 us (3%)
    all_gather x2, blocking collectives, body(): block_rows = lax.all_gather(text_piece, 'group', axis=0, tiled=True)  25 us
    all_gather x1, blocking collectives, body(): images = lax.all_gather(img_low, 'group', axis=0, tiled=True)  11.1 us
    dot_general x2, matrix products, body(): jnp.dot(weights_low, block_rows, preferred_element_type=jnp.float32)  5.04 us
    dot_general x2, matrix products, body(): lax.dot_general(weights_low, images, contract_first, preferred_element_ty...  4.5 us
    dot_general x1, matrix products, body(): lax.dot_general(img_back, head_weight, contract_last, preferred_element_t...  3.29 us
    dot_general x1, matrix products, body(): jnp.dot(img_feat, head_weight, preferred_element_type=jnp.float32)  1.8 us
    mul x1, other arithmetic, unit_back(): (grad_in - unit_rows * jnp.sum(unit_rows * grad_in, axis=-1, keepdims=Tru...  1.74 us
  transfers between devices with their start and end apart: 2, of which 0 were waited for; matrix products, arithmetic and copies ran while one was open for 19% of the time, Pallas kernels for 0%

commit v1 on v0

v1 whole, which is shorter than its diff:
```python
import functools

import jax
import jax.numpy as jnp
from jax import lax
from jax.experimental import pallas as pl
from jax.experimental.pallas import tpu as pltpu
from jax.sharding import PartitionSpec as P

EPS = 1e-06
F32 = jnp.float32
BF16 = jnp.bfloat16
CONTRACT_LAST = (((1,), (1,)), ((), ()))
VMEM = pl.BlockSpec(memory_space=pltpu.VMEM)
SMEM = pl.BlockSpec(memory_space=pltpu.SMEM)


def to_unit(values):
    inverse = lax.rsqrt(jnp.sum(values * values, axis=-1, keepdims=True) + EPS)
    return values * inverse, inverse


def unit_back(grad_in, unit_rows, inverse):
    return (grad_in - unit_rows * jnp.sum(unit_rows * grad_in, axis=-1, keepdims=True)) * inverse


def project_kernel(img_ref, head_ref, unit_ref, inv_ref, low_ref):
    projected = jnp.dot(img_ref[...], head_ref[...], preferred_element_type=F32)
    unit, inverse = to_unit(projected)
    unit_ref[...] = unit
    inv_ref[...] = inverse
    low_ref[...] = unit.astype(BF16)


def meet(scale, bias, left, right, rows):
    z = scale * lax.dot_general(left, right, CONTRACT_LAST, preferred_element_type=F32) + bias
    row_ids = lax.broadcasted_iota(jnp.int32, z.shape, 0)
    col_ids = lax.broadcasted_iota(jnp.int32, z.shape, 1)
    positive = jnp.where((row_ids == col_ids) & (row_ids < rows), 1.0, 0.0)
    weight = (1.0 / (1.0 + jnp.exp(-z)) - positive).astype(BF16)
    return scale * jnp.dot(weight, right, preferred_element_type=F32)


def image_kernel(factor_ref, bias_ref, own_ref, visit_ref, *refs):
    text_refs, (grad_ref, back_ref) = refs[:-2], refs[-2:]
    rows = own_ref.shape[0]
    texts = jnp.concatenate([to_unit(ref[...].astype(F32))[0].astype(BF16) for ref in text_refs], axis=0)
    left = jnp.concatenate([own_ref[...], visit_ref[...]], axis=0)
    scale = jnp.exp(jnp.full((1, 1), factor_ref[0], F32))
    grad = meet(scale, bias_ref[0], left, texts, rows)
    grad_ref[...] = grad[:rows]
    back_ref[...] = grad[rows:].astype(BF16)


def text_kernel(factor_ref, bias_ref, own_ref, visit_ref, *refs):
    image_refs, (grad_ref, back_ref) = refs[:-2], refs[-2:]
    rows = own_ref.shape[0]
    images = jnp.concatenate([ref[...] for ref in image_refs], axis=0)
    left = jnp.concatenate(
        [to_unit(ref[...].astype(F32))[0].astype(BF16) for ref in (own_ref, visit_ref)], axis=0
    )
    scale = jnp.exp(jnp.full((1, 1), factor_ref[0], F32))
    grad = meet(scale, bias_ref[0], left, images, rows)
    grad_ref[...] = grad[:rows]
    back_ref[...] = grad[rows:].astype(BF16)


def feat_kernel(grad_ref, back_ref, unit_ref, inv_ref, head_ref, out_ref, low_ref):
    @pl.when(pl.program_id(0) == 0)
    def _():
        grad = grad_ref[...] + back_ref[...].astype(F32)
        low_ref[...] = unit_back(grad, unit_ref[...], inv_ref[...]).astype(BF16)

    out_ref[...] = lax.dot_general(low_ref[...], head_ref[...], CONTRACT_LAST, preferred_element_type=F32)


def text_out_kernel(grad_ref, back_ref, text_ref, out_ref):
    unit, inverse = to_unit(text_ref[...].astype(F32))
    out_ref[...] = unit_back(grad_ref[...] + back_ref[...].astype(F32), unit, inverse)


def body(img_feat, head_weight, text_emb, natural_exponent_factor, bias):
    rows, width = img_feat.shape
    emb = text_emb.shape[1]
    n_blk, n_group = lax.axis_size("blk"), lax.axis_size("group")
    shape = jax.ShapeDtypeStruct
    sub = functools.partial(pl.pallas_call)

    def to_peer(piece, k):
        if n_group & (n_group - 1) == 0:
            route = [(i, i ^ k) for i in range(n_group)]
        else:
            route = [(i, (i + k) % n_group) for i in range(n_group)]
        return lax.ppermute(piece, "group", route)

    def to_block(piece, distance):
        return lax.ppermute(piece, "blk", [(i, (i + distance) % n_blk) for i in range(n_blk)])

    texts = [text_emb] + [to_peer(text_emb, k) for k in range(1, n_group)]
    text_visit = to_block(text_emb, 1)

    img_unit, img_inv, img_low = sub(
        project_kernel,
        out_shape=(shape((rows, emb), F32), shape((rows, 1), F32), shape((rows, emb), BF16)),
        in_specs=[VMEM] * 2,
        out_specs=(VMEM,) * 3,
    )(img_feat, head_weight)

    img_visit = to_block(img_low, -1)
    images = [img_low] + [to_peer(img_low, k) for k in range(1, n_group)]

    pair = (shape((rows, emb), F32), shape((rows, emb), BF16))
    grad_img, img_return = sub(
        image_kernel,
        out_shape=pair,
        in_specs=[SMEM] * 2 + [VMEM] * (2 + n_group),
        out_specs=(VMEM,) * 2,
    )(natural_exponent_factor, bias, img_low, img_visit, *texts)
    img_back = to_block(img_return, 1)

    grad_txt, txt_return = sub(
        text_kernel,
        out_shape=pair,
        in_specs=[SMEM] * 2 + [VMEM] * (2 + n_group),
        out_specs=(VMEM,) * 2,
    )(natural_exponent_factor, bias, text_emb, text_visit, *images)
    txt_back = to_block(txt_return, -1)

    tile = 768 if width % 768 == 0 else width
    whole = lambda *dims: pl.BlockSpec(dims, lambda j: (0, 0))
    d_feat = sub(
        feat_kernel,
        grid=(width // tile,),
        out_shape=shape((rows, width), F32),
        in_specs=[
            whole(rows, emb),
            whole(rows, emb),
            whole(rows, emb),
            whole(rows, 1),
            pl.BlockSpec((tile, emb), lambda j: (j, 0)),
        ],
        out_specs=pl.BlockSpec((rows, tile), lambda j: (0, j)),
        scratch_shapes=[pltpu.VMEM((rows, emb), BF16)],
    )(grad_img, img_back, img_unit, img_inv, head_weight)

    d_text = sub(
        text_out_kernel, out_shape=shape((rows, emb), F32), in_specs=[VMEM] * 3, out_specs=VMEM
    )(grad_txt, txt_back, text_emb)
    return d_feat, d_text


def solution(mesh):
    return jax.shard_map(
        body,
        mesh=mesh,
        in_specs=(P(("blk", "group"), None), P(), P(("blk", "group"), None), P(), P()),
        out_specs=(P(("blk", "group"), None), P(("blk", "group"), None)),
        check_vma=False,
    )
```

time: 58.3 us -> 40.9 us (0.70)
  blocking collectives: 36.1 us -> 0 us
  Pallas kernels: 0 us -> 15.6 us
  matrix products: 14.6 us -> 0 us
  starting transfers between devices: 0.51 us -> 14.5 us
  waiting for transfers between devices: 0.01 us -> 5.17 us
  other arithmetic: 4.67 us -> 0 us
  local copies, waits for them, and re-layouts: 0.01 us -> 3.35 us
    all_gather x3 -> x0, blocking collectives: 36.1 us -> none  [the longest x2 25 us: body(): block_rows = lax.all_gather(text_piece, 'group', axis=0, tiled=True)]
    pallas_call x0 -> x5, Pallas kernels: none -> 15.6 us  [the longest x1 4.91 us: body(): sub(feat_kernel, grid=(width // tile,), out_shape=shape((rows, width), F3...]
    dot_general x6 -> x0, matrix products: 14.6 us -> none  [the longest x2 5.04 us: body(): jnp.dot(weights_low, block_rows, preferred_element_type=jnp.float32)]
    ppermute x2 -> x10, starting transfers between devices: 0.51 us -> 14.5 us  [the longest x6 9.4 us: to_peer(): return lax.ppermute(piece, 'group', route)]
    ppermute x2 -> x10, waiting for transfers between devices: 0.01 us -> 5.17 us  [the longest x4 3.79 us: to_block(): lax.ppermute(piece, 'blk', [(i, (i + distance) % n_blk) for i in range(n_...]
    unnamed x4 -> x22, local copies, waits for them, and re-layouts: 0.01 us -> 3.35 us
    convert_element_type x2 -> x0, other arithmetic: 1.75 us -> none  [the longest x1 1 us: body(): text_piece = txt_unit.astype(jnp.bfloat16)]
    mul x1 -> x0, other arithmetic: 1.74 us -> none  [unit_back(): (grad_in - unit_rows * jnp.sum(unit_rows * grad_in, axis=-1, keepdims=Tru...]
  transfers between devices with their start and end apart: 2 -> 10, of which waited for: 0 -> 2; matrix products, arithmetic and copies ran while one was open for 19% -> 0% of each run, Pallas kernels for 0% -> 26%
where the time goes in v1:
time: 40.9 us; the launch traced here: 40.6 us
  Pallas kernels  15.6 us (38%)
  starting transfers between devices  14.5 us (35%)
  waiting for transfers between devices  5.17 us (13%)
  local copies, waits for them, and re-layouts  3.35 us (8%)
  between operations  2.04 us (5%)
    ppermute x6, starting transfers between devices, to_peer(): return lax.ppermute(piece, 'group', route)  9.4 us
    ppermute x4, starting transfers between devices, to_block(): lax.ppermute(piece, 'blk', [(i, (i + distance) % n_blk) for i in range(n_...  5.05 us
    pallas_call x1, Pallas kernels, body(): sub(feat_kernel, grid=(width // tile,), out_shape=shape((rows, width), F3...  4.91 us
    ppermute x4, waiting for transfers between devices, to_block(): lax.ppermute(piece, 'blk', [(i, (i + distance) % n_blk) for i in range(n_...  3.79 us
    pallas_call x1, Pallas kernels, body(): sub(project_kernel, out_shape=(shape((rows, emb), F32), shape((rows, 1),...  3.57 us
    unnamed x22, local copies, waits for them, and re-layouts  3.35 us
    pallas_call x1, Pallas kernels, body(): sub(image_kernel, out_shape=pair, in_specs=[SMEM] * 2 + [VMEM] * (2 + n_g...  2.62 us
    pallas_call x1, Pallas kernels, body(): sub(text_kernel, out_shape=pair, in_specs=[SMEM] * 2 + [VMEM] * (2 + n_gr...  2.57 us
  transfers between devices with their start and end apart: 10, of which 2 were waited for; matrix products, arithmetic and copies ran while one was open for 0% of the time, Pallas kernels for 26%

profile of v1, /device:TPU:0, one launch (start us, length us, event | category | flops | bytes accessed | tf_op | source)
XLA Modules:
  0.0 40.6 jit_solution(11665222543355106400)
XLA Ops:
  0.6 0.0 copy-start
  0.6 0.5 %collective-permute-start.5 = (bf16[128,512]{1,0:T(8,128)(2,1)}, bf16[128,512]{1,0:T(8,128)(2,1)S(1)}, u32[]{:S(2)}, u32[]{:S(2)}) collective-permute-start(bf16[128,512]{1,0:T(8,128)(2,1)} %text_ref.1), channel_id=1, source_target_pairs={{0,4},{4,8},{8,12},{12,16},{16,20},{20,24},{24,28},{28,0},{1,5},{5... | collective-permute-start | bytes 393224 | tf_op jit(solution)/shard_map/ppermute | solution.py:97
  1.1 3.6 %shard_map.68 = (f32[128,512]{1,0:T(8,128)}, f32[128,1]{1,0:T(8,128)}, bf16[128,512]{1,0:T(8,128)(2,1)}) custom-call(bf16[128,3072]{1,0:T(8,128)(2,1)} %img_ref.1, bf16[3072,512]{1,0:T(8,128)(2,1)} %head_ref.3), custom_call_target="tpu_custom_call" | custom-call | tf_op jit(solution)/shard_map/pallas_call | solution.py:102
  4.7 3.5 %collective-permute-start.8 = (bf16[128,512]{1,0:T(8,128)(2,1)}, bf16[128,512]{1,0:T(8,128)(2,1)S(1)}, u32[]{:S(2)}, u32[]{:S(2)}) collective-permute-start(bf16[128,512]{1,0:T(8,128)(2,1)} %get-tuple-element.9.own_ref.refs_0_), channel_id=1, source_target_pairs={{0,3},{1,2},{2,1},{3,0},{4,7},{5,6},{6,5},{7,4},{8,11},{9,10},{10,... | collective-permute-start | bytes 393224 | tf_op jit(solution)/shard_map/ppermute | solution.py:94
  8.2 0.5 %collective-permute-start.7 = (bf16[128,512]{1,0:T(8,128)(2,1)}, bf16[128,512]{1,0:T(8,128)(2,1)S(1)}, u32[]{:S(2)}, u32[]{:S(2)}) collective-permute-start(bf16[128,512]{1,0:T(8,128)(2,1)} %get-tuple-element.9.own_ref.refs_0_), channel_id=1, source_target_pairs={{0,2},{1,3},{2,0},{3,1},{4,6},{5,7},{6,4},{7,5},{8,10},{9,11},{10,... | collective-permute-start | bytes 393224 | tf_op jit(solution)/shard_map/ppermute | solution.py:94
  8.7 0.1 collective-permute-start.6
  8.7 0.0 copy-done
  8.7 2.9 %collective-permute-start.3 = (bf16[128,512]{1,0:T(8,128)(2,1)S(1)}, bf16[128,512]{1,0:T(8,128)(2,1)S(1)}, u32[]{:S(2)}, u32[]{:S(2)}) collective-permute-start(bf16[128,512]{1,0:T(8,128)(2,1)S(1)} %copy-done), channel_id=1, source_target_pairs={{0,3},{1,2},{2,1},{3,0},{4,7},{5,6},{6,5},{7,4},{8,11},{9,10},{10,... | collective-permute-start | bytes 393224 | tf_op jit(solution)/shard_map/ppermute | solution.py:94
  11.7 0.0 collective-permute-done.5.visit_ref
  11.7 0.0 copy-start.3
  11.7 0.5 %collective-permute-start.2 = (bf16[128,512]{1,0:T(8,128)(2,1)S(1)}, bf16[128,512]{1,0:T(8,128)(2,1)S(1)}, u32[]{:S(2)}, u32[]{:S(2)}) collective-permute-start(bf16[128,512]{1,0:T(8,128)(2,1)S(1)} %copy-done), channel_id=1, source_target_pairs={{0,2},{1,3},{2,0},{3,1},{4,6},{5,7},{6,4},{7,5},{8,10},{9,11},{10,... | collective-permute-start | bytes 393224 | tf_op jit(solution)/shard_map/ppermute | solution.py:94
  12.2 0.0 collective-permute-done.8.refs_3_
  12.2 0.0 copy-start.5
  12.2 2.0 %collective-permute-start.1 = (bf16[128,512]{1,0:T(8,128)(2,1)S(1)}, bf16[128,512]{1,0:T(8,128)(2,1)S(1)}, u32[]{:S(2)}, u32[]{:S(2)}) collective-permute-start(bf16[128,512]{1,0:T(8,128)(2,1)S(1)} %copy-done), channel_id=1, source_target_pairs={{0,1},{1,0},{2,3},{3,2},{4,5},{5,4},{6,7},{7,6},{8,9},{9,8},{10,11... | collective-permute-start | bytes 393224 | tf_op jit(solution)/shard_map/ppermute | solution.py:94
  14.1 1.4 %collective-permute-done.7.refs_2_ = bf16[128,512]{1,0:T(8,128)(2,1)S(1)} collective-permute-done((bf16[128,512]{1,0:T(8,128)(2,1)}, bf16[128,512]{1,0:T(8,128)(2,1)S(1)}, u32[]{:S(2)}, u32[]{:S(2)}) %collective-permute-start.7) | collective-permute-done | bytes 131104 | tf_op jit(solution)/shard_map/ppermute | solution.py:94
  15.5 0.0 copy-start.7
  15.5 3.9 %collective-permute-start = (bf16[128,512]{1,0:T(8,128)(2,1)}, bf16[128,512]{1,0:T(8,128)(2,1)S(1)}, u32[]{:S(2)}, u32[]{:S(2)}) collective-permute-start(bf16[128,512]{1,0:T(8,128)(2,1)} %get-tuple-element.9.own_ref.refs_0_), channel_id=1, source_target_pairs={{0,28},{4,0},{8,4},{12,8},{16,12},{20,16},{24,20},{28,24},{1,29},{... | collective-permute-start | bytes 393224 | tf_op jit(solution)/shard_map/ppermute | solution.py:97
  20.7 0.0 collective-permute-done.6.refs_1_
  20.7 0.0 copy-done.3
  20.7 0.0 copy-done.5
  20.7 0.0 copy-done.7
  20.7 0.0 copy-start.8
  20.7 0.6 %copy-done.8 = bf16[128,512]{1,0:T(8,128)(2,1)} copy-done((bf16[128,512]{1,0:T(8,128)(2,1)}, bf16[128,512]{1,0:T(8,128)(2,1)S(1)}, u32[]{:S(2)}) %copy-start.8) | copy-done | bytes 131096
  21.4 2.6 %shard_map.71 = (f32[128,512]{1,0:T(8,128)}, bf16[128,512]{1,0:T(8,128)(2,1)}) custom-call(f32[1]{0:T(128)S(6)} %copy.7.factor_ref, f32[1]{0:T(128)S(6)} %copy.8.bias_ref, bf16[128,512]{1,0:T(8,128)(2,1)} %text_ref.1, bf16[128,512]{1,0:T(8,128)(2,1)} %copy-done.3, bf16[128,512]{1,0:T(8,128)(2,1)} %get-tuple-element.9.own_ref.refs_0_, ...), custom_call_target="tpu_custom_call" | custom-call | tf_op jit(solution)/shard_map/pallas_call | solution.py:121
  24.0 0.7 %collective-permute-start.9 = (bf16[128,512]{1,0:T(8,128)(2,1)}, bf16[128,512]{1,0:T(8,128)(2,1)S(1)}, u32[]{:S(2)}, u32[]{:S(2)}) collective-permute-start(bf16[128,512]{1,0:T(8,128)(2,1)} %get-tuple-element.15), channel_id=1, source_target_pairs={{0,28},{4,0},{8,4},{12,8},{16,12},{20,16},{24,20},{28,24},{1,29},{... | collective-permute-start | bytes 393224 | tf_op jit(solution)/shard_map/ppermute | solution.py:97
  24.6 0.0 collective-permute-done.3.refs_3_
  24.6 0.0 copy-start.2
  24.6 0.0 collective-permute-done.2.refs_2_
  24.6 0.0 copy-start.4
  24.6 0.0 collective-permute-done.1.refs_1_
  24.7 0.0 copy-start.6
  24.7 0.0 collective-permute-done.visit_ref
  24.7 0.6 %copy-done.2 = bf16[128,512]{1,0:T(8,128)(2,1)} copy-done((bf16[128,512]{1,0:T(8,128)(2,1)}, bf16[128,512]{1,0:T(8,128)(2,1)S(1)}, u32[]{:S(2)}) %copy-start.2) | copy-done | bytes 131096
  25.3 0.1 copy-done.4
  25.3 0.1 copy-done.6
  25.4 0.0 copy-start.9
  25.4 0.7 %copy-done.9 = bf16[128,512]{1,0:T(8,128)(2,1)} copy-done((bf16[128,512]{1,0:T(8,128)(2,1)}, bf16[128,512]{1,0:T(8,128)(2,1)S(1)}, u32[]{:S(2)}) %copy-start.9) | copy-done | bytes 131096
  26.0 2.6 %shard_map.69 = (f32[128,512]{1,0:T(8,128)}, bf16[128,512]{1,0:T(8,128)(2,1)}) custom-call(f32[1]{0:T(128)S(6)} %copy.7.factor_ref, f32[1]{0:T(128)S(6)} %copy.8.bias_ref, bf16[128,512]{1,0:T(8,128)(2,1)} %get-tuple-element.9.own_ref.refs_0_, bf16[128,512]{1,0:T(8,128)(2,1)} %copy-done.9, bf16[128,512]{1,0:T(8,128)(2,1)} %text_ref.1, ...), custom_call_target="tpu_custom_call" | custom-call | tf_op jit(solution)/shard_map/pallas_call | solution.py:113
  28.7 0.0 collective-permute-start.4
  28.7 0.0 collective-permute-done.9.back_ref
  28.7 0.0 copy-start.10
  28.7 0.7 %copy-done.10 = bf16[128,512]{1,0:T(8,128)(2,1)} copy-done((bf16[128,512]{1,0:T(8,128)(2,1)}, bf16[128,512]{1,0:T(8,128)(2,1)S(1)}, u32[]{:S(2)}) %copy-start.10) | copy-done | bytes 131096
  29.3 1.9 %shard_map.72 = f32[128,512]{1,0:T(8,128)} custom-call(f32[128,512]{1,0:T(8,128)} %get-tuple-element.14.grad_ref, bf16[128,512]{1,0:T(8,128)(2,1)} %copy-done.10, bf16[128,512]{1,0:T(8,128)(2,1)} %text_ref.1), custom_call_target="tpu_custom_call" | custom-call | tf_op jit(solution)/shard_map/pallas_call | solution.py:146
  31.3 3.8 %collective-permute-done.4.back_ref = bf16[128,512]{1,0:T(8,128)(2,1)S(1)} collective-permute-done((bf16[128,512]{1,0:T(8,128)(2,1)}, bf16[128,512]{1,0:T(8,128)(2,1)S(1)}, u32[]{:S(2)}, u32[]{:S(2)}) %collective-permute-start.4) | collective-permute-done | bytes 131104 | tf_op jit(solution)/shard_map/ppermute | solution.py:97
  35.1 0.0 copy-start.1
  35.1 0.7 %copy-done.1 = bf16[128,512]{1,0:T(8,128)(2,1)} copy-done((bf16[128,512]{1,0:T(8,128)(2,1)}, bf16[128,512]{1,0:T(8,128)(2,1)S(1)}, u32[]{:S(2)}) %copy-start.1) | copy-done | bytes 131096
  35.7 4.9 %shard_map.70 = f32[128,3072]{1,0:T(8,128)} custom-call(f32[128,512]{1,0:T(8,128)} %get-tuple-element.10.grad_ref, bf16[128,512]{1,0:T(8,128)(2,1)} %copy-done.1, f32[128,512]{1,0:T(8,128)} %get-tuple-element.12.unit_ref, f32[128,1]{1,0:T(8,128)} %get-tuple-element.13.inv_ref, bf16[3072,512]{1,0:T(8,128)(2,1)} %head_ref.3), custom_call_target="tpu_custom_call" | custom-call | tf_op jit(solution)/shard_map/pallas_call | solution.py:131
Async XLA Ops:
  0.6 8.1 %copy-start = (bf16[128,512]{1,0:T(8,128)(2,1)S(1)}, bf16[128,512]{1,0:T(8,128)(2,1)}, u32[]{:S(2)}) copy-start(bf16[128,512]{1,0:T(8,128)(2,1)} %text_ref.1) | copy-start | bytes 393220
  0.6 11.0 %collective-permute-start.5 = (bf16[128,512]{1,0:T(8,128)(2,1)}, bf16[128,512]{1,0:T(8,128)(2,1)S(1)}, u32[]{:S(2)}, u32[]{:S(2)}) collective-permute-start(bf16[128,512]{1,0:T(8,128)(2,1)} %text_ref.1), channel_id=1, source_target_pairs={{0,4},{4,8},{8,12},{12,16},{16,20},{20,24},{24,28},{28,0},{1,5},{5... | collective-permute-start | bytes 393224 | tf_op jit(solution)/shard_map/ppermute | solution.py:97
  4.7 7.5 %collective-permute-start.8 = (bf16[128,512]{1,0:T(8,128)(2,1)}, bf16[128,512]{1,0:T(8,128)(2,1)S(1)}, u32[]{:S(2)}, u32[]{:S(2)}) collective-permute-start(bf16[128,512]{1,0:T(8,128)(2,1)} %get-tuple-element.9.own_ref.refs_0_), channel_id=1, source_target_pairs={{0,3},{1,2},{2,1},{3,0},{4,7},{5,6},{6,5},{7,4},{8,11},{9,10},{10,... | collective-permute-start | bytes 393224 | tf_op jit(solution)/shard_map/ppermute | solution.py:94
  8.2 7.3 %collective-permute-start.7 = (bf16[128,512]{1,0:T(8,128)(2,1)}, bf16[128,512]{1,0:T(8,128)(2,1)S(1)}, u32[]{:S(2)}, u32[]{:S(2)}) collective-permute-start(bf16[128,512]{1,0:T(8,128)(2,1)} %get-tuple-element.9.own_ref.refs_0_), channel_id=1, source_target_pairs={{0,2},{1,3},{2,0},{3,1},{4,6},{5,7},{6,4},{7,5},{8,10},{9,11},{10,... | collective-permute-start | bytes 393224 | tf_op jit(solution)/shard_map/ppermute | solution.py:94
  8.7 12.0 %collective-permute-start.6 = (bf16[128,512]{1,0:T(8,128)(2,1)}, bf16[128,512]{1,0:T(8,128)(2,1)S(1)}, u32[]{:S(2)}, u32[]{:S(2)}) collective-permute-start(bf16[128,512]{1,0:T(8,128)(2,1)} %get-tuple-element.9.own_ref.refs_0_), channel_id=1, source_target_pairs={{0,1},{1,0},{2,3},{3,2},{4,5},{5,4},{6,7},{7,6},{8,9},{9,8},{10,11... | collective-permute-start | bytes 393224 | tf_op jit(solution)/shard_map/ppermute | solution.py:94
  8.7 15.9 %collective-permute-start.3 = (bf16[128,512]{1,0:T(8,128)(2,1)S(1)}, bf16[128,512]{1,0:T(8,128)(2,1)S(1)}, u32[]{:S(2)}, u32[]{:S(2)}) collective-permute-start(bf16[128,512]{1,0:T(8,128)(2,1)S(1)} %copy-done), channel_id=1, source_target_pairs={{0,3},{1,2},{2,1},{3,0},{4,7},{5,6},{6,5},{7,4},{8,11},{9,10},{10,... | collective-permute-start | bytes 393224 | tf_op jit(solution)/shard_map/ppermute | solution.py:94
  11.7 9.0 %copy-start.3 = (bf16[128,512]{1,0:T(8,128)(2,1)}, bf16[128,512]{1,0:T(8,128)(2,1)S(1)}, u32[]{:S(2)}) copy-start(bf16[128,512]{1,0:T(8,128)(2,1)S(1)} %collective-permute-done.5.visit_ref) | copy-start | bytes 393220
  11.7 13.0 %collective-permute-start.2 = (bf16[128,512]{1,0:T(8,128)(2,1)S(1)}, bf16[128,512]{1,0:T(8,128)(2,1)S(1)}, u32[]{:S(2)}, u32[]{:S(2)}) collective-permute-start(bf16[128,512]{1,0:T(8,128)(2,1)S(1)} %copy-done), channel_id=1, source_target_pairs={{0,2},{1,3},{2,0},{3,1},{4,6},{5,7},{6,4},{7,5},{8,10},{9,11},{10,... | collective-permute-start | bytes 393224 | tf_op jit(solution)/shard_map/ppermute | solution.py:94
  12.2 8.5 %copy-start.5 = (bf16[128,512]{1,0:T(8,128)(2,1)}, bf16[128,512]{1,0:T(8,128)(2,1)S(1)}, u32[]{:S(2)}) copy-start(bf16[128,512]{1,0:T(8,128)(2,1)S(1)} %collective-permute-done.8.refs_3_) | copy-start | bytes 393220
  12.2 12.5 %collective-permute-start.1 = (bf16[128,512]{1,0:T(8,128)(2,1)S(1)}, bf16[128,512]{1,0:T(8,128)(2,1)S(1)}, u32[]{:S(2)}, u32[]{:S(2)}) collective-permute-start(bf16[128,512]{1,0:T(8,128)(2,1)S(1)} %copy-done), channel_id=1, source_target_pairs={{0,1},{1,0},{2,3},{3,2},{4,5},{5,4},{6,7},{7,6},{8,9},{9,8},{10,11... | collective-permute-start | bytes 393224 | tf_op jit(solution)/shard_map/ppermute | solution.py:94
  15.5 5.2 %copy-start.7 = (bf16[128,512]{1,0:T(8,128)(2,1)}, bf16[128,512]{1,0:T(8,128)(2,1)S(1)}, u32[]{:S(2)}) copy-start(bf16[128,512]{1,0:T(8,128)(2,1)S(1)} %collective-permute-done.7.refs_2_) | copy-start | bytes 393220
  15.5 9.2 %collective-permute-start = (bf16[128,512]{1,0:T(8,128)(2,1)}, bf16[128,512]{1,0:T(8,128)(2,1)S(1)}, u32[]{:S(2)}, u32[]{:S(2)}) collective-permute-start(bf16[128,512]{1,0:T(8,128)(2,1)} %get-tuple-element.9.own_ref.refs_0_), channel_id=1, source_target_pairs={{0,28},{4,0},{8,4},{12,8},{16,12},{20,16},{24,20},{28,24},{1,29},{... | collective-permute-start | bytes 393224 | tf_op jit(solution)/shard_map/ppermute | solution.py:97
  20.7 0.7 %copy-start.8 = (bf16[128,512]{1,0:T(8,128)(2,1)}, bf16[128,512]{1,0:T(8,128)(2,1)S(1)}, u32[]{:S(2)}) copy-start(bf16[128,512]{1,0:T(8,128)(2,1)S(1)} %collective-permute-done.6.refs_1_) | copy-start | bytes 393220
  24.0 4.7 %collective-permute-start.9 = (bf16[128,512]{1,0:T(8,128)(2,1)}, bf16[128,512]{1,0:T(8,128)(2,1)S(1)}, u32[]{:S(2)}, u32[]{:S(2)}) collective-permute-start(bf16[128,512]{1,0:T(8,128)(2,1)} %get-tuple-element.15), channel_id=1, source_target_pairs={{0,28},{4,0},{8,4},{12,8},{16,12},{20,16},{24,20},{28,24},{1,29},{... | collective-permute-start | bytes 393224 | tf_op jit(solution)/shard_map/ppermute | solution.py:97
  24.6 0.6 %copy-start.2 = (bf16[128,512]{1,0:T(8,128)(2,1)}, bf16[128,512]{1,0:T(8,128)(2,1)S(1)}, u32[]{:S(2)}) copy-start(bf16[128,512]{1,0:T(8,128)(2,1)S(1)} %collective-permute-done.3.refs_3_) | copy-start | bytes 393220
  24.6 0.7 %copy-start.4 = (bf16[128,512]{1,0:T(8,128)(2,1)}, bf16[128,512]{1,0:T(8,128)(2,1)S(1)}, u32[]{:S(2)}) copy-start(bf16[128,512]{1,0:T(8,128)(2,1)S(1)} %collective-permute-done.2.refs_2_) | copy-start | bytes 393220
  24.7 0.7 %copy-start.6 = (bf16[128,512]{1,0:T(8,128)(2,1)}, bf16[128,512]{1,0:T(8,128)(2,1)S(1)}, u32[]{:S(2)}) copy-start(bf16[128,512]{1,0:T(8,128)(2,1)S(1)} %collective-permute-done.1.refs_1_) | copy-start | bytes 393220
  25.4 0.7 %copy-start.9 = (bf16[128,512]{1,0:T(8,128)(2,1)}, bf16[128,512]{1,0:T(8,128)(2,1)S(1)}, u32[]{:S(2)}) copy-start(bf16[128,512]{1,0:T(8,128)(2,1)S(1)} %collective-permute-done.visit_ref) | copy-start | bytes 393220
  28.7 6.4 %collective-permute-start.4 = (bf16[128,512]{1,0:T(8,128)(2,1)}, bf16[128,512]{1,0:T(8,128)(2,1)S(1)}, u32[]{:S(2)}, u32[]{:S(2)}) collective-permute-start(bf16[128,512]{1,0:T(8,128)(2,1)} %get-tuple-element.11), channel_id=1, source_target_pairs={{0,4},{4,8},{8,12},{12,16},{16,20},{20,24},{24,28},{28,0},{1,5},{5... | collective-permute-start | bytes 393224 | tf_op jit(solution)/shard_map/ppermute | solution.py:97
  28.7 0.7 %copy-start.10 = (bf16[128,512]{1,0:T(8,128)(2,1)}, bf16[128,512]{1,0:T(8,128)(2,1)S(1)}, u32[]{:S(2)}) copy-start(bf16[128,512]{1,0:T(8,128)(2,1)S(1)} %collective-permute-done.9.back_ref) | copy-start | bytes 393220
  35.1 0.7 %copy-start.1 = (bf16[128,512]{1,0:T(8,128)(2,1)}, bf16[128,512]{1,0:T(8,128)(2,1)S(1)}, u32[]{:S(2)}) copy-start(bf16[128,512]{1,0:T(8,128)(2,1)S(1)} %collective-permute-done.4.back_ref) | copy-start | bytes 393220

commit v2 on v1

--- a/solution.py
+++ b/solution.py
@@ -84,7 +84,12 @@
     emb = text_emb.shape[1]
     n_blk, n_group = lax.axis_size("blk"), lax.axis_size("group")
     shape = jax.ShapeDtypeStruct
-    sub = functools.partial(pl.pallas_call)
+    sub = functools.partial(
+        pl.pallas_call, compiler_params=pltpu.CompilerParams(vmem_limit_bytes=16 * 2**20)
+    )
+
+    def cost(flops, moved):
+        return pl.CostEstimate(flops=flops, bytes_accessed=moved, transcendentals=0)
 
     def to_peer(piece, k):
         if n_group & (n_group - 1) == 0:
@@ -101,6 +106,7 @@
 
     img_unit, img_inv, img_low = sub(
         project_kernel,
+        cost_estimate=cost(2 * rows * width * emb, 2 * width * (rows + emb)),
         out_shape=(shape((rows, emb), F32), shape((rows, 1), F32), shape((rows, emb), BF16)),
         in_specs=[VMEM] * 2,
         out_specs=(VMEM,) * 3,
@@ -112,6 +118,7 @@
     pair = (shape((rows, emb), F32), shape((rows, emb), BF16))
     grad_img, img_return = sub(
         image_kernel,
+        cost_estimate=cost(8 * rows * rows * n_group * emb, 4 * rows * emb * (n_group + 4)),
         out_shape=pair,
         in_specs=[SMEM] * 2 + [VMEM] * (2 + n_group),
         out_specs=(VMEM,) * 2,
@@ -120,6 +127,7 @@
 
     grad_txt, txt_return = sub(
         text_kernel,
+        cost_estimate=cost(8 * rows * rows * n_group * emb, 4 * rows * emb * (n_group + 4)),
         out_shape=pair,
         in_specs=[SMEM] * 2 + [VMEM] * (2 + n_group),
         out_specs=(VMEM,) * 2,
@@ -130,6 +138,7 @@
     whole = lambda *dims: pl.BlockSpec(dims, lambda j: (0, 0))
     d_feat = sub(
         feat_kernel,
+        cost_estimate=cost(2 * rows * width * emb, 4 * width * (rows + emb)),
         grid=(width // tile,),
         out_shape=shape((rows, width), F32),
         in_specs=[

time: 40.9 us -> 32 us (0.78)
  Pallas kernels: 15.6 us -> 5.73 us
  waiting for transfers between devices: 5.17 us -> 6.67 us
    pallas_call x4, Pallas kernels: 13.7 us -> 4.83 us  [the longest x1 2.81 us: body(): sub(feat_kernel, cost_estimate=cost(2 * rows * width * emb, 4 * width * (...]
    ppermute x4, waiting for transfers between devices: 3.79 us -> 5.28 us  [to_block(): lax.ppermute(piece, 'blk', [(i, (i + distance) % n_blk) for i in range(n_...]
    pallas_call x1, Pallas kernels: 1.95 us -> 0.9 us  [body(): sub(text_out_kernel, out_shape=shape((rows, emb), F32), in_specs=[VMEM] *...]
    unnamed x22 -> x8, local copies, waits for them, and re-layouts: 3.35 us -> 3.03 us
  transfers between devices with their start and end apart: 10 -> 10, of which waited for: 2 -> 3; matrix products, arithmetic and copies ran while one was open for 0% -> 0% of each run, Pallas kernels for 26% -> 9%
where the time goes in v2:
time: 32 us; the launch traced here: 31.8 us
  starting transfers between devices  14.4 us (45%)
  waiting for transfers between devices  6.67 us (21%)
  Pallas kernels  5.73 us (18%)
  local copies, waits for them, and re-layouts  3.03 us (9%)
  between operations  1.99 us (6%)
    ppermute x6, starting transfers between devices, to_peer(): return lax.ppermute(piece, 'group', route)  9.25 us
    ppermute x4, waiting for transfers between devices, to_block(): lax.ppermute(piece, 'blk', [(i, (i + distance) % n_blk) for i in range(n_...  5.28 us
    ppermute x4, starting transfers between devices, to_block(): lax.ppermute(piece, 'blk', [(i, (i + distance) % n_blk) for i in range(n_...  5.17 us
    unnamed x8, local copies, waits for them, and re-layouts  3.03 us
    pallas_call x1, Pallas kernels, body(): sub(feat_kernel, cost_estimate=cost(2 * rows * width * emb, 4 * width * (...  2.81 us
    ppermute x6, waiting for transfers between devices, to_peer(): return lax.ppermute(piece, 'group', route)  1.39 us
    pallas_call x1, Pallas kernels, body(): sub(text_out_kernel, out_shape=shape((rows, emb), F32), in_specs=[VMEM] *...  0.9 us
    pallas_call x1, Pallas kernels, body(): sub(image_kernel, cost_estimate=cost(8 * rows * rows * n_group * emb, 4 *...  0.7 us
  transfers between devices with their start and end apart: 10, of which 3 were waited for; matrix products, arithmetic and copies ran while one was open for 0% of the time, Pallas kernels for 9%

profile of v2, /device:TPU:0, one launch (start us, length us, event | category | flops | bytes accessed | tf_op | source)
XLA Modules:
  0.0 31.8 jit_solution(17363621875732380326)
XLA Ops:
  0.6 0.5 %collective-permute-start.5 = (bf16[128,512]{1,0:T(8,128)(2,1)}, bf16[128,512]{1,0:T(8,128)(2,1)S(1)}, u32[]{:S(2)}, u32[]{:S(2)}) collective-permute-start(bf16[128,512]{1,0:T(8,128)(2,1)} %text_ref.1), channel_id=1, source_target_pairs={{0,4},{4,8},{8,12},{12,16},{16,20},{20,24},{24,28},{28,0},{1,5},{5... | collective-permute-start | bytes 393224 | tf_op jit(solution)/shard_map/ppermute | solution.py:102
  1.1 0.0 copy-start
  1.1 1.9 %copy-done = bf16[3072,512]{1,0:T(8,128)(2,1)S(1)} copy-done((bf16[3072,512]{1,0:T(8,128)(2,1)S(1)}, bf16[3072,512]{1,0:T(8,128)(2,1)}, u32[]{:S(2)}) %copy-start) | copy-done | bytes 3145752
  3.0 0.0 copy-start.2
  3.0 1.1 %copy-done.2 = bf16[128,3072]{1,0:T(8,128)(2,1)S(1)} copy-done((bf16[128,3072]{1,0:T(8,128)(2,1)S(1)}, bf16[128,3072]{1,0:T(8,128)(2,1)}, u32[]{:S(2)}) %copy-start.2) | copy-done | bytes 786456
  4.2 0.0 copy-start.3
  4.2 0.0 copy-start.1
  4.2 0.7 %shard_map.68 = (f32[128,512]{1,0:T(8,128)S(1)}, f32[128,1]{1,0:T(8,128)S(1)}, bf16[128,512]{1,0:T(8,128)(2,1)S(1)}) custom-call(bf16[128,3072]{1,0:T(8,128)(2,1)S(1)} %copy-done.2, bf16[3072,512]{1,0:T(8,128)(2,1)S(1)} %copy-done), custom_call_target="tpu_custom_call" | custom-call | flops 402653184 | bytes 3932160 | tf_op jit(solution)/shard_map/pallas_call | solution.py:107
  4.8 3.5 %collective-permute-start.8 = (bf16[128,512]{1,0:T(8,128)(2,1)S(1)}, bf16[128,512]{1,0:T(8,128)(2,1)S(1)}, u32[]{:S(2)}, u32[]{:S(2)}) collective-permute-start(bf16[128,512]{1,0:T(8,128)(2,1)S(1)} %get-tuple-element.9.own_ref.refs_0_), channel_id=1, source_target_pairs={{0,3},{1,2},{2,1},{3,0},{4,7},{5,6},{6,5},{7,4},{8,11},{9,10},{10,... | collective-permute-start | bytes 393224 | tf_op jit(solution)/shard_map/ppermute | solution.py:99
  8.4 0.5 %collective-permute-start.7 = (bf16[128,512]{1,0:T(8,128)(2,1)S(1)}, bf16[128,512]{1,0:T(8,128)(2,1)S(1)}, u32[]{:S(2)}, u32[]{:S(2)}) collective-permute-start(bf16[128,512]{1,0:T(8,128)(2,1)S(1)} %get-tuple-element.9.own_ref.refs_0_), channel_id=1, source_target_pairs={{0,2},{1,3},{2,0},{3,1},{4,6},{5,7},{6,4},{7,5},{8,10},{9,11},{10,... | collective-permute-start | bytes 393224 | tf_op jit(solution)/shard_map/ppermute | solution.py:99
  8.9 0.1 collective-permute-start.6
  9.0 0.0 copy-done.3
  9.0 2.8 %collective-permute-start.3 = (bf16[128,512]{1,0:T(8,128)(2,1)S(1)}, bf16[128,512]{1,0:T(8,128)(2,1)S(1)}, u32[]{:S(2)}, u32[]{:S(2)}) collective-permute-start(bf16[128,512]{1,0:T(8,128)(2,1)S(1)} %copy-done.3), channel_id=1, source_target_pairs={{0,3},{1,2},{2,1},{3,0},{4,7},{5,6},{6,5},{7,4},{8,11},{9,10},{10,... | collective-permute-start | bytes 393224 | tf_op jit(solution)/shard_map/ppermute | solution.py:99
  11.8 0.0 collective-permute-done.5.visit_ref
  11.9 0.5 %collective-permute-start.2 = (bf16[128,512]{1,0:T(8,128)(2,1)S(1)}, bf16[128,512]{1,0:T(8,128)(2,1)S(1)}, u32[]{:S(2)}, u32[]{:S(2)}) collective-permute-start(bf16[128,512]{1,0:T(8,128)(2,1)S(1)} %copy-done.3), channel_id=1, source_target_pairs={{0,2},{1,3},{2,0},{3,1},{4,6},{5,7},{6,4},{7,5},{8,10},{9,11},{10,... | collective-permute-start | bytes 393224 | tf_op jit(solution)/shard_map/ppermute | solution.py:99
  12.4 0.0 collective-permute-done.8.refs_3_
  12.4 1.7 %collective-permute-start.1 = (bf16[128,512]{1,0:T(8,128)(2,1)S(1)}, bf16[128,512]{1,0:T(8,128)(2,1)S(1)}, u32[]{:S(2)}, u32[]{:S(2)}) collective-permute-start(bf16[128,512]{1,0:T(8,128)(2,1)S(1)} %copy-done.3), channel_id=1, source_target_pairs={{0,1},{1,0},{2,3},{3,2},{4,5},{5,4},{6,7},{7,6},{8,9},{9,8},{10,11... | collective-permute-start | bytes 393224 | tf_op jit(solution)/shard_map/ppermute | solution.py:99
  14.1 1.4 %collective-permute-done.7.refs_2_ = bf16[128,512]{1,0:T(8,128)(2,1)S(1)} collective-permute-done((bf16[128,512]{1,0:T(8,128)(2,1)S(1)}, bf16[128,512]{1,0:T(8,128)(2,1)S(1)}, u32[]{:S(2)}, u32[]{:S(2)}) %collective-permute-start.7) | collective-permute-done | bytes 131104 | tf_op jit(solution)/shard_map/ppermute | solution.py:99
  15.5 3.9 %collective-permute-start = (bf16[128,512]{1,0:T(8,128)(2,1)S(1)}, bf16[128,512]{1,0:T(8,128)(2,1)S(1)}, u32[]{:S(2)}, u32[]{:S(2)}) collective-permute-start(bf16[128,512]{1,0:T(8,128)(2,1)S(1)} %get-tuple-element.9.own_ref.refs_0_), channel_id=1, source_target_pairs={{0,28},{4,0},{8,4},{12,8},{16,12},{20,16},{24,20},{28,24},{1,29},{... | collective-permute-start | bytes 393224 | tf_op jit(solution)/shard_map/ppermute | solution.py:102
  20.7 0.0 collective-permute-done.6.refs_1_
  20.7 0.6 %shard_map.71 = (f32[128,512]{1,0:T(8,128)S(1)}, bf16[128,512]{1,0:T(8,128)(2,1)S(1)}) custom-call(f32[1]{0:T(128)S(6)} %copy.7.factor_ref, f32[1]{0:T(128)S(6)} %copy.8.bias_ref, bf16[128,512]{1,0:T(8,128)(2,1)S(1)} %copy-done.3, bf16[128,512]{1,0:T(8,128)(2,1)S(1)} %collective-permute-done.5.visit_ref, ...), custom_call_target="tpu_custom_call" | custom-call | flops 268435456 | bytes 2097152 | tf_op jit(solution)/shard_map/pallas_call | solution.py:128
  21.3 0.7 %collective-permute-start.9 = (bf16[128,512]{1,0:T(8,128)(2,1)S(1)}, bf16[128,512]{1,0:T(8,128)(2,1)S(1)}, u32[]{:S(2)}, u32[]{:S(2)}) collective-permute-start(bf16[128,512]{1,0:T(8,128)(2,1)S(1)} %get-tuple-element.15), channel_id=1, source_target_pairs={{0,28},{4,0},{8,4},{12,8},{16,12},{20,16},{24,20},{28,24},{1,29},{... | collective-permute-start | bytes 393224 | tf_op jit(solution)/shard_map/ppermute | solution.py:102
  22.0 0.0 collective-permute-done.3.refs_3_
  22.0 0.0 collective-permute-done.2.refs_2_
  22.1 0.0 collective-permute-done.1.refs_1_
  22.1 0.0 collective-permute-done.visit_ref
  22.1 0.7 %shard_map.69 = (f32[128,512]{1,0:T(8,128)S(1)}, bf16[128,512]{1,0:T(8,128)(2,1)S(1)}) custom-call(f32[1]{0:T(128)S(6)} %copy.7.factor_ref, f32[1]{0:T(128)S(6)} %copy.8.bias_ref, bf16[128,512]{1,0:T(8,128)(2,1)S(1)} %get-tuple-element.9.own_ref.refs_0_, bf16[128,512]{1,0:T(8,128)(2,1)S(1)} %collective-permute-done.visit_ref, ...), custom_call_target="tpu_custom_call" | custom-call | flops 268435456 | bytes 2097152 | tf_op jit(solution)/shard_map/pallas_call | solution.py:119
  22.8 0.1 collective-permute-start.4
  22.8 1.7 %collective-permute-done.9.back_ref = bf16[128,512]{1,0:T(8,128)(2,1)S(1)} collective-permute-done((bf16[128,512]{1,0:T(8,128)(2,1)S(1)}, bf16[128,512]{1,0:T(8,128)(2,1)S(1)}, u32[]{:S(2)}, u32[]{:S(2)}) %collective-permute-start.9) | collective-permute-done | bytes 131104 | tf_op jit(solution)/shard_map/ppermute | solution.py:102
  24.6 0.9 %shard_map.72 = f32[128,512]{1,0:T(8,128)} custom-call(f32[128,512]{1,0:T(8,128)S(1)} %get-tuple-element.14.grad_ref, bf16[128,512]{1,0:T(8,128)(2,1)S(1)} %collective-permute-done.9.back_ref, bf16[128,512]{1,0:T(8,128)(2,1)S(1)} %copy-done.3), custom_call_target="tpu_custom_call" | custom-call | tf_op jit(solution)/shard_map/pallas_call | solution.py:155
  25.5 3.5 %collective-permute-done.4.back_ref = bf16[128,512]{1,0:T(8,128)(2,1)S(1)} collective-permute-done((bf16[128,512]{1,0:T(8,128)(2,1)S(1)}, bf16[128,512]{1,0:T(8,128)(2,1)S(1)}, u32[]{:S(2)}, u32[]{:S(2)}) %collective-permute-start.4) | collective-permute-done | bytes 131104 | tf_op jit(solution)/shard_map/ppermute | solution.py:102
  29.0 0.0 copy-done.1
  29.0 2.8 %shard_map.70 = f32[128,3072]{1,0:T(8,128)} custom-call(f32[128,512]{1,0:T(8,128)S(1)} %get-tuple-element.10.grad_ref, bf16[128,512]{1,0:T(8,128)(2,1)S(1)} %collective-permute-done.4.back_ref, f32[128,512]{1,0:T(8,128)S(1)} %get-tuple-element.12.unit_ref, f32[128,1]{1,0:T(8,128)S(1)} %get-tuple-element.13.inv_ref, bf16[3072,512]{1,0:T(8,128)(2,1)S(1)} %copy-done.1), custom_call_target="tpu_custom_call" | custom-call | flops 402653184 | bytes 7864320 | tf_op jit(solution)/shard_map/pallas_call | solution.py:139
Async XLA Ops:
  0.6 11.2 %collective-permute-start.5 = (bf16[128,512]{1,0:T(8,128)(2,1)}, bf16[128,512]{1,0:T(8,128)(2,1)S(1)}, u32[]{:S(2)}, u32[]{:S(2)}) collective-permute-start(bf16[128,512]{1,0:T(8,128)(2,1)} %text_ref.1), channel_id=1, source_target_pairs={{0,4},{4,8},{8,12},{12,16},{16,20},{20,24},{24,28},{28,0},{1,5},{5... | collective-permute-start | bytes 393224 | tf_op jit(solution)/shard_map/ppermute | solution.py:102
  1.1 1.9 %copy-start = (bf16[3072,512]{1,0:T(8,128)(2,1)S(1)}, bf16[3072,512]{1,0:T(8,128)(2,1)}, u32[]{:S(2)}) copy-start(bf16[3072,512]{1,0:T(8,128)(2,1)} %head_ref.3) | copy-start | bytes 9437188
  3.0 1.1 %copy-start.2 = (bf16[128,3072]{1,0:T(8,128)(2,1)S(1)}, bf16[128,3072]{1,0:T(8,128)(2,1)}, u32[]{:S(2)}) copy-start(bf16[128,3072]{1,0:T(8,128)(2,1)} %img_ref.1) | copy-start | bytes 2359300
  4.2 4.8 %copy-start.3 = (bf16[128,512]{1,0:T(8,128)(2,1)S(1)}, bf16[128,512]{1,0:T(8,128)(2,1)}, u32[]{:S(2)}) copy-start(bf16[128,512]{1,0:T(8,128)(2,1)} %text_ref.1) | copy-start | bytes 393220
  4.2 24.9 %copy-start.1 = (bf16[3072,512]{1,0:T(8,128)(2,1)S(1)}, bf16[3072,512]{1,0:T(8,128)(2,1)}, u32[]{:S(2)}) copy-start(bf16[3072,512]{1,0:T(8,128)(2,1)} %head_ref.3) | copy-start | bytes 9437188
  4.8 7.5 %collective-permute-start.8 = (bf16[128,512]{1,0:T(8,128)(2,1)S(1)}, bf16[128,512]{1,0:T(8,128)(2,1)S(1)}, u32[]{:S(2)}, u32[]{:S(2)}) collective-permute-start(bf16[128,512]{1,0:T(8,128)(2,1)S(1)} %get-tuple-element.9.own_ref.refs_0_), channel_id=1, source_target_pairs={{0,3},{1,2},{2,1},{3,0},{4,7},{5,6},{6,5},{7,4},{8,11},{9,10},{10,... | collective-permute-start | bytes 393224 | tf_op jit(solution)/shard_map/ppermute | solution.py:99
  8.4 7.1 %collective-permute-start.7 = (bf16[128,512]{1,0:T(8,128)(2,1)S(1)}, bf16[128,512]{1,0:T(8,128)(2,1)S(1)}, u32[]{:S(2)}, u32[]{:S(2)}) collective-permute-start(bf16[128,512]{1,0:T(8,128)(2,1)S(1)} %get-tuple-element.9.own_ref.refs_0_), channel_id=1, source_target_pairs={{0,2},{1,3},{2,0},{3,1},{4,6},{5,7},{6,4},{7,5},{8,10},{9,11},{10,... | collective-permute-start | bytes 393224 | tf_op jit(solution)/shard_map/ppermute | solution.py:99
  8.9 11.8 %collective-permute-start.6 = (bf16[128,512]{1,0:T(8,128)(2,1)S(1)}, bf16[128,512]{1,0:T(8,128)(2,1)S(1)}, u32[]{:S(2)}, u32[]{:S(2)}) collective-permute-start(bf16[128,512]{1,0:T(8,128)(2,1)S(1)} %get-tuple-element.9.own_ref.refs_0_), channel_id=1, source_target_pairs={{0,1},{1,0},{2,3},{3,2},{4,5},{5,4},{6,7},{7,6},{8,9},{9,8},{10,11... | collective-permute-start | bytes 393224 | tf_op jit(solution)/shard_map/ppermute | solution.py:99
  9.0 13.0 %collective-permute-start.3 = (bf16[128,512]{1,0:T(8,128)(2,1)S(1)}, bf16[128,512]{1,0:T(8,128)(2,1)S(1)}, u32[]{:S(2)}, u32[]{:S(2)}) collective-permute-start(bf16[128,512]{1,0:T(8,128)(2,1)S(1)} %copy-done.3), channel_id=1, source_target_pairs={{0,3},{1,2},{2,1},{3,0},{4,7},{5,6},{6,5},{7,4},{8,11},{9,10},{10,... | collective-permute-start | bytes 393224 | tf_op jit(solution)/shard_map/ppermute | solution.py:99
  11.9 10.2 %collective-permute-start.2 = (bf16[128,512]{1,0:T(8,128)(2,1)S(1)}, bf16[128,512]{1,0:T(8,128)(2,1)S(1)}, u32[]{:S(2)}, u32[]{:S(2)}) collective-permute-start(bf16[128,512]{1,0:T(8,128)(2,1)S(1)} %copy-done.3), channel_id=1, source_target_pairs={{0,2},{1,3},{2,0},{3,1},{4,6},{5,7},{6,4},{7,5},{8,10},{9,11},{10,... | collective-permute-start | bytes 393224 | tf_op jit(solution)/shard_map/ppermute | solution.py:99
  12.4 9.7 %collective-permute-start.1 = (bf16[128,512]{1,0:T(8,128)(2,1)S(1)}, bf16[128,512]{1,0:T(8,128)(2,1)S(1)}, u32[]{:S(2)}, u32[]{:S(2)}) collective-permute-start(bf16[128,512]{1,0:T(8,128)(2,1)S(1)} %copy-done.3), channel_id=1, source_target_pairs={{0,1},{1,0},{2,3},{3,2},{4,5},{5,4},{6,7},{7,6},{8,9},{9,8},{10,11... | collective-permute-start | bytes 393224 | tf_op jit(solution)/shard_map/ppermute | solution.py:99
  15.5 6.6 %collective-permute-start = (bf16[128,512]{1,0:T(8,128)(2,1)S(1)}, bf16[128,512]{1,0:T(8,128)(2,1)S(1)}, u32[]{:S(2)}, u32[]{:S(2)}) collective-permute-start(bf16[128,512]{1,0:T(8,128)(2,1)S(1)} %get-tuple-element.9.own_ref.refs_0_), channel_id=1, source_target_pairs={{0,28},{4,0},{8,4},{12,8},{16,12},{20,16},{24,20},{28,24},{1,29},{... | collective-permute-start | bytes 393224 | tf_op jit(solution)/shard_map/ppermute | solution.py:102
  21.3 3.2 %collective-permute-start.9 = (bf16[128,512]{1,0:T(8,128)(2,1)S(1)}, bf16[128,512]{1,0:T(8,128)(2,1)S(1)}, u32[]{:S(2)}, u32[]{:S(2)}) collective-permute-start(bf16[128,512]{1,0:T(8,128)(2,1)S(1)} %get-tuple-element.15), channel_id=1, source_target_pairs={{0,28},{4,0},{8,4},{12,8},{16,12},{20,16},{24,20},{28,24},{1,29},{... | collective-permute-start | bytes 393224 | tf_op jit(solution)/shard_map/ppermute | solution.py:102
  22.8 6.2 %collective-permute-start.4 = (bf16[128,512]{1,0:T(8,128)(2,1)S(1)}, bf16[128,512]{1,0:T(8,128)(2,1)S(1)}, u32[]{:S(2)}, u32[]{:S(2)}) collective-permute-start(bf16[128,512]{1,0:T(8,128)(2,1)S(1)} %get-tuple-element.11), channel_id=1, source_target_pairs={{0,4},{4,8},{8,12},{12,16},{16,20},{20,24},{24,28},{28,0},{1,5},{5... | collective-permute-start | bytes 393224 | tf_op jit(solution)/shard_map/ppermute | solution.py:102

commit v3 on v1

v3 whole, which is shorter than its diff:
```python
import functools
import math

import jax
import jax.numpy as jnp
from jax import lax
from jax.experimental import pallas as pl
from jax.experimental.pallas import tpu as pltpu
from jax.sharding import PartitionSpec as P

EPS = 1e-06
F32 = jnp.float32
BF16 = jnp.bfloat16
CONTRACT_LAST = (((1,), (1,)), ((), ()))
VMEM = pl.BlockSpec(memory_space=pltpu.VMEM)
SMEM = pl.BlockSpec(memory_space=pltpu.SMEM)
ANY = pl.BlockSpec(memory_space=pl.ANY)
HBM = pl.BlockSpec(memory_space=pltpu.HBM)


def to_unit(values):
    inverse = lax.rsqrt(jnp.sum(values * values, axis=-1, keepdims=True) + EPS)
    return values * inverse, inverse


def unit_back(grad_in, unit_rows, inverse):
    return (grad_in - unit_rows * jnp.sum(unit_rows * grad_in, axis=-1, keepdims=True)) * inverse


def text_kernel(text_ref, unit_ref, inv_ref, low_ref):
    unit, inverse = to_unit(text_ref[...].astype(F32))
    unit_ref[...] = unit
    inv_ref[...] = inverse
    low_ref[...] = unit.astype(BF16)


def project_kernel(img_ref, head_ref, unit_ref, inv_ref, low_ref):
    projected = jnp.dot(img_ref[...], head_ref[...], preferred_element_type=F32)
    unit, inverse = to_unit(projected)
    unit_ref[...] = unit
    inv_ref[...] = inverse
    low_ref[...] = unit.astype(BF16)


def meet(scale, bias, left, right, rows):
    z = scale * lax.dot_general(left, right, CONTRACT_LAST, preferred_element_type=F32) + bias
    row_ids = lax.broadcasted_iota(jnp.int32, z.shape, 0)
    col_ids = lax.broadcasted_iota(jnp.int32, z.shape, 1)
    positive = jnp.where((row_ids == col_ids) & (row_ids < rows), 1.0, 0.0)
    weight = (1.0 / (1.0 + jnp.exp(-z)) - positive).astype(BF16)
    return scale * jnp.dot(weight, right, preferred_element_type=F32)


def meet_kernel(n_left, factor_ref, bias_ref, after_ref, *refs):
    left_refs, refs = refs[:n_left], refs[n_left:]
    right_refs, (grad_ref, *out_refs) = refs[:-n_left], refs[-n_left:]
    rows = grad_ref.shape[0]
    left = jnp.concatenate([ref[...] for ref in left_refs], axis=0)
    right = jnp.concatenate([ref[...] for ref in right_refs], axis=0)
    scale = jnp.exp(factor_ref[...])
    grad = meet(scale, bias_ref[...], left, right, rows)
    grad_ref[...] = grad[:rows]
    for k, ref in enumerate(out_refs, 1):
        ref[...] = grad[k * rows : (k + 1) * rows].astype(BF16)


def feat_kernel(grad_ref, unit_ref, inv_ref, head_ref, *refs):
    peer_refs, (out_ref, flag_ref, out_here, sems) = refs[:-4], refs[-4:]
    parts = sems.shape[0]
    width = head_ref.shape[0] // parts
    grad = grad_ref[...]
    for ref in peer_refs:
        grad += ref[...].astype(F32)
    low = unit_back(grad, unit_ref[...], inv_ref[...]).astype(BF16)
    copies = []
    for i in range(parts):
        span = pl.ds(i * width, width)
        out_here[:, span] = lax.dot_general(low, head_ref[span], CONTRACT_LAST, preferred_element_type=F32)
        copy = pltpu.make_async_copy(out_here.at[:, span], out_ref.at[:, span], sems.at[i])
        copy.start()
        copies.append(copy)
    for copy in copies:
        copy.wait()
    flag_ref[...] = jnp.zeros_like(flag_ref)


def text_out_kernel(after_ref, grad_ref, unit_ref, inv_ref, *refs):
    peer_refs, out_ref = refs[:-1], refs[-1]
    grad = grad_ref[...]
    for ref in peer_refs:
        grad += ref[...].astype(F32)
    out_ref[...] = unit_back(grad, unit_ref[...], inv_ref[...])


def body(img_feat, head_weight, text_emb, natural_exponent_factor, bias):
    rows, width = img_feat.shape
    emb = text_emb.shape[1]
    n_blk, n_group = lax.axis_size("blk"), lax.axis_size("group")
    n_col = next(k for k in range(math.isqrt(n_group), 0, -1) if n_group % k == 0)
    n_row = n_group // n_col
    shape = jax.ShapeDtypeStruct
    parts = 4 if width % 512 == 0 else 1

    def kernel(body, flops, moved, **options):
        return pl.pallas_call(
            body,
            cost_estimate=pl.CostEstimate(flops=flops, bytes_accessed=moved, transcendentals=0),
            compiler_params=pltpu.CompilerParams(vmem_limit_bytes=16 * 2**20),
            **options,
        )

    def along_row(piece, k):
        route = [(g, g // n_col * n_col + (g + k) % n_col) for g in range(n_group)]
        return lax.ppermute(piece, "group", route)

    def along_column(piece, k):
        route = [(g, (g // n_col + k) % n_row * n_col + g % n_col) for g in range(n_group)]
        return lax.ppermute(piece, "group", route)

    def to_block(piece, distance):
        return lax.ppermute(piece, "blk", [(i, (i + distance) % n_blk) for i in range(n_blk)])

    unit_shapes = (shape((rows, emb), F32), shape((rows, 1), F32), shape((rows, emb), BF16))
    txt_unit, txt_inv, txt_low = kernel(
        text_kernel,
        2 * rows * width * emb * 20,
        20 * width * (rows + emb),
        out_shape=unit_shapes,
        in_specs=[VMEM],
        out_specs=(VMEM,) * 3,
    )(text_emb)
    texts = [txt_low] + [along_column(txt_low, k) for k in range(1, n_row)]
    earlier_texts = [to_block(piece, 1) for piece in texts]

    img_unit, img_inv, img_low = kernel(
        project_kernel,
        2 * rows * width * emb,
        2 * width * (rows + emb),
        out_shape=unit_shapes,
        in_specs=[VMEM] * 2,
        out_specs=(VMEM,) * 3,
    )(img_feat, head_weight)

    images = [img_low] + [along_row(img_low, k) for k in range(1, n_col)]
    later_images = [to_block(piece, -1) for piece in images]

    def meetings(left, right, after):
        n_left = len(left)
        return kernel(
            functools.partial(meet_kernel, n_left),
            4 * n_left * len(right) * rows * rows * emb,
            2 * rows * emb * (2 * n_left + len(right)),
            out_shape=(shape((rows, emb), F32),) + (shape((rows, emb), BF16),) * (n_left - 1),
            in_specs=[VMEM] * 2 + [ANY] + [VMEM] * (n_left + len(right)),
            out_specs=(VMEM,) * n_left,
        )(natural_exponent_factor.reshape(1, 1), bias.reshape(1, 1), after, *left, *right)

    grad_img, *img_terms = meetings(images, texts + earlier_texts, bias)
    img_peers = [along_row(term, -k) for k, term in enumerate(img_terms, 1)]
    grad_txt, *txt_terms = meetings(texts, images + later_images, grad_img)
    txt_peers = [along_column(term, -k) for k, term in enumerate(txt_terms, 1)]

    d_feat, flag = kernel(
        feat_kernel,
        2 * rows * width * emb,
        4 * width * (rows + emb),
        out_shape=(shape((rows, width), F32), shape((8, 128), F32)),
        in_specs=[VMEM] * (4 + len(img_peers)),
        out_specs=(HBM, VMEM),
        scratch_shapes=[pltpu.VMEM((rows, width), F32), pltpu.SemaphoreType.DMA((parts,))],
    )(grad_img, img_unit, img_inv, head_weight, *img_peers)

    d_text = kernel(
        text_out_kernel,
        8 * rows * emb,
        12 * rows * emb,
        out_shape=shape((rows, emb), F32),
        in_specs=[ANY] + [VMEM] * (3 + len(txt_peers)),
        out_specs=VMEM,
    )(flag, grad_txt, txt_unit, txt_inv, *txt_peers)
    return d_feat, d_text


def solution(mesh):
    return jax.shard_map(
        body,
        mesh=mesh,
        in_specs=(P(("blk", "group"), None), P(), P(("blk", "group"), None), P(), P()),
        out_specs=(P(("blk", "group"), None), P(("blk", "group"), None)),
        check_vma=False,
    )
```

time: 40.9 us -> 24.4 us (0.60)
  Pallas kernels: 15.6 us -> 4.86 us
  starting transfers between devices: 14.5 us -> 11.8 us
  local copies, waits for them, and re-layouts: 3.35 us -> 1.06 us
  waiting for transfers between devices: 5.17 us -> 4.61 us
    pallas_call x5 -> x6, Pallas kernels: 15.6 us -> 4.86 us  [the longest x1 1.97 us: body(): kernel(feat_kernel, 2 * rows * width * emb, 4 * width * (rows + emb), out...]
    ppermute x4, waiting for transfers between devices: 3.79 us -> 1.2 us  [to_block(): lax.ppermute(piece, 'blk', [(i, (i + distance) % n_blk) for i in range(n_...]
    unnamed x22 -> x6, local copies, waits for them, and re-layouts: 3.35 us -> 1.06 us
    ppermute x6 -> x4, waiting for transfers between devices: 1.38 us -> 3.41 us  [the longest x2 2.23 us: along_column(): return lax.ppermute(piece, 'group', route)]
    ppermute x6 -> x4, starting transfers between devices: 9.4 us -> 7.81 us  [the longest x2 4.62 us: along_column(): return lax.ppermute(piece, 'group', route)]
    ppermute x4, starting transfers between devices: 5.05 us -> 3.94 us  [to_block(): lax.ppermute(piece, 'blk', [(i, (i + distance) % n_blk) for i in range(n_...]
  transfers between devices with their start and end apart: 10 -> 8, of which waited for: 2 -> 4; matrix products, arithmetic and copies ran while one was open for 0% -> 0% of each run, Pallas kernels for 26% -> 16%
where the time goes in v3:
time: 24.4 us; the launch traced here: 24.3 us
  starting transfers between devices  11.8 us (48%)
  Pallas kernels  4.86 us (20%)
  waiting for transfers between devices  4.61 us (19%)
  between operations  2 us (8%)
  local copies, waits for them, and re-layouts  1.06 us (4%)
    ppermute x2, starting transfers between devices, along_column(): return lax.ppermute(piece, 'group', route)  4.62 us
    ppermute x4, starting transfers between devices, to_block(): lax.ppermute(piece, 'blk', [(i, (i + distance) % n_blk) for i in range(n_...  3.94 us
    ppermute x2, starting transfers between devices, along_row(): return lax.ppermute(piece, 'group', route)  3.19 us
    ppermute x2, waiting for transfers between devices, along_column(): return lax.ppermute(piece, 'group', route)  2.23 us
    pallas_call x1, Pallas kernels, body(): kernel(feat_kernel, 2 * rows * width * emb, 4 * width * (rows + emb), out...  1.97 us
    pallas_call x2, Pallas kernels, meetings(): kernel(functools.partial(meet_kernel, n_left), 4 * n_left * len(right) *...  1.24 us
    ppermute x4, waiting for transfers between devices, to_block(): lax.ppermute(piece, 'blk', [(i, (i + distance) % n_blk) for i in range(n_...  1.2 us
    ppermute x2, waiting for transfers between devices, along_row(): return lax.ppermute(piece, 'group', route)  1.18 us
  transfers between devices with their start and end apart: 8, of which 4 were waited for; matrix products, arithmetic and copies ran while one was open for 0% of the time, Pallas kernels for 16%

profile of v3, /device:TPU:0, one launch (start us, length us, event | category | flops | bytes accessed | tf_op | source)
XLA Modules:
  0.0 24.3 jit_solution(12291473420446178587)
XLA Ops:
  0.6 0.0 copy-start
  0.6 0.0 copy-start.1
  0.6 0.0 copy-start.2
  0.7 1.0 %copy-done.2 = bf16[128,512]{1,0:T(8,128)(2,1)S(1)} copy-done((bf16[128,512]{1,0:T(8,128)(2,1)S(1)}, bf16[128,512]{1,0:T(8,128)(2,1)}, u32[]{:S(2)}) %copy-start.2) | copy-done | bytes 131096
  1.7 0.1 shard_map.69
  1.8 3.0 %collective-permute-start.1 = (bf16[128,512]{1,0:T(8,128)(2,1)S(1)}, bf16[128,512]{1,0:T(8,128)(2,1)S(1)}, u32[]{:S(2)}, u32[]{:S(2)}) collective-permute-start(bf16[128,512]{1,0:T(8,128)(2,1)S(1)} %get-tuple-element.15.refs_2_.refs_0_), channel_id=1, source_target_pairs={{0,2},{1,3},{2,0},{3,1},{4,6},{5,7},{6,4},{7,5},{8,10},{9,11},{10,... | collective-permute-start | bytes 393224 | tf_op jit(solution)/shard_map/ppermute | solution.py:118
  4.9 0.0 copy-done
  4.9 0.0 copy-done.1
  4.9 0.7 %shard_map.68 = (f32[128,512]{1,0:T(8,128)S(1)}, f32[128,1]{1,0:T(8,128)S(1)}, bf16[128,512]{1,0:T(8,128)(2,1)S(1)}) custom-call(bf16[128,3072]{1,0:T(8,128)(2,1)S(1)} %copy-done.1, bf16[3072,512]{1,0:T(8,128)(2,1)S(1)} %copy-done), custom_call_target="tpu_custom_call" | custom-call | flops 402653184 | bytes 3932160 | tf_op jit(solution)/shard_map/pallas_call | solution.py:135
  5.5 1.6 %collective-permute-start = (bf16[128,512]{1,0:T(8,128)(2,1)S(1)}, bf16[128,512]{1,0:T(8,128)(2,1)S(1)}, u32[]{:S(2)}, u32[]{:S(2)}) collective-permute-start(bf16[128,512]{1,0:T(8,128)(2,1)S(1)} %get-tuple-element.14.refs_0_.refs_2_), channel_id=1, source_target_pairs={{0,1},{1,0},{2,3},{3,2},{4,5},{5,4},{6,7},{7,6},{8,9},{9,8},{10,11... | collective-permute-start | bytes 393224 | tf_op jit(solution)/shard_map/ppermute | solution.py:114
  7.1 0.0 collective-permute-start.2
  7.1 1.3 %collective-permute-done.1.refs_3_.refs_1_ = bf16[128,512]{1,0:T(8,128)(2,1)S(1)} collective-permute-done((bf16[128,512]{1,0:T(8,128)(2,1)S(1)}, bf16[128,512]{1,0:T(8,128)(2,1)S(1)}, u32[]{:S(2)}, u32[]{:S(2)}) %collective-permute-start.1) | collective-permute-done | bytes 131104 | tf_op jit(solution)/shard_map/ppermute | solution.py:118
  8.4 0.4 %collective-permute-start.3 = (bf16[128,512]{1,0:T(8,128)(2,1)S(1)}, bf16[128,512]{1,0:T(8,128)(2,1)S(1)}, u32[]{:S(2)}, u32[]{:S(2)}) collective-permute-start(bf16[128,512]{1,0:T(8,128)(2,1)S(1)} %collective-permute-done.1.refs_3_.refs_1_), channel_id=1, source_target_pairs={{0,4},{4,8},{8,12},{12,16},{16,20},{20,24},{24,28},{28,0},{1,5},{5... | collective-permute-start | bytes 393224 | tf_op jit(solution)/shard_map/ppermute | solution.py:121
  8.8 3.1 %collective-permute-start.5 = (bf16[128,512]{1,0:T(8,128)(2,1)S(1)}, bf16[128,512]{1,0:T(8,128)(2,1)S(1)}, u32[]{:S(2)}, u32[]{:S(2)}) collective-permute-start(bf16[128,512]{1,0:T(8,128)(2,1)S(1)} %get-tuple-element.14.refs_0_.refs_2_), channel_id=1, source_target_pairs={{0,28},{4,0},{8,4},{12,8},{16,12},{20,16},{24,20},{28,24},{1,29},{... | collective-permute-start | bytes 393224 | tf_op jit(solution)/shard_map/ppermute | solution.py:121
  11.9 0.0 collective-permute-done.refs_1_.refs_3_
  11.9 0.4 %collective-permute-start.6 = (bf16[128,512]{1,0:T(8,128)(2,1)S(1)}, bf16[128,512]{1,0:T(8,128)(2,1)S(1)}, u32[]{:S(2)}, u32[]{:S(2)}) collective-permute-start(bf16[128,512]{1,0:T(8,128)(2,1)S(1)} %collective-permute-done.refs_1_.refs_3_), channel_id=1, source_target_pairs={{0,28},{4,0},{8,4},{12,8},{16,12},{20,16},{24,20},{28,24},{1,29},{... | collective-permute-start | bytes 393224 | tf_op jit(solution)/shard_map/ppermute | solution.py:121
  13.6 0.0 collective-permute-done.2.refs_4_
  13.6 1.2 %collective-permute-done.3.refs_5_ = bf16[128,512]{1,0:T(8,128)(2,1)S(1)} collective-permute-done((bf16[128,512]{1,0:T(8,128)(2,1)S(1)}, bf16[128,512]{1,0:T(8,128)(2,1)S(1)}, u32[]{:S(2)}, u32[]{:S(2)}) %collective-permute-start.3) | collective-permute-done | bytes 131104 | tf_op jit(solution)/shard_map/ppermute | solution.py:121
  14.8 0.6 %shard_map.70 = (f32[128,512]{1,0:T(8,128)S(1)}, bf16[128,512]{1,0:T(8,128)(2,1)S(1)}) custom-call(f32[1,1]{1,0:T(1,128)} %bitcast.2.factor_ref, f32[1,1]{1,0:T(1,128)} %bitcast.4.bias_ref, f32[1]{0:T(128)} %copy.8.after_ref, bf16[128,512]{1,0:T(8,128)(2,1)S(1)} %get-tuple-element.14.refs_0_.refs_2_, ...), custom_call_target="tpu_custom_call" | custom-call | flops 268435456 | bytes 1048576 | tf_op jit(solution)/shard_map/pallas_call | solution.py:149
  15.4 1.6 %collective-permute-start.4 = (bf16[128,512]{1,0:T(8,128)(2,1)S(1)}, bf16[128,512]{1,0:T(8,128)(2,1)S(1)}, u32[]{:S(2)}, u32[]{:S(2)}) collective-permute-start(bf16[128,512]{1,0:T(8,128)(2,1)S(1)} %get-tuple-element.19), channel_id=1, source_target_pairs={{0,1},{1,0},{2,3},{3,2},{4,5},{5,4},{6,7},{7,6},{8,9},{9,8},{10,11... | collective-permute-start | bytes 393224 | tf_op jit(solution)/shard_map/ppermute | solution.py:114
  17.1 0.0 collective-permute-done.5.refs_4_
  17.1 0.0 collective-permute-done.6.refs_5_
  17.1 0.6 %shard_map.72 = (f32[128,512]{1,0:T(8,128)S(1)}, bf16[128,512]{1,0:T(8,128)(2,1)S(1)}) custom-call(f32[1,1]{1,0:T(1,128)} %bitcast.3.factor_ref, f32[1,1]{1,0:T(1,128)} %bitcast.5.bias_ref, f32[128,512]{1,0:T(8,128)S(1)} %get-tuple-element.16.grad_ref.after_ref, bf16[128,512]{1,0:T(8,128)(2,1)S(1)} %get-tuple-element.15.refs_2_.refs_0_, ...), custom_call_target="tpu_custom_call" | custom-call | flops 268435456 | bytes 1048576 | tf_op jit(solution)/shard_map/pallas_call | solution.py:149
  17.7 1.6 %collective-permute-start.7 = (bf16[128,512]{1,0:T(8,128)(2,1)S(1)}, bf16[128,512]{1,0:T(8,128)(2,1)S(1)}, u32[]{:S(2)}, u32[]{:S(2)}) collective-permute-start(bf16[128,512]{1,0:T(8,128)(2,1)S(1)} %get-tuple-element.25), channel_id=1, source_target_pairs={{0,2},{1,3},{2,0},{3,1},{4,6},{5,7},{6,4},{7,5},{8,10},{9,11},{10,... | collective-permute-start | bytes 393224 | tf_op jit(solution)/shard_map/ppermute | solution.py:118
  19.3 1.2 %collective-permute-done.4.refs_0_ = bf16[128,512]{1,0:T(8,128)(2,1)S(1)} collective-permute-done((bf16[128,512]{1,0:T(8,128)(2,1)S(1)}, bf16[128,512]{1,0:T(8,128)(2,1)S(1)}, u32[]{:S(2)}, u32[]{:S(2)}) %collective-permute-start.4) | collective-permute-done | bytes 131104 | tf_op jit(solution)/shard_map/ppermute | solution.py:114
  20.5 2.0 %shard_map.71 = (f32[128,3072]{1,0:T(8,128)}, f32[8,128]{1,0:T(8,128)S(1)}) custom-call(f32[128,512]{1,0:T(8,128)S(1)} %get-tuple-element.16.grad_ref.after_ref, f32[128,512]{1,0:T(8,128)S(1)} %get-tuple-element.17.unit_ref, f32[128,1]{1,0:T(8,128)S(1)} %get-tuple-element.18.inv_ref, bf16[3072,512]{1,0:T(8,128)(2,1)S(1)} %copy-done, ...), custom_call_target="tpu_custom_call" | custom-call | flops 402653184 | bytes 7864320 | tf_op jit(solution)/shard_map/pallas_call | solution.py:163
  22.4 1.0 %collective-permute-done.7.refs_0_ = bf16[128,512]{1,0:T(8,128)(2,1)S(1)} collective-permute-done((bf16[128,512]{1,0:T(8,128)(2,1)S(1)}, bf16[128,512]{1,0:T(8,128)(2,1)S(1)}, u32[]{:S(2)}, u32[]{:S(2)}) %collective-permute-start.7) | collective-permute-done | bytes 131104 | tf_op jit(solution)/shard_map/ppermute | solution.py:118
  23.4 0.9 %shard_map.73 = f32[128,512]{1,0:T(8,128)} custom-call(f32[8,128]{1,0:T(8,128)S(1)} %get-tuple-element.21.after_ref, f32[128,512]{1,0:T(8,128)S(1)} %get-tuple-element.22.grad_ref, f32[128,512]{1,0:T(8,128)S(1)} %get-tuple-element.23.unit_ref, f32[128,1]{1,0:T(8,128)S(1)} %get-tuple-element.24.inv_ref, bf16[128,512]{1,0:T(8,128)(2,1)S(1)} %collective-permute-done.7.refs_0_), custom_call_target="tpu_custom_call" | custom-call | flops 524288 | bytes 786432 | tf_op jit(solution)/shard_map/pallas_call | solution.py:173
Async XLA Ops:
  0.6 4.2 %copy-start = (bf16[3072,512]{1,0:T(8,128)(2,1)S(1)}, bf16[3072,512]{1,0:T(8,128)(2,1)}, u32[]{:S(2)}) copy-start(bf16[3072,512]{1,0:T(8,128)(2,1)} %head_ref.3) | copy-start | bytes 9437188
  0.6 4.2 %copy-start.1 = (bf16[128,3072]{1,0:T(8,128)(2,1)S(1)}, bf16[128,3072]{1,0:T(8,128)(2,1)}, u32[]{:S(2)}) copy-start(bf16[128,3072]{1,0:T(8,128)(2,1)} %img_ref.1) | copy-start | bytes 2359300
  0.6 1.1 %copy-start.2 = (bf16[128,512]{1,0:T(8,128)(2,1)S(1)}, bf16[128,512]{1,0:T(8,128)(2,1)}, u32[]{:S(2)}) copy-start(bf16[128,512]{1,0:T(8,128)(2,1)} %text_ref.1) | copy-start | bytes 393220
  1.8 6.5 %collective-permute-start.1 = (bf16[128,512]{1,0:T(8,128)(2,1)S(1)}, bf16[128,512]{1,0:T(8,128)(2,1)S(1)}, u32[]{:S(2)}, u32[]{:S(2)}) collective-permute-start(bf16[128,512]{1,0:T(8,128)(2,1)S(1)} %get-tuple-element.15.refs_2_.refs_0_), channel_id=1, source_target_pairs={{0,2},{1,3},{2,0},{3,1},{4,6},{5,7},{6,4},{7,5},{8,10},{9,11},{10,... | collective-permute-start | bytes 393224 | tf_op jit(solution)/shard_map/ppermute | solution.py:118
  5.5 6.4 %collective-permute-start = (bf16[128,512]{1,0:T(8,128)(2,1)S(1)}, bf16[128,512]{1,0:T(8,128)(2,1)S(1)}, u32[]{:S(2)}, u32[]{:S(2)}) collective-permute-start(bf16[128,512]{1,0:T(8,128)(2,1)S(1)} %get-tuple-element.14.refs_0_.refs_2_), channel_id=1, source_target_pairs={{0,1},{1,0},{2,3},{3,2},{4,5},{5,4},{6,7},{7,6},{8,9},{9,8},{10,11... | collective-permute-start | bytes 393224 | tf_op jit(solution)/shard_map/ppermute | solution.py:114
  7.1 6.5 %collective-permute-start.2 = (bf16[128,512]{1,0:T(8,128)(2,1)S(1)}, bf16[128,512]{1,0:T(8,128)(2,1)S(1)}, u32[]{:S(2)}, u32[]{:S(2)}) collective-permute-start(bf16[128,512]{1,0:T(8,128)(2,1)S(1)} %get-tuple-element.15.refs_2_.refs_0_), channel_id=1, source_target_pairs={{0,4},{4,8},{8,12},{12,16},{16,20},{20,24},{24,28},{28,0},{1,5},{5... | collective-permute-start | bytes 393224 | tf_op jit(solution)/shard_map/ppermute | solution.py:121
  8.4 6.4 %collective-permute-start.3 = (bf16[128,512]{1,0:T(8,128)(2,1)S(1)}, bf16[128,512]{1,0:T(8,128)(2,1)S(1)}, u32[]{:S(2)}, u32[]{:S(2)}) collective-permute-start(bf16[128,512]{1,0:T(8,128)(2,1)S(1)} %collective-permute-done.1.refs_3_.refs_1_), channel_id=1, source_target_pairs={{0,4},{4,8},{8,12},{12,16},{16,20},{20,24},{24,28},{28,0},{1,5},{5... | collective-permute-start | bytes 393224 | tf_op jit(solution)/shard_map/ppermute | solution.py:121
  8.8 8.3 %collective-permute-start.5 = (bf16[128,512]{1,0:T(8,128)(2,1)S(1)}, bf16[128,512]{1,0:T(8,128)(2,1)S(1)}, u32[]{:S(2)}, u32[]{:S(2)}) collective-permute-start(bf16[128,512]{1,0:T(8,128)(2,1)S(1)} %get-tuple-element.14.refs_0_.refs_2_), channel_id=1, source_target_pairs={{0,28},{4,0},{8,4},{12,8},{16,12},{20,16},{24,20},{28,24},{1,29},{... | collective-permute-start | bytes 393224 | tf_op jit(solution)/shard_map/ppermute | solution.py:121
  11.9 5.2 %collective-permute-start.6 = (bf16[128,512]{1,0:T(8,128)(2,1)S(1)}, bf16[128,512]{1,0:T(8,128)(2,1)S(1)}, u32[]{:S(2)}, u32[]{:S(2)}) collective-permute-start(bf16[128,512]{1,0:T(8,128)(2,1)S(1)} %collective-permute-done.refs_1_.refs_3_), channel_id=1, source_target_pairs={{0,28},{4,0},{8,4},{12,8},{16,12},{20,16},{24,20},{28,24},{1,29},{... | collective-permute-start | bytes 393224 | tf_op jit(solution)/shard_map/ppermute | solution.py:121
  15.4 5.0 %collective-permute-start.4 = (bf16[128,512]{1,0:T(8,128)(2,1)S(1)}, bf16[128,512]{1,0:T(8,128)(2,1)S(1)}, u32[]{:S(2)}, u32[]{:S(2)}) collective-permute-start(bf16[128,512]{1,0:T(8,128)(2,1)S(1)} %get-tuple-element.19), channel_id=1, source_target_pairs={{0,1},{1,0},{2,3},{3,2},{4,5},{5,4},{6,7},{7,6},{8,9},{9,8},{10,11... | collective-permute-start | bytes 393224 | tf_op jit(solution)/shard_map/ppermute | solution.py:114
  17.7 5.7 %collective-permute-start.7 = (bf16[128,512]{1,0:T(8,128)(2,1)S(1)}, bf16[128,512]{1,0:T(8,128)(2,1)S(1)}, u32[]{:S(2)}, u32[]{:S(2)}) collective-permute-start(bf16[128,512]{1,0:T(8,128)(2,1)S(1)} %get-tuple-element.25), channel_id=1, source_target_pairs={{0,2},{1,3},{2,0},{3,1},{4,6},{5,7},{6,4},{7,5},{8,10},{9,11},{10,... | collective-permute-start | bytes 393224 | tf_op jit(solution)/shard_map/ppermute | solution.py:118

commit v4 on v3

--- a/solution.py
+++ b/solution.py
@@ -27,14 +27,7 @@
     return (grad_in - unit_rows * jnp.sum(unit_rows * grad_in, axis=-1, keepdims=True)) * inverse
 
 
-def text_kernel(text_ref, unit_ref, inv_ref, low_ref):
-    unit, inverse = to_unit(text_ref[...].astype(F32))
-    unit_ref[...] = unit
-    inv_ref[...] = inverse
-    low_ref[...] = unit.astype(BF16)
-
-
-def project_kernel(img_ref, head_ref, unit_ref, inv_ref, low_ref):
+def project_kernel(after_ref, img_ref, head_ref, unit_ref, inv_ref, low_ref):
     projected = jnp.dot(img_ref[...], head_ref[...], preferred_element_type=F32)
     unit, inverse = to_unit(projected)
     unit_ref[...] = unit
@@ -51,14 +44,19 @@
     return scale * jnp.dot(weight, right, preferred_element_type=F32)
 
 
-def meet_kernel(n_left, factor_ref, bias_ref, after_ref, *refs):
+def text_low(ref):
+    return to_unit(ref[...].astype(F32))[0].astype(BF16)
+
+
+def meet_kernel(left_is_text, n_left, n_out, scalar_ref, after_ref, *refs):
     left_refs, refs = refs[:n_left], refs[n_left:]
-    right_refs, (grad_ref, *out_refs) = refs[:-n_left], refs[-n_left:]
+    right_refs, (grad_ref, *out_refs) = refs[:-n_out], refs[-n_out:]
     rows = grad_ref.shape[0]
-    left = jnp.concatenate([ref[...] for ref in left_refs], axis=0)
-    right = jnp.concatenate([ref[...] for ref in right_refs], axis=0)
-    scale = jnp.exp(factor_ref[...])
-    grad = meet(scale, bias_ref[...], left, right, rows)
+    plain = lambda ref: ref[...]
+    read_left, read_right = (text_low, plain) if left_is_text else (plain, text_low)
+    left = jnp.concatenate([read_left(ref) for ref in left_refs], axis=0)
+    right = jnp.concatenate([read_right(ref) for ref in right_refs], axis=0)
+    grad = meet(scalar_ref[0:1, 0:1], scalar_ref[1:2, 0:1], left, right, rows)
     grad_ref[...] = grad[:rows]
     for k, ref in enumerate(out_refs, 1):
         ref[...] = grad[k * rows : (k + 1) * rows].astype(BF16)
@@ -84,12 +82,17 @@
     flag_ref[...] = jnp.zeros_like(flag_ref)
 
 
-def text_out_kernel(after_ref, grad_ref, unit_ref, inv_ref, *refs):
+def mark_kernel(*refs):
+    refs[-1][...] = jnp.zeros_like(refs[-1])
+
+
+def text_out_kernel(after_ref, grad_ref, text_ref, *refs):
     peer_refs, out_ref = refs[:-1], refs[-1]
     grad = grad_ref[...]
     for ref in peer_refs:
         grad += ref[...].astype(F32)
-    out_ref[...] = unit_back(grad, unit_ref[...], inv_ref[...])
+    unit, inverse = to_unit(text_ref[...].astype(F32))
+    out_ref[...] = unit_back(grad, unit, inverse)
 
 
 def body(img_feat, head_weight, text_emb, natural_exponent_factor, bias):
@@ -109,56 +112,70 @@
             **options,
         )
 
-    def along_row(piece, k):
-        route = [(g, g // n_col * n_col + (g + k) % n_col) for g in range(n_group)]
-        return lax.ppermute(piece, "group", route)
-
-    def along_column(piece, k):
-        route = [(g, (g // n_col + k) % n_row * n_col + g % n_col) for g in range(n_group)]
-        return lax.ppermute(piece, "group", route)
-
-    def to_block(piece, distance):
-        return lax.ppermute(piece, "blk", [(i, (i + distance) % n_blk) for i in range(n_blk)])
+    side = n_col if n_row == n_col else 0
+
+    def route(image_side, distance, k):
+        pairs = []
+        for i in range(n_blk):
+            j = (i + distance) % n_blk
+            along_row = image_side if side == 0 or j % 2 == 0 else not image_side
+            for g in range(n_group):
+                r, c = g // n_col, g % n_col
+                r, c = (r, (c + k) % n_col) if along_row else ((r + k) % n_row, c)
+                pairs.append((i * n_group + g, j * n_group + r * n_col + c))
+        return pairs
+
+    def send(piece, image_side, distance, k):
+        return lax.ppermute(piece, ("blk", "group"), route(image_side, distance, k))
+
+    def marked(after):
+        return kernel(
+            mark_kernel,
+            2 * rows * emb,
+            4 * rows * emb,
+            out_shape=shape((8, 128), F32),
+            in_specs=[ANY] * len(after),
+            out_specs=VMEM,
+        )(*after)
+
+    first = lax.broadcasted_iota(jnp.int32, (8, 128), 0) == 0
+    scalars = jnp.where(first, jnp.exp(natural_exponent_factor[0]), bias[0])
 
     unit_shapes = (shape((rows, emb), F32), shape((rows, 1), F32), shape((rows, emb), BF16))
-    txt_unit, txt_inv, txt_low = kernel(
-        text_kernel,
-        2 * rows * width * emb * 20,
-        20 * width * (rows + emb),
-        out_shape=unit_shapes,
-        in_specs=[VMEM],
-        out_specs=(VMEM,) * 3,
-    )(text_emb)
-    texts = [txt_low] + [along_column(txt_low, k) for k in range(1, n_row)]
-    earlier_texts = [to_block(piece, 1) for piece in texts]
+    early = kernel(
+        mark_kernel, 40 * rows * width * emb, 20 * width * (rows + emb), out_shape=shape((8, 128), F32), out_specs=VMEM
+    )()
+    early = lax.ppermute(early, "blk", [(i, i ^ 1 if n_blk % 2 == 0 else i) for i in range(n_blk)])
+    earlier_texts = [send(text_emb, False, 1, k) for k in range(n_row)]
+    texts = [text_emb] + [send(text_emb, False, 0, k) for k in range(1, n_row)]
 
     img_unit, img_inv, img_low = kernel(
         project_kernel,
         2 * rows * width * emb,
         2 * width * (rows + emb),
         out_shape=unit_shapes,
-        in_specs=[VMEM] * 2,
+        in_specs=[ANY] + [VMEM] * 2,
         out_specs=(VMEM,) * 3,
-    )(img_feat, head_weight)
-
-    images = [img_low] + [along_row(img_low, k) for k in range(1, n_col)]
-    later_images = [to_block(piece, -1) for piece in images]
-
-    def meetings(left, right, after):
+    )(early, img_feat, head_weight)
+
+    images = [img_low] + [send(img_low, True, 0, k) for k in range(1, n_col)]
+    later_images = [send(img_low, True, -1, k) for k in range(n_col)]
+
+    def meetings(left, right, after, left_is_text):
         n_left = len(left)
         return kernel(
-            functools.partial(meet_kernel, n_left),
+            functools.partial(meet_kernel, left_is_text, n_left, sum(p.shape[0] for p in left) // rows),
             4 * n_left * len(right) * rows * rows * emb,
             2 * rows * emb * (2 * n_left + len(right)),
-            out_shape=(shape((rows, emb), F32),) + (shape((rows, emb), BF16),) * (n_left - 1),
-            in_specs=[VMEM] * 2 + [ANY] + [VMEM] * (n_left + len(right)),
-            out_specs=(VMEM,) * n_left,
-        )(natural_exponent_factor.reshape(1, 1), bias.reshape(1, 1), after, *left, *right)
-
-    grad_img, *img_terms = meetings(images, texts + earlier_texts, bias)
-    img_peers = [along_row(term, -k) for k, term in enumerate(img_terms, 1)]
-    grad_txt, *txt_terms = meetings(texts, images + later_images, grad_img)
-    txt_peers = [along_column(term, -k) for k, term in enumerate(txt_terms, 1)]
+            out_shape=(shape((rows, emb), F32),) + (shape((rows, emb), BF16),) * (sum(p.shape[0] for p in left) // rows - 1),
+            in_specs=[VMEM, ANY] + [VMEM] * (n_left + len(right)),
+            out_specs=(VMEM,) * (sum(p.shape[0] for p in left) // rows),
+        )(scalars, after, *left, *right)
+
+    grad_img, *img_terms = meetings(images, texts + earlier_texts, marked(earlier_texts), False)
+    img_peers = [send(term, True, 0, -k) for k, term in enumerate(img_terms, 1)]
+    grad_txt, *txt_terms = meetings(texts, images + later_images, grad_img, True)
+    txt_peers = [send(term, False, 0, -k) for k, term in enumerate(txt_terms, 1)]
 
     d_feat, flag = kernel(
         feat_kernel,
@@ -175,9 +192,9 @@
         8 * rows * emb,
         12 * rows * emb,
         out_shape=shape((rows, emb), F32),
-        in_specs=[ANY] + [VMEM] * (3 + len(txt_peers)),
+        in_specs=[ANY] + [VMEM] * (2 + len(txt_peers)),
         out_specs=VMEM,
-    )(flag, grad_txt, txt_unit, txt_inv, *txt_peers)
+    )(flag, grad_txt, text_emb, *txt_peers)
     return d_feat, d_text
 
 

time: 24.4 us -> 22.8 us (0.934)
  waiting for transfers between devices: 4.61 us -> 2.87 us
  starting transfers between devices: 11.8 us -> 12.8 us
  local copies, waits for them, and re-layouts: 1.06 us -> 0.08 us
    ppermute x8 -> x9, waiting for transfers between devices: 4.61 us -> 2.87 us  [the longest x8 2.87 us: send(): return lax.ppermute(piece, ('blk', 'group'), route(image_side, distance, k))]
    unnamed x6, local copies, waits for them, and re-layouts: 1.06 us -> 0.01 us
    ppermute x8 -> x9, starting transfers between devices: 11.8 us -> 12.8 us  [the longest x8 11.1 us: send(): return lax.ppermute(piece, ('blk', 'group'), route(image_side, distance, k))]
    pallas_call x3 -> x4, Pallas kernels: 1.36 us -> 1.36 us  [the longest x2 1.35 us: meetings(): kernel(functools.partial(meet_kernel, left_is_text, n_left, sum((p.shape[...]
  transfers between devices with their start and end apart: 8 -> 9, of which waited for: 4 -> 2; matrix products, arithmetic and copies ran while one was open for 0% -> 0% of each run, Pallas kernels for 16% -> 18%
where the time goes in v4:
time: 22.8 us; the launch traced here: 22.7 us
  starting transfers between devices  12.8 us (56%)
  Pallas kernels  4.9 us (21%)
  waiting for transfers between devices  2.87 us (13%)
  between operations  2.05 us (9%)
    ppermute x8, starting transfers between devices, send(): return lax.ppermute(piece, ('blk', 'group'), route(image_side, distance, k))  11.1 us
    ppermute x8, waiting for transfers between devices, send(): return lax.ppermute(piece, ('blk', 'group'), route(image_side, distance, k))  2.87 us
    pallas_call x1, Pallas kernels, body(): kernel(feat_kernel, 2 * rows * width * emb, 4 * width * (rows + emb), out...  1.97 us
    ppermute x1, starting transfers between devices, body(): lax.ppermute(early, 'blk', [(i, i ^ 1 if n_blk % 2 == 0 else i) for i in...  1.72 us
    pallas_call x2, Pallas kernels, meetings(): kernel(functools.partial(meet_kernel, left_is_text, n_left, sum((p.shape[...  1.35 us
    pallas_call x1, Pallas kernels, body(): kernel(text_out_kernel, 8 * rows * emb, 12 * rows * emb, out_shape=shape(...  0.91 us
    pallas_call x1, Pallas kernels, body(): kernel(project_kernel, 2 * rows * width * emb, 2 * width * (rows + emb),...  0.67 us
  transfers between devices with their start and end apart: 9, of which 2 were waited for; matrix products, arithmetic and copies ran while one was open for 0% of the time, Pallas kernels for 18%

profile of v4, /device:TPU:0, one launch (start us, length us, event | category | flops | bytes accessed | tf_op | source)
XLA Modules:
  0.0 22.7 jit_solution(10642198236014218116)
XLA Ops:
  0.6 0.0 copy-start.2
  0.6 0.0 copy-start
  0.6 0.0 copy-start.1
  0.7 2.4 %collective-permute-start.1 = (bf16[128,512]{1,0:T(8,128)(2,1)}, bf16[128,512]{1,0:T(8,128)(2,1)S(1)}, u32[]{:S(2)}, u32[]{:S(2)}) collective-permute-start(bf16[128,512]{1,0:T(8,128)(2,1)} %text_ref.1), channel_id=1, source_target_pairs={{0,5},{1,4},{2,7},{3,6},{4,10},{5,11},{6,8},{7,9},{8,13},{9,12},{1... | collective-permute-start | bytes 393224 | tf_op jit(solution)/shard_map/ppermute | solution.py:129
  3.1 1.7 %collective-permute-start.2 = (f32[8,128]{1,0:T(8,128)S(1)}, f32[8,128]{1,0:T(8,128)S(1)}, u32[]{:S(2)}, u32[]{:S(2)}) collective-permute-start(f32[8,128]{1,0:T(8,128)S(1)} %shard_map.69), channel_id=1, source_target_pairs={{0,4},{4,0},{8,12},{12,8},{16,20},{20,16},{24,28},{28,24},{1,5},{5... | collective-permute-start | bytes 12296 | tf_op jit(solution)/shard_map/ppermute | solution.py:148
  4.8 0.0 copy-done.2
  4.8 0.5 %collective-permute-start.4 = (bf16[128,512]{1,0:T(8,128)(2,1)S(1)}, bf16[128,512]{1,0:T(8,128)(2,1)S(1)}, u32[]{:S(2)}, u32[]{:S(2)}) collective-permute-start(bf16[128,512]{1,0:T(8,128)(2,1)S(1)} %copy-done.2), channel_id=1, source_target_pairs={{0,2},{1,3},{2,0},{3,1},{4,5},{5,4},{6,7},{7,6},{8,10},{9,11},{10,... | collective-permute-start | bytes 393224 | tf_op jit(solution)/shard_map/ppermute | solution.py:129
  5.3 0.8 %collective-permute-start = (bf16[128,512]{1,0:T(8,128)(2,1)S(1)}, bf16[128,512]{1,0:T(8,128)(2,1)S(1)}, u32[]{:S(2)}, u32[]{:S(2)}) collective-permute-start(bf16[128,512]{1,0:T(8,128)(2,1)S(1)} %copy-done.2), channel_id=1, source_target_pairs={{0,4},{1,5},{2,6},{3,7},{4,8},{5,9},{6,10},{7,11},{8,12},{9,13},{1... | collective-permute-start | bytes 393224 | tf_op jit(solution)/shard_map/ppermute | solution.py:129
  6.1 0.0 collective-permute-done.2.after_ref
  6.1 0.0 copy-done
  6.1 0.0 copy-done.1
  6.1 0.7 %shard_map.70 = (f32[128,512]{1,0:T(8,128)S(1)}, f32[128,1]{1,0:T(8,128)S(1)}, bf16[128,512]{1,0:T(8,128)(2,1)S(1)}) custom-call(f32[8,128]{1,0:T(8,128)S(1)} %collective-permute-done.2.after_ref, bf16[128,3072]{1,0:T(8,128)(2,1)S(1)} %copy-done.1, bf16[3072,512]{1,0:T(8,128)(2,1)S(1)} %copy-done), custom_call_target="tpu_custom_call" | custom-call | flops 402653184 | bytes 3932160 | tf_op jit(solution)/shard_map/pallas_call | solution.py:152
  6.8 1.1 %collective-permute-start.3 = (bf16[128,512]{1,0:T(8,128)(2,1)S(1)}, bf16[128,512]{1,0:T(8,128)(2,1)S(1)}, u32[]{:S(2)}, u32[]{:S(2)}) collective-permute-start(bf16[128,512]{1,0:T(8,128)(2,1)S(1)} %get-tuple-element.11.refs_0_.refs_2_), channel_id=1, source_target_pairs={{0,1},{1,0},{2,3},{3,2},{4,6},{5,7},{6,4},{7,5},{8,9},{9,8},{10,11... | collective-permute-start | bytes 393224 | tf_op jit(solution)/shard_map/ppermute | solution.py:129
  9.2 3.0 %collective-permute-start.7 = (bf16[128,512]{1,0:T(8,128)(2,1)S(1)}, bf16[128,512]{1,0:T(8,128)(2,1)S(1)}, u32[]{:S(2)}, u32[]{:S(2)}) collective-permute-start(bf16[128,512]{1,0:T(8,128)(2,1)S(1)} %get-tuple-element.11.refs_0_.refs_2_), channel_id=1, source_target_pairs={{0,30},{1,31},{2,28},{3,29},{4,1},{5,0},{6,3},{7,2},{8,6},{9,7},{1... | collective-permute-start | bytes 393224 | tf_op jit(solution)/shard_map/ppermute | solution.py:129
  12.2 0.0 collective-permute-done.1.refs_1_.refs_5_
  12.2 0.1 collective-permute-start.6
  12.3 0.0 collective-permute-done.refs_0_.refs_4_
  12.3 0.0 collective-permute-done.4.refs_3_.refs_1_
  12.3 0.0 collective-permute-done.3.refs_1_.refs_3_
  12.4 0.1 iota.7.scalar_ref
  12.4 0.7 %shard_map.71 = (f32[128,512]{1,0:T(8,128)S(1)}, bf16[128,512]{1,0:T(8,128)(2,1)S(1)}) custom-call(f32[8,128]{1,0:T(8,128)S(1)} %iota.7.scalar_ref, f32[8,128]{1,0:T(8,128)S(1)} %shard_map.68.after_ref, bf16[128,512]{1,0:T(8,128)(2,1)S(1)} %get-tuple-element.11.refs_0_.refs_2_, bf16[128,512]{1,0:T(8,128)(2,1)S(1)} %collective-permute-done.3.refs_1_.refs_3_, ...), custom_call_target="tpu_custom_call" | custom-call | flops 268435456 | bytes 1048576 | tf_op jit(solution)/shard_map/pallas_call | solution.py:166
  13.1 1.6 %collective-permute-start.5 = (bf16[128,512]{1,0:T(8,128)(2,1)S(1)}, bf16[128,512]{1,0:T(8,128)(2,1)S(1)}, u32[]{:S(2)}, u32[]{:S(2)}) collective-permute-start(bf16[128,512]{1,0:T(8,128)(2,1)S(1)} %get-tuple-element.15), channel_id=1, source_target_pairs={{0,1},{1,0},{2,3},{3,2},{4,6},{5,7},{6,4},{7,5},{8,9},{9,8},{10,11... | collective-permute-start | bytes 393224 | tf_op jit(solution)/shard_map/ppermute | solution.py:129
  14.7 0.0 collective-permute-done.7.refs_5_
  14.7 1.4 %collective-permute-done.6.refs_4_ = bf16[128,512]{1,0:T(8,128)(2,1)S(1)} collective-permute-done((bf16[128,512]{1,0:T(8,128)(2,1)S(1)}, bf16[128,512]{1,0:T(8,128)(2,1)S(1)}, u32[]{:S(2)}, u32[]{:S(2)}) %collective-permute-start.6) | collective-permute-done | bytes 131104 | tf_op jit(solution)/shard_map/ppermute | solution.py:129
  16.1 0.7 %shard_map.73 = (f32[128,512]{1,0:T(8,128)S(1)}, bf16[128,512]{1,0:T(8,128)(2,1)S(1)}) custom-call(f32[8,128]{1,0:T(8,128)S(1)} %iota.7.scalar_ref, f32[128,512]{1,0:T(8,128)S(1)} %get-tuple-element.12.grad_ref.after_ref, bf16[128,512]{1,0:T(8,128)(2,1)S(1)} %copy-done.2, bf16[128,512]{1,0:T(8,128)(2,1)S(1)} %collective-permute-done.4.refs_3_.refs_1_, ...), custom_call_target="tpu_custom_call" | custom-call | flops 268435456 | bytes 1048576 | tf_op jit(solution)/shard_map/pallas_call | solution.py:166
  16.7 1.6 %collective-permute-start.8 = (bf16[128,512]{1,0:T(8,128)(2,1)S(1)}, bf16[128,512]{1,0:T(8,128)(2,1)S(1)}, u32[]{:S(2)}, u32[]{:S(2)}) collective-permute-start(bf16[128,512]{1,0:T(8,128)(2,1)S(1)} %get-tuple-element.19), channel_id=1, source_target_pairs={{0,2},{1,3},{2,0},{3,1},{4,5},{5,4},{6,7},{7,6},{8,10},{9,11},{10,... | collective-permute-start | bytes 393224 | tf_op jit(solution)/shard_map/ppermute | solution.py:129
  18.3 0.0 collective-permute-done.5.refs_0_
  18.3 2.0 %shard_map.72 = (f32[128,3072]{1,0:T(8,128)}, f32[8,128]{1,0:T(8,128)S(1)}) custom-call(f32[128,512]{1,0:T(8,128)S(1)} %get-tuple-element.12.grad_ref.after_ref, f32[128,512]{1,0:T(8,128)S(1)} %get-tuple-element.13.unit_ref, f32[128,1]{1,0:T(8,128)S(1)} %get-tuple-element.14.inv_ref, bf16[3072,512]{1,0:T(8,128)(2,1)S(1)} %copy-done, ...), custom_call_target="tpu_custom_call" | custom-call | flops 402653184 | bytes 7864320 | tf_op jit(solution)/shard_map/pallas_call | solution.py:180
  20.3 1.5 %collective-permute-done.8.refs_0_ = bf16[128,512]{1,0:T(8,128)(2,1)S(1)} collective-permute-done((bf16[128,512]{1,0:T(8,128)(2,1)S(1)}, bf16[128,512]{1,0:T(8,128)(2,1)S(1)}, u32[]{:S(2)}, u32[]{:S(2)}) %collective-permute-start.8) | collective-permute-done | bytes 131104 | tf_op jit(solution)/shard_map/ppermute | solution.py:129
  21.8 0.9 %shard_map.74 = f32[128,512]{1,0:T(8,128)} custom-call(f32[8,128]{1,0:T(8,128)S(1)} %get-tuple-element.17.after_ref, f32[128,512]{1,0:T(8,128)S(1)} %get-tuple-element.18.grad_ref, bf16[128,512]{1,0:T(8,128)(2,1)S(1)} %copy-done.2, bf16[128,512]{1,0:T(8,128)(2,1)S(1)} %collective-permute-done.8.refs_0_), custom_call_target="tpu_custom_call" | custom-call | flops 524288 | bytes 786432 | tf_op jit(solution)/shard_map/pallas_call | solution.py:190
  (3 shorter events, 0.0 us)
Async XLA Ops:
  0.6 4.2 %copy-start.2 = (bf16[128,512]{1,0:T(8,128)(2,1)S(1)}, bf16[128,512]{1,0:T(8,128)(2,1)}, u32[]{:S(2)}) copy-start(bf16[128,512]{1,0:T(8,128)(2,1)} %text_ref.1) | copy-start | bytes 393220
  0.6 5.5 %copy-start = (bf16[3072,512]{1,0:T(8,128)(2,1)S(1)}, bf16[3072,512]{1,0:T(8,128)(2,1)}, u32[]{:S(2)}) copy-start(bf16[3072,512]{1,0:T(8,128)(2,1)} %head_ref.3) | copy-start | bytes 9437188
  0.6 5.4 %copy-start.1 = (bf16[128,3072]{1,0:T(8,128)(2,1)S(1)}, bf16[128,3072]{1,0:T(8,128)(2,1)}, u32[]{:S(2)}) copy-start(bf16[128,3072]{1,0:T(8,128)(2,1)} %img_ref.1) | copy-start | bytes 2359300
  0.7 11.5 %collective-permute-start.1 = (bf16[128,512]{1,0:T(8,128)(2,1)}, bf16[128,512]{1,0:T(8,128)(2,1)S(1)}, u32[]{:S(2)}, u32[]{:S(2)}) collective-permute-start(bf16[128,512]{1,0:T(8,128)(2,1)} %text_ref.1), channel_id=1, source_target_pairs={{0,5},{1,4},{2,7},{3,6},{4,10},{5,11},{6,8},{7,9},{8,13},{9,12},{1... | collective-permute-start | bytes 393224 | tf_op jit(solution)/shard_map/ppermute | solution.py:129
  3.1 3.0 %collective-permute-start.2 = (f32[8,128]{1,0:T(8,128)S(1)}, f32[8,128]{1,0:T(8,128)S(1)}, u32[]{:S(2)}, u32[]{:S(2)}) collective-permute-start(f32[8,128]{1,0:T(8,128)S(1)} %shard_map.69), channel_id=1, source_target_pairs={{0,4},{4,0},{8,12},{12,8},{16,20},{20,16},{24,28},{28,24},{1,5},{5... | collective-permute-start | bytes 12296 | tf_op jit(solution)/shard_map/ppermute | solution.py:148
  4.8 7.5 %collective-permute-start.4 = (bf16[128,512]{1,0:T(8,128)(2,1)S(1)}, bf16[128,512]{1,0:T(8,128)(2,1)S(1)}, u32[]{:S(2)}, u32[]{:S(2)}) collective-permute-start(bf16[128,512]{1,0:T(8,128)(2,1)S(1)} %copy-done.2), channel_id=1, source_target_pairs={{0,2},{1,3},{2,0},{3,1},{4,5},{5,4},{6,7},{7,6},{8,10},{9,11},{10,... | collective-permute-start | bytes 393224 | tf_op jit(solution)/shard_map/ppermute | solution.py:129
  5.3 7.0 %collective-permute-start = (bf16[128,512]{1,0:T(8,128)(2,1)S(1)}, bf16[128,512]{1,0:T(8,128)(2,1)S(1)}, u32[]{:S(2)}, u32[]{:S(2)}) collective-permute-start(bf16[128,512]{1,0:T(8,128)(2,1)S(1)} %copy-done.2), channel_id=1, source_target_pairs={{0,4},{1,5},{2,6},{3,7},{4,8},{5,9},{6,10},{7,11},{8,12},{9,13},{1... | collective-permute-start | bytes 393224 | tf_op jit(solution)/shard_map/ppermute | solution.py:129
  6.8 5.6 %collective-permute-start.3 = (bf16[128,512]{1,0:T(8,128)(2,1)S(1)}, bf16[128,512]{1,0:T(8,128)(2,1)S(1)}, u32[]{:S(2)}, u32[]{:S(2)}) collective-permute-start(bf16[128,512]{1,0:T(8,128)(2,1)S(1)} %get-tuple-element.11.refs_0_.refs_2_), channel_id=1, source_target_pairs={{0,1},{1,0},{2,3},{3,2},{4,6},{5,7},{6,4},{7,5},{8,9},{9,8},{10,11... | collective-permute-start | bytes 393224 | tf_op jit(solution)/shard_map/ppermute | solution.py:129
  9.2 5.5 %collective-permute-start.7 = (bf16[128,512]{1,0:T(8,128)(2,1)S(1)}, bf16[128,512]{1,0:T(8,128)(2,1)S(1)}, u32[]{:S(2)}, u32[]{:S(2)}) collective-permute-start(bf16[128,512]{1,0:T(8,128)(2,1)S(1)} %get-tuple-element.11.refs_0_.refs_2_), channel_id=1, source_target_pairs={{0,30},{1,31},{2,28},{3,29},{4,1},{5,0},{6,3},{7,2},{8,6},{9,7},{1... | collective-permute-start | bytes 393224 | tf_op jit(solution)/shard_map/ppermute | solution.py:129
  12.2 3.9 %collective-permute-start.6 = (bf16[128,512]{1,0:T(8,128)(2,1)S(1)}, bf16[128,512]{1,0:T(8,128)(2,1)S(1)}, u32[]{:S(2)}, u32[]{:S(2)}) collective-permute-start(bf16[128,512]{1,0:T(8,128)(2,1)S(1)} %get-tuple-element.11.refs_0_.refs_2_), channel_id=1, source_target_pairs={{0,28},{1,29},{2,30},{3,31},{4,0},{5,1},{6,2},{7,3},{8,4},{9,5},{1... | collective-permute-start | bytes 393224 | tf_op jit(solution)/shard_map/ppermute | solution.py:129
  13.1 5.2 %collective-permute-start.5 = (bf16[128,512]{1,0:T(8,128)(2,1)S(1)}, bf16[128,512]{1,0:T(8,128)(2,1)S(1)}, u32[]{:S(2)}, u32[]{:S(2)}) collective-permute-start(bf16[128,512]{1,0:T(8,128)(2,1)S(1)} %get-tuple-element.15), channel_id=1, source_target_pairs={{0,1},{1,0},{2,3},{3,2},{4,6},{5,7},{6,4},{7,5},{8,9},{9,8},{10,11... | collective-permute-start | bytes 393224 | tf_op jit(solution)/shard_map/ppermute | solution.py:129
  16.7 5.0 %collective-permute-start.8 = (bf16[128,512]{1,0:T(8,128)(2,1)S(1)}, bf16[128,512]{1,0:T(8,128)(2,1)S(1)}, u32[]{:S(2)}, u32[]{:S(2)}) collective-permute-start(bf16[128,512]{1,0:T(8,128)(2,1)S(1)} %get-tuple-element.19), channel_id=1, source_target_pairs={{0,2},{1,3},{2,0},{3,1},{4,5},{5,4},{6,7},{7,6},{8,10},{9,11},{10,... | collective-permute-start | bytes 393224 | tf_op jit(solution)/shard_map/ppermute | solution.py:129

commit v5 on v4

--- a/solution.py
+++ b/solution.py
@@ -42,6 +42,11 @@
     positive = jnp.where((row_ids == col_ids) & (row_ids < rows), 1.0, 0.0)
     weight = (1.0 / (1.0 + jnp.exp(-z)) - positive).astype(BF16)
     return scale * jnp.dot(weight, right, preferred_element_type=F32)
+
+
+def scalar_kernel(factor_ref, bias_ref, *refs):
+    first = lax.broadcasted_iota(jnp.int32, refs[-1].shape, 0) == 0
+    refs[-1][...] = jnp.where(first, jnp.exp(jnp.full(refs[-1].shape, factor_ref[0], F32)), bias_ref[0])
 
 
 def text_low(ref):
@@ -138,8 +143,6 @@
             out_specs=VMEM,
         )(*after)
 
-    first = lax.broadcasted_iota(jnp.int32, (8, 128), 0) == 0
-    scalars = jnp.where(first, jnp.exp(natural_exponent_factor[0]), bias[0])
 
     unit_shapes = (shape((rows, emb), F32), shape((rows, 1), F32), shape((rows, emb), BF16))
     early = kernel(
@@ -172,7 +175,16 @@
             out_specs=(VMEM,) * (sum(p.shape[0] for p in left) // rows),
         )(scalars, after, *left, *right)
 
-    grad_img, *img_terms = meetings(images, texts + earlier_texts, marked(earlier_texts), False)
+    arrived = earlier_texts
+    scalars = kernel(
+        scalar_kernel,
+        0,
+        0,
+        out_shape=shape((8, 128), F32),
+        in_specs=[SMEM] * 2 + [ANY] * len(arrived),
+        out_specs=VMEM,
+    )(natural_exponent_factor, bias, *arrived)
+    grad_img, *img_terms = meetings(images, texts + earlier_texts, scalars, False)
     img_peers = [send(term, True, 0, -k) for k, term in enumerate(img_terms, 1)]
     grad_txt, *txt_terms = meetings(texts, images + later_images, grad_img, True)
     txt_peers = [send(term, False, 0, -k) for k, term in enumerate(txt_terms, 1)]

time: 22.8 us -> 21.5 us (0.943)
  waiting for transfers between devices: 2.87 us -> 1.22 us
  starting transfers between devices: 12.8 us -> 13.1 us
    ppermute x8, waiting for transfers between devices: 2.87 us -> 1.22 us  [send(): return lax.ppermute(piece, ('blk', 'group'), route(image_side, distance, k))]
    ppermute x8, starting transfers between devices: 11.1 us -> 11.4 us  [send(): return lax.ppermute(piece, ('blk', 'group'), route(image_side, distance, k))]
  transfers between devices with their start and end apart: 9 -> 9, of which waited for: 2 -> 3; matrix products, arithmetic and copies ran while one was open for 0% -> 0% of each run, Pallas kernels for 18% -> 19%
where the time goes in v5:
time: 21.5 us; the launch traced here: 21.3 us
  starting transfers between devices  13.1 us (61%)
  Pallas kernels  4.91 us (23%)
  between operations  2.01 us (9%)
  waiting for transfers between devices  1.22 us (6%)
    ppermute x8, starting transfers between devices, send(): return lax.ppermute(piece, ('blk', 'group'), route(image_side, distance, k))  11.4 us
    pallas_call x1, Pallas kernels, body(): kernel(feat_kernel, 2 * rows * width * emb, 4 * width * (rows + emb), out...  1.96 us
    ppermute x1, starting transfers between devices, body(): lax.ppermute(early, 'blk', [(i, i ^ 1 if n_blk % 2 == 0 else i) for i in...  1.72 us
    pallas_call x2, Pallas kernels, meetings(): kernel(functools.partial(meet_kernel, left_is_text, n_left, sum((p.shape[...  1.36 us
    ppermute x8, waiting for transfers between devices, send(): return lax.ppermute(piece, ('blk', 'group'), route(image_side, distance, k))  1.22 us
    pallas_call x1, Pallas kernels, body(): kernel(text_out_kernel, 8 * rows * emb, 12 * rows * emb, out_shape=shape(...  0.91 us
    pallas_call x1, Pallas kernels, body(): kernel(project_kernel, 2 * rows * width * emb, 2 * width * (rows + emb),...  0.67 us
  transfers between devices with their start and end apart: 9, of which 3 were waited for; matrix products, arithmetic and copies ran while one was open for 0% of the time, Pallas kernels for 19%

profile of v5, /device:TPU:0, one launch (start us, length us, event | category | flops | bytes accessed | tf_op | source)
XLA Modules:
  0.0 21.3 jit_solution(14363581436788692582)
XLA Ops:
  0.6 0.0 copy-start.2
  0.6 0.0 copy-start
  0.6 0.0 copy-start.1
  0.7 2.4 %collective-permute-start.1 = (bf16[128,512]{1,0:T(8,128)(2,1)}, bf16[128,512]{1,0:T(8,128)(2,1)S(1)}, u32[]{:S(2)}, u32[]{:S(2)}) collective-permute-start(bf16[128,512]{1,0:T(8,128)(2,1)} %text_ref.1), channel_id=1, source_target_pairs={{0,5},{1,4},{2,7},{3,6},{4,10},{5,11},{6,8},{7,9},{8,13},{9,12},{1... | collective-permute-start | bytes 393224 | tf_op jit(solution)/shard_map/ppermute | solution.py:134
  3.1 1.7 %collective-permute-start.2 = (f32[8,128]{1,0:T(8,128)S(1)}, f32[8,128]{1,0:T(8,128)S(1)}, u32[]{:S(2)}, u32[]{:S(2)}) collective-permute-start(f32[8,128]{1,0:T(8,128)S(1)} %shard_map.69), channel_id=1, source_target_pairs={{0,4},{4,0},{8,12},{12,8},{16,20},{20,16},{24,28},{28,24},{1,5},{5... | collective-permute-start | bytes 12296 | tf_op jit(solution)/shard_map/ppermute | solution.py:151
  4.8 0.0 copy-done.2
  4.8 0.5 %collective-permute-start.4 = (bf16[128,512]{1,0:T(8,128)(2,1)S(1)}, bf16[128,512]{1,0:T(8,128)(2,1)S(1)}, u32[]{:S(2)}, u32[]{:S(2)}) collective-permute-start(bf16[128,512]{1,0:T(8,128)(2,1)S(1)} %copy-done.2), channel_id=1, source_target_pairs={{0,2},{1,3},{2,0},{3,1},{4,5},{5,4},{6,7},{7,6},{8,10},{9,11},{10,... | collective-permute-start | bytes 393224 | tf_op jit(solution)/shard_map/ppermute | solution.py:134
  5.3 0.8 %collective-permute-start = (bf16[128,512]{1,0:T(8,128)(2,1)S(1)}, bf16[128,512]{1,0:T(8,128)(2,1)S(1)}, u32[]{:S(2)}, u32[]{:S(2)}) collective-permute-start(bf16[128,512]{1,0:T(8,128)(2,1)S(1)} %copy-done.2), channel_id=1, source_target_pairs={{0,4},{1,5},{2,6},{3,7},{4,8},{5,9},{6,10},{7,11},{8,12},{9,13},{1... | collective-permute-start | bytes 393224 | tf_op jit(solution)/shard_map/ppermute | solution.py:134
  6.1 0.0 collective-permute-done.2.after_ref
  6.1 0.0 copy-done
  6.1 0.0 copy-done.1
  6.1 0.7 %shard_map.70 = (f32[128,512]{1,0:T(8,128)S(1)}, f32[128,1]{1,0:T(8,128)S(1)}, bf16[128,512]{1,0:T(8,128)(2,1)S(1)}) custom-call(f32[8,128]{1,0:T(8,128)S(1)} %collective-permute-done.2.after_ref, bf16[128,3072]{1,0:T(8,128)(2,1)S(1)} %copy-done.1, bf16[3072,512]{1,0:T(8,128)(2,1)S(1)} %copy-done), custom_call_target="tpu_custom_call" | custom-call | flops 402653184 | bytes 3932160 | tf_op jit(solution)/shard_map/pallas_call | solution.py:155
  6.8 1.1 %collective-permute-start.3 = (bf16[128,512]{1,0:T(8,128)(2,1)S(1)}, bf16[128,512]{1,0:T(8,128)(2,1)S(1)}, u32[]{:S(2)}, u32[]{:S(2)}) collective-permute-start(bf16[128,512]{1,0:T(8,128)(2,1)S(1)} %get-tuple-element.11.refs_0_.refs_2_), channel_id=1, source_target_pairs={{0,1},{1,0},{2,3},{3,2},{4,6},{5,7},{6,4},{7,5},{8,9},{9,8},{10,11... | collective-permute-start | bytes 393224 | tf_op jit(solution)/shard_map/ppermute | solution.py:134
  7.9 2.9 %collective-permute-start.7 = (bf16[128,512]{1,0:T(8,128)(2,1)S(1)}, bf16[128,512]{1,0:T(8,128)(2,1)S(1)}, u32[]{:S(2)}, u32[]{:S(2)}) collective-permute-start(bf16[128,512]{1,0:T(8,128)(2,1)S(1)} %get-tuple-element.11.refs_0_.refs_2_), channel_id=1, source_target_pairs={{0,30},{1,31},{2,28},{3,29},{4,1},{5,0},{6,3},{7,2},{8,6},{9,7},{1... | collective-permute-start | bytes 393224 | tf_op jit(solution)/shard_map/ppermute | solution.py:134
  10.8 0.0 collective-permute-done.1.refs_1_.refs_5_
  10.8 0.1 collective-permute-start.6
  12.2 0.0 collective-permute-done.refs_0_.refs_4_
  12.2 0.0 collective-permute-done.4.refs_3_.refs_1_
  12.2 0.1 collective-permute-done.3.refs_1_.refs_3_
  12.3 0.7 %shard_map.71 = (f32[128,512]{1,0:T(8,128)S(1)}, bf16[128,512]{1,0:T(8,128)(2,1)S(1)}) custom-call(f32[8,128]{1,0:T(8,128)S(1)} %shard_map.68.scalar_ref.after_ref, f32[8,128]{1,0:T(8,128)S(1)} %shard_map.68.scalar_ref.after_ref, bf16[128,512]{1,0:T(8,128)(2,1)S(1)} %get-tuple-element.11.refs_0_.refs_2_, ...), custom_call_target="tpu_custom_call" | custom-call | flops 268435456 | bytes 1048576 | tf_op jit(solution)/shard_map/pallas_call | solution.py:169
  13.0 1.7 %collective-permute-start.5 = (bf16[128,512]{1,0:T(8,128)(2,1)S(1)}, bf16[128,512]{1,0:T(8,128)(2,1)S(1)}, u32[]{:S(2)}, u32[]{:S(2)}) collective-permute-start(bf16[128,512]{1,0:T(8,128)(2,1)S(1)} %get-tuple-element.15), channel_id=1, source_target_pairs={{0,1},{1,0},{2,3},{3,2},{4,6},{5,7},{6,4},{7,5},{8,9},{9,8},{10,11... | collective-permute-start | bytes 393224 | tf_op jit(solution)/shard_map/ppermute | solution.py:134
  14.7 0.0 collective-permute-done.7.refs_5_
  14.7 0.0 collective-permute-done.6.refs_4_
  14.7 0.7 %shard_map.73 = (f32[128,512]{1,0:T(8,128)S(1)}, bf16[128,512]{1,0:T(8,128)(2,1)S(1)}) custom-call(f32[8,128]{1,0:T(8,128)S(1)} %shard_map.68.scalar_ref.after_ref, f32[128,512]{1,0:T(8,128)S(1)} %get-tuple-element.12.grad_ref.after_ref, bf16[128,512]{1,0:T(8,128)(2,1)S(1)} %copy-done.2, bf16[128,512]{1,0:T(8,128)(2,1)S(1)} %collective-permute-done.4.refs_3_.refs_1_, ...), custom_call_target="tpu_custom_call" | custom-call | flops 268435456 | bytes 1048576 | tf_op jit(solution)/shard_map/pallas_call | solution.py:169
  15.4 2.0 %collective-permute-start.8 = (bf16[128,512]{1,0:T(8,128)(2,1)S(1)}, bf16[128,512]{1,0:T(8,128)(2,1)S(1)}, u32[]{:S(2)}, u32[]{:S(2)}) collective-permute-start(bf16[128,512]{1,0:T(8,128)(2,1)S(1)} %get-tuple-element.19), channel_id=1, source_target_pairs={{0,2},{1,3},{2,0},{3,1},{4,5},{5,4},{6,7},{7,6},{8,10},{9,11},{10,... | collective-permute-start | bytes 393224 | tf_op jit(solution)/shard_map/ppermute | solution.py:134
  17.3 0.7 %collective-permute-done.5.refs_0_ = bf16[128,512]{1,0:T(8,128)(2,1)S(1)} collective-permute-done((bf16[128,512]{1,0:T(8,128)(2,1)S(1)}, bf16[128,512]{1,0:T(8,128)(2,1)S(1)}, u32[]{:S(2)}, u32[]{:S(2)}) %collective-permute-start.5) | collective-permute-done | bytes 131104 | tf_op jit(solution)/shard_map/ppermute | solution.py:134
  18.0 2.0 %shard_map.72 = (f32[128,3072]{1,0:T(8,128)}, f32[8,128]{1,0:T(8,128)S(1)}) custom-call(f32[128,512]{1,0:T(8,128)S(1)} %get-tuple-element.12.grad_ref.after_ref, f32[128,512]{1,0:T(8,128)S(1)} %get-tuple-element.13.unit_ref, f32[128,1]{1,0:T(8,128)S(1)} %get-tuple-element.14.inv_ref, bf16[3072,512]{1,0:T(8,128)(2,1)S(1)} %copy-done, ...), custom_call_target="tpu_custom_call" | custom-call | flops 402653184 | bytes 7864320 | tf_op jit(solution)/shard_map/pallas_call | solution.py:192
  20.0 0.4 %collective-permute-done.8.refs_0_ = bf16[128,512]{1,0:T(8,128)(2,1)S(1)} collective-permute-done((bf16[128,512]{1,0:T(8,128)(2,1)S(1)}, bf16[128,512]{1,0:T(8,128)(2,1)S(1)}, u32[]{:S(2)}, u32[]{:S(2)}) %collective-permute-start.8) | collective-permute-done | bytes 131104 | tf_op jit(solution)/shard_map/ppermute | solution.py:134
  20.4 0.9 %shard_map.74 = f32[128,512]{1,0:T(8,128)} custom-call(f32[8,128]{1,0:T(8,128)S(1)} %get-tuple-element.17.after_ref, f32[128,512]{1,0:T(8,128)S(1)} %get-tuple-element.18.grad_ref, bf16[128,512]{1,0:T(8,128)(2,1)S(1)} %copy-done.2, bf16[128,512]{1,0:T(8,128)(2,1)S(1)} %collective-permute-done.8.refs_0_), custom_call_target="tpu_custom_call" | custom-call | flops 524288 | bytes 786432 | tf_op jit(solution)/shard_map/pallas_call | solution.py:202
  (2 shorter events, 0.0 us)
Async XLA Ops:
  0.6 4.2 %copy-start.2 = (bf16[128,512]{1,0:T(8,128)(2,1)S(1)}, bf16[128,512]{1,0:T(8,128)(2,1)}, u32[]{:S(2)}) copy-start(bf16[128,512]{1,0:T(8,128)(2,1)} %text_ref.1) | copy-start | bytes 393220
  0.6 5.5 %copy-start = (bf16[3072,512]{1,0:T(8,128)(2,1)S(1)}, bf16[3072,512]{1,0:T(8,128)(2,1)}, u32[]{:S(2)}) copy-start(bf16[3072,512]{1,0:T(8,128)(2,1)} %head_ref.3) | copy-start | bytes 9437188
  0.6 5.4 %copy-start.1 = (bf16[128,3072]{1,0:T(8,128)(2,1)S(1)}, bf16[128,3072]{1,0:T(8,128)(2,1)}, u32[]{:S(2)}) copy-start(bf16[128,3072]{1,0:T(8,128)(2,1)} %img_ref.1) | copy-start | bytes 2359300
  0.7 10.1 %collective-permute-start.1 = (bf16[128,512]{1,0:T(8,128)(2,1)}, bf16[128,512]{1,0:T(8,128)(2,1)S(1)}, u32[]{:S(2)}, u32[]{:S(2)}) collective-permute-start(bf16[128,512]{1,0:T(8,128)(2,1)} %text_ref.1), channel_id=1, source_target_pairs={{0,5},{1,4},{2,7},{3,6},{4,10},{5,11},{6,8},{7,9},{8,13},{9,12},{1... | collective-permute-start | bytes 393224 | tf_op jit(solution)/shard_map/ppermute | solution.py:134
  3.1 3.0 %collective-permute-start.2 = (f32[8,128]{1,0:T(8,128)S(1)}, f32[8,128]{1,0:T(8,128)S(1)}, u32[]{:S(2)}, u32[]{:S(2)}) collective-permute-start(f32[8,128]{1,0:T(8,128)S(1)} %shard_map.69), channel_id=1, source_target_pairs={{0,4},{4,0},{8,12},{12,8},{16,20},{20,16},{24,28},{28,24},{1,5},{5... | collective-permute-start | bytes 12296 | tf_op jit(solution)/shard_map/ppermute | solution.py:151
  4.8 7.4 %collective-permute-start.4 = (bf16[128,512]{1,0:T(8,128)(2,1)S(1)}, bf16[128,512]{1,0:T(8,128)(2,1)S(1)}, u32[]{:S(2)}, u32[]{:S(2)}) collective-permute-start(bf16[128,512]{1,0:T(8,128)(2,1)S(1)} %copy-done.2), channel_id=1, source_target_pairs={{0,2},{1,3},{2,0},{3,1},{4,5},{5,4},{6,7},{7,6},{8,10},{9,11},{10,... | collective-permute-start | bytes 393224 | tf_op jit(solution)/shard_map/ppermute | solution.py:134
  5.3 6.8 %collective-permute-start = (bf16[128,512]{1,0:T(8,128)(2,1)S(1)}, bf16[128,512]{1,0:T(8,128)(2,1)S(1)}, u32[]{:S(2)}, u32[]{:S(2)}) collective-permute-start(bf16[128,512]{1,0:T(8,128)(2,1)S(1)} %copy-done.2), channel_id=1, source_target_pairs={{0,4},{1,5},{2,6},{3,7},{4,8},{5,9},{6,10},{7,11},{8,12},{9,13},{1... | collective-permute-start | bytes 393224 | tf_op jit(solution)/shard_map/ppermute | solution.py:134
  6.8 5.5 %collective-permute-start.3 = (bf16[128,512]{1,0:T(8,128)(2,1)S(1)}, bf16[128,512]{1,0:T(8,128)(2,1)S(1)}, u32[]{:S(2)}, u32[]{:S(2)}) collective-permute-start(bf16[128,512]{1,0:T(8,128)(2,1)S(1)} %get-tuple-element.11.refs_0_.refs_2_), channel_id=1, source_target_pairs={{0,1},{1,0},{2,3},{3,2},{4,6},{5,7},{6,4},{7,5},{8,9},{9,8},{10,11... | collective-permute-start | bytes 393224 | tf_op jit(solution)/shard_map/ppermute | solution.py:134
  7.9 6.8 %collective-permute-start.7 = (bf16[128,512]{1,0:T(8,128)(2,1)S(1)}, bf16[128,512]{1,0:T(8,128)(2,1)S(1)}, u32[]{:S(2)}, u32[]{:S(2)}) collective-permute-start(bf16[128,512]{1,0:T(8,128)(2,1)S(1)} %get-tuple-element.11.refs_0_.refs_2_), channel_id=1, source_target_pairs={{0,30},{1,31},{2,28},{3,29},{4,1},{5,0},{6,3},{7,2},{8,6},{9,7},{1... | collective-permute-start | bytes 393224 | tf_op jit(solution)/shard_map/ppermute | solution.py:134
  10.8 3.9 %collective-permute-start.6 = (bf16[128,512]{1,0:T(8,128)(2,1)S(1)}, bf16[128,512]{1,0:T(8,128)(2,1)S(1)}, u32[]{:S(2)}, u32[]{:S(2)}) collective-permute-start(bf16[128,512]{1,0:T(8,128)(2,1)S(1)} %get-tuple-element.11.refs_0_.refs_2_), channel_id=1, source_target_pairs={{0,28},{1,29},{2,30},{3,31},{4,0},{5,1},{6,2},{7,3},{8,4},{9,5},{1... | collective-permute-start | bytes 393224 | tf_op jit(solution)/shard_map/ppermute | solution.py:134
  13.0 5.0 %collective-permute-start.5 = (bf16[128,512]{1,0:T(8,128)(2,1)S(1)}, bf16[128,512]{1,0:T(8,128)(2,1)S(1)}, u32[]{:S(2)}, u32[]{:S(2)}) collective-permute-start(bf16[128,512]{1,0:T(8,128)(2,1)S(1)} %get-tuple-element.15), channel_id=1, source_target_pairs={{0,1},{1,0},{2,3},{3,2},{4,6},{5,7},{6,4},{7,5},{8,9},{9,8},{10,11... | collective-permute-start | bytes 393224 | tf_op jit(solution)/shard_map/ppermute | solution.py:134
  15.4 5.0 %collective-permute-start.8 = (bf16[128,512]{1,0:T(8,128)(2,1)S(1)}, bf16[128,512]{1,0:T(8,128)(2,1)S(1)}, u32[]{:S(2)}, u32[]{:S(2)}) collective-permute-start(bf16[128,512]{1,0:T(8,128)(2,1)S(1)} %get-tuple-element.19), channel_id=1, source_target_pairs={{0,2},{1,3},{2,0},{3,1},{4,5},{5,4},{6,7},{7,6},{8,10},{9,11},{10,... | collective-permute-start | bytes 393224 | tf_op jit(solution)/shard_map/ppermute | solution.py:134

commit v6 on v4

v6 whole, which is shorter than its diff:
```python
import functools
import math

import jax
import jax.numpy as jnp
from jax import lax
from jax.experimental import pallas as pl
from jax.experimental.pallas import tpu as pltpu
from jax.sharding import PartitionSpec as P

EPS = 1e-06
LOG2_E = math.log2(math.e)
F32 = jnp.float32
BF16 = jnp.bfloat16
CONTRACT_LAST = (((1,), (1,)), ((), ()))
VMEM = pl.BlockSpec(memory_space=pltpu.VMEM)
ANY = pl.BlockSpec(memory_space=pl.ANY)
HBM = pl.BlockSpec(memory_space=pltpu.HBM)


def to_unit(values):
    inverse = lax.rsqrt(jnp.sum(values * values, axis=-1, keepdims=True) + EPS)
    return values * inverse, inverse


def unit_back(grad_in, unit_rows, inverse):
    return (grad_in - unit_rows * jnp.sum(unit_rows * grad_in, axis=-1, keepdims=True)) * inverse


def project_kernel(after_ref, img_ref, head_ref, unit_ref, inv_ref, low_ref):
    projected = jnp.dot(img_ref[...], head_ref[...], preferred_element_type=F32)
    unit, inverse = to_unit(projected)
    unit_ref[...] = unit
    inv_ref[...] = inverse
    low_ref[...] = unit.astype(BF16)


def text_low(ref):
    return to_unit(ref[...].astype(F32))[0].astype(BF16)


def low_kernel(text_ref, after_ref, low_ref):
    low_ref[...] = text_low(text_ref)


def meet(scalar_ref, left, right, weight_ref, grad_ref, term_refs):
    rows = grad_ref.shape[0]
    scale, bias = scalar_ref[0:1, 0:1], scalar_ref[1:2, 0:1]
    similarity = lax.dot_general(left, right, CONTRACT_LAST, preferred_element_type=F32)
    power = jnp.exp2(similarity * (scale * -LOG2_E) + bias * -LOG2_E)
    sigmoid = 1.0 / (1.0 + power)
    weight_ref[...] = sigmoid.astype(BF16)
    row_ids = lax.broadcasted_iota(jnp.int32, (rows, rows), 0)
    col_ids = lax.broadcasted_iota(jnp.int32, (rows, rows), 1)
    own = sigmoid[:rows, :rows]
    weight_ref[:rows, :rows] = jnp.where(row_ids == col_ids, own - 1.0, own).astype(BF16)
    grad = scale * jnp.dot(weight_ref[...], right, preferred_element_type=F32)
    grad_ref[...] = grad[:rows]
    for k, ref in enumerate(term_refs, 1):
        ref[...] = grad[k * rows : (k + 1) * rows].astype(BF16)


def image_kernel(n_col, n_row, scalar_ref, *refs):
    refs = refs[n_row:]
    image_refs, refs = refs[:n_col], refs[n_col:]
    raw_refs, refs = refs[:n_row], refs[n_row:]
    earlier_refs, refs = refs[:n_row], refs[n_row:]
    (grad_ref, *term_refs), weight_ref = refs[:-1], refs[-1]
    images = jnp.concatenate([ref[...] for ref in image_refs], axis=0)
    texts = jnp.concatenate([text_low(ref) for ref in raw_refs] + [ref[...] for ref in earlier_refs], axis=0)
    meet(scalar_ref, images, texts, weight_ref, grad_ref, term_refs)


def text_kernel(n_row, n_image, scalar_ref, after_ref, *refs):
    text_refs, refs = refs[:n_row], refs[n_row:]
    image_refs, refs = refs[:n_image], refs[n_image:]
    (grad_ref, *term_refs), weight_ref = refs[:-1], refs[-1]
    texts = jnp.concatenate([text_low(ref) for ref in text_refs], axis=0)
    images = jnp.concatenate([ref[...] for ref in image_refs], axis=0)
    meet(scalar_ref, texts, images, weight_ref, grad_ref, term_refs)


def feat_kernel(grad_ref, unit_ref, inv_ref, head_ref, text_ref, *refs):
    peer_refs, (out_ref, text_unit_ref, text_inv_ref, out_here, sems) = refs[:-5], refs[-5:]
    parts = sems.shape[0]
    width = head_ref.shape[0] // parts
    grad = grad_ref[...]
    for ref in peer_refs:
        grad += ref[...].astype(F32)
    low = unit_back(grad, unit_ref[...], inv_ref[...]).astype(BF16)
    copies = []
    for i in range(parts):
        span = pl.ds(i * width, width)
        out_here[:, span] = lax.dot_general(low, head_ref[span], CONTRACT_LAST, preferred_element_type=F32)
        copy = pltpu.make_async_copy(out_here.at[:, span], out_ref.at[:, span], sems.at[i])
        copy.start()
        copies.append(copy)
    text_unit_ref[...], text_inv_ref[...] = to_unit(text_ref[...].astype(F32))
    for copy in copies:
        copy.wait()


def mark_kernel(out_ref):
    out_ref[...] = jnp.zeros_like(out_ref)


def text_out_kernel(grad_ref, unit_ref, inv_ref, *refs):
    peer_refs, out_ref = refs[:-1], refs[-1]
    grad = grad_ref[...]
    for ref in peer_refs:
        grad += ref[...].astype(F32)
    out_ref[...] = unit_back(grad, unit_ref[...], inv_ref[...])


def body(img_feat, head_weight, text_emb, natural_exponent_factor, bias):
    rows, width = img_feat.shape
    emb = text_emb.shape[1]
    n_blk, n_group = lax.axis_size("blk"), lax.axis_size("group")
    n_col = next(k for k in range(math.isqrt(n_group), 0, -1) if n_group % k == 0)
    n_row = n_group // n_col
    shape = jax.ShapeDtypeStruct
    parts = 8 if width % 1024 == 0 else 1

    def kernel(body, flops, moved, **options):
        return pl.pallas_call(
            body,
            cost_estimate=pl.CostEstimate(flops=flops, bytes_accessed=moved, transcendentals=0),
            compiler_params=pltpu.CompilerParams(vmem_limit_bytes=16 * 2**20),
            **options,
        )

    side = n_col if n_row == n_col else 0

    def route(image_side, distance, k):
        pairs = []
        for i in range(n_blk):
            j = (i + distance) % n_blk
            along_row = image_side if side == 0 or j % 2 == 1 else not image_side
            for g in range(n_group):
                r, c = g // n_col, g % n_col
                r, c = (r, (c + k) % n_col) if along_row else ((r + k) % n_row, c)
                pairs.append((i * n_group + g, j * n_group + r * n_col + c))
        return pairs

    def send(piece, image_side, distance, k):
        return lax.ppermute(piece, ("blk", "group"), route(image_side, distance, k))

    first = lax.broadcasted_iota(jnp.int32, (8, 128), 0) == 0
    scalars = jnp.where(first, jnp.exp(natural_exponent_factor[0]), bias[0])

    unit_shapes = (shape((rows, emb), F32), shape((rows, 1), F32), shape((rows, emb), BF16))
    early = kernel(
        mark_kernel, 40 * rows * width * emb, 20 * width * (rows + emb), out_shape=shape((8, 128), F32), out_specs=VMEM
    )()
    earlier_texts = [send(text_emb, False, 1, k) for k in range(n_row)]
    texts = [text_emb] + [send(text_emb, False, 0, k) for k in range(1, n_row)]

    img_unit, img_inv, img_low = kernel(
        project_kernel,
        2 * rows * width * emb,
        2 * width * (rows + emb),
        out_shape=unit_shapes,
        in_specs=[ANY] + [VMEM] * 2,
        out_specs=(VMEM,) * 3,
    )(early, img_feat, head_weight)

    images = [img_low] + [send(img_low, True, 0, k) for k in range(1, n_col)]
    later_images = [send(img_low, True, -1, k) for k in range(n_col)]

    low_piece, grad_piece = shape((rows, emb), BF16), shape((rows, emb), F32)
    earlier_lows, after = [], scalars
    for piece in earlier_texts:
        after = kernel(
            low_kernel,
            8 * rows * emb,
            4 * rows * emb,
            out_shape=low_piece,
            in_specs=[VMEM, ANY],
            out_specs=VMEM,
        )(piece, after)
        earlier_lows.append(after)

    grad_img, *img_terms = kernel(
        functools.partial(image_kernel, n_col, n_row),
        8 * n_col * n_row * rows * rows * emb,
        2 * rows * emb * (2 * n_col + 3 * n_row),
        out_shape=(grad_piece,) + (low_piece,) * (n_col - 1),
        in_specs=[VMEM] + [ANY] * n_row + [VMEM] * (n_col + 2 * n_row),
        out_specs=(VMEM,) * n_col,
        scratch_shapes=[pltpu.VMEM((n_col * rows, 2 * n_row * rows), BF16)],
    )(scalars, *earlier_texts, *images, *texts, *earlier_lows)
    img_peers = [send(term, True, 0, -k) for k, term in enumerate(img_terms, 1)]

    grad_txt, *txt_terms = kernel(
        functools.partial(text_kernel, n_row, 2 * n_col),
        8 * n_col * n_row * rows * rows * emb,
        2 * rows * emb * (2 * n_col + 3 * n_row),
        out_shape=(grad_piece,) + (low_piece,) * (n_row - 1),
        in_specs=[VMEM, ANY] + [VMEM] * (n_row + 2 * n_col),
        out_specs=(VMEM,) * n_row,
        scratch_shapes=[pltpu.VMEM((n_row * rows, 2 * n_col * rows), BF16)],
    )(scalars, grad_img, *texts, *images, *later_images)
    txt_peers = [send(term, False, 0, -k) for k, term in enumerate(txt_terms, 1)]

    d_feat, txt_unit, txt_inv = kernel(
        feat_kernel,
        2 * rows * width * emb,
        4 * width * (rows + emb),
        out_shape=(shape((rows, width), F32), grad_piece, shape((rows, 1), F32)),
        in_specs=[VMEM] * (5 + len(img_peers)),
        out_specs=(HBM, VMEM, VMEM),
        scratch_shapes=[pltpu.VMEM((rows, width), F32), pltpu.SemaphoreType.DMA((parts,))],
    )(grad_img, img_unit, img_inv, head_weight, text_emb, *img_peers)

    d_text = kernel(
        text_out_kernel,
        8 * rows * emb,
        12 * rows * emb,
        out_shape=shape((rows, emb), F32),
        in_specs=[VMEM] * (3 + len(txt_peers)),
        out_specs=VMEM,
    )(grad_txt, txt_unit, txt_inv, *txt_peers)
    return d_feat, d_text


def solution(mesh):
    return jax.shard_map(
        body,
        mesh=mesh,
        in_specs=(P(("blk", "group"), None), P(), P(("blk", "group"), None), P(), P()),
        out_specs=(P(("blk", "group"), None), P(("blk", "group"), None)),
        check_vma=False,
    )
```

time: 22.8 us -> 21.3 us (0.934)
  waiting for transfers between devices: 2.87 us -> 2.04 us
  starting transfers between devices: 12.8 us -> 12 us
    ppermute x1 -> x0, starting transfers between devices: 1.72 us -> none  [body(): lax.ppermute(early, 'blk', [(i, i ^ 1 if n_blk % 2 == 0 else i) for i in...]
    ppermute x8, starting transfers between devices: 11.1 us -> 12 us  [send(): return lax.ppermute(piece, ('blk', 'group'), route(image_side, distance, k))]
    ppermute x8, waiting for transfers between devices: 2.87 us -> 2.04 us  [send(): return lax.ppermute(piece, ('blk', 'group'), route(image_side, distance, k))]
    pallas_call x3 -> x4, Pallas kernels: 1.36 us -> 1.54 us  [the longest x1 0.67 us: body(): kernel(functools.partial(text_kernel, n_row, 2 * n_col), 8 * n_col * n_ro...]
  transfers between devices with their start and end apart: 9 -> 8, of which waited for: 2 -> 3; matrix products, arithmetic and copies ran while one was open for 0% -> 0% of each run, Pallas kernels for 18% -> 20%
where the time goes in v6:
time: 21.3 us; the launch traced here: 21.2 us
  starting transfers between devices  12 us (56%)
  Pallas kernels  5.01 us (24%)
  between operations  2.06 us (10%)
  waiting for transfers between devices  2.04 us (10%)
    ppermute x8, starting transfers between devices, send(): return lax.ppermute(piece, ('blk', 'group'), route(image_side, distance, k))  12 us
    ppermute x8, waiting for transfers between devices, send(): return lax.ppermute(piece, ('blk', 'group'), route(image_side, distance, k))  2.04 us
    pallas_call x1, Pallas kernels, body(): kernel(feat_kernel, 2 * rows * width * emb, 4 * width * (rows + emb), out...  1.94 us
    pallas_call x1, Pallas kernels, body(): kernel(text_out_kernel, 8 * rows * emb, 12 * rows * emb, out_shape=shape(...  0.85 us
    pallas_call x1, Pallas kernels, body(): kernel(project_kernel, 2 * rows * width * emb, 2 * width * (rows + emb),...  0.67 us
    pallas_call x1, Pallas kernels, body(): kernel(functools.partial(text_kernel, n_row, 2 * n_col), 8 * n_col * n_ro...  0.67 us
    pallas_call x1, Pallas kernels, body(): kernel(functools.partial(image_kernel, n_col, n_row), 8 * n_col * n_row *...  0.65 us
  transfers between devices with their start and end apart: 8, of which 3 were waited for; matrix products, arithmetic and copies ran while one was open for 0% of the time, Pallas kernels for 20%

profile of v6, /device:TPU:0, one launch (start us, length us, event | category | flops | bytes accessed | tf_op | source)
XLA Modules:
  0.0 21.2 jit_solution(14249049539748830253)
XLA Ops:
  0.6 0.0 copy-start
  0.6 0.0 copy-start.2
  0.6 3.0 %collective-permute-start.3 = (bf16[128,512]{1,0:T(8,128)(2,1)}, bf16[128,512]{1,0:T(8,128)(2,1)S(1)}, u32[]{:S(2)}, u32[]{:S(2)}) collective-permute-start(bf16[128,512]{1,0:T(8,128)(2,1)} %refs_0_.1), channel_id=1, source_target_pairs={{0,1},{1,0},{2,3},{3,2},{4,6},{5,7},{6,4},{7,5},{8,9},{9,8},{10,11... | collective-permute-start | bytes 393224 | tf_op jit(solution)/shard_map/ppermute | solution.py:146
  3.7 0.0 collective-permute-start.1
  3.7 1.7 %collective-permute-start = (bf16[128,512]{1,0:T(8,128)(2,1)}, bf16[128,512]{1,0:T(8,128)(2,1)S(1)}, u32[]{:S(2)}, u32[]{:S(2)}) collective-permute-start(bf16[128,512]{1,0:T(8,128)(2,1)} %refs_0_.1), channel_id=1, source_target_pairs={{0,4},{1,5},{2,6},{3,7},{4,8},{5,9},{6,10},{7,11},{8,12},{9,13},{1... | collective-permute-start | bytes 393224 | tf_op jit(solution)/shard_map/ppermute | solution.py:146
  5.3 0.0 copy-done
  5.3 0.0 copy-done.2
  5.3 0.0 copy-start.1
  5.3 0.7 %shard_map.69 = (f32[128,512]{1,0:T(8,128)S(1)}, f32[128,1]{1,0:T(8,128)S(1)}, bf16[128,512]{1,0:T(8,128)(2,1)S(1)}) custom-call(f32[8,128]{1,0:T(8,128)S(1)} %shard_map.68.after_ref, bf16[128,3072]{1,0:T(8,128)(2,1)S(1)} %copy-done.2, bf16[3072,512]{1,0:T(8,128)(2,1)S(1)} %copy-done), custom_call_target="tpu_custom_call" | custom-call | flops 402653184 | bytes 3932160 | tf_op jit(solution)/shard_map/pallas_call | solution.py:158
  6.0 1.6 %collective-permute-start.2 = (bf16[128,512]{1,0:T(8,128)(2,1)S(1)}, bf16[128,512]{1,0:T(8,128)(2,1)S(1)}, u32[]{:S(2)}, u32[]{:S(2)}) collective-permute-start(bf16[128,512]{1,0:T(8,128)(2,1)S(1)} %get-tuple-element.12.refs_2_), channel_id=1, source_target_pairs={{0,2},{1,3},{2,0},{3,1},{4,5},{5,4},{6,7},{7,6},{8,10},{9,11},{10,... | collective-permute-start | bytes 393224 | tf_op jit(solution)/shard_map/ppermute | solution.py:146
  7.6 1.5 %collective-permute-start.6 = (bf16[128,512]{1,0:T(8,128)(2,1)S(1)}, bf16[128,512]{1,0:T(8,128)(2,1)S(1)}, u32[]{:S(2)}, u32[]{:S(2)}) collective-permute-start(bf16[128,512]{1,0:T(8,128)(2,1)S(1)} %get-tuple-element.12.refs_2_), channel_id=1, source_target_pairs={{0,29},{1,28},{2,31},{3,30},{4,2},{5,3},{6,0},{7,1},{8,5},{9,4},{1... | collective-permute-start | bytes 393224 | tf_op jit(solution)/shard_map/ppermute | solution.py:146
  10.5 0.5 %collective-permute-done.text_ref.refs_0_ = bf16[128,512]{1,0:T(8,128)(2,1)S(1)} collective-permute-done((bf16[128,512]{1,0:T(8,128)(2,1)}, bf16[128,512]{1,0:T(8,128)(2,1)S(1)}, u32[]{:S(2)}, u32[]{:S(2)}) %collective-permute-start) | collective-permute-done | bytes 131104 | tf_op jit(solution)/shard_map/ppermute | solution.py:146
  11.0 0.7 %collective-permute-start.5 = (bf16[128,512]{1,0:T(8,128)(2,1)S(1)}, bf16[128,512]{1,0:T(8,128)(2,1)S(1)}, u32[]{:S(2)}, u32[]{:S(2)}) collective-permute-start(bf16[128,512]{1,0:T(8,128)(2,1)S(1)} %get-tuple-element.12.refs_2_), channel_id=1, source_target_pairs={{0,28},{1,29},{2,30},{3,31},{4,0},{5,1},{6,2},{7,3},{8,4},{9,5},{1... | collective-permute-start | bytes 393224 | tf_op jit(solution)/shard_map/ppermute | solution.py:146
  11.7 0.1 iota.7.after_ref.scalar_ref
  11.7 0.1 shard_map.70.after_ref.refs_6_
  11.8 0.0 collective-permute-done.1.text_ref.refs_1_
  11.9 0.1 shard_map.71.refs_7_
  12.0 0.0 collective-permute-done.3.refs_5_.refs_1_
  12.0 0.0 collective-permute-done.2.refs_3_
  12.0 0.0 copy-done.1
  12.0 0.7 %shard_map.72 = (f32[128,512]{1,0:T(8,128)S(1)}, bf16[128,512]{1,0:T(8,128)(2,1)S(1)}) custom-call(f32[8,128]{1,0:T(8,128)S(1)} %iota.7.after_ref.scalar_ref, bf16[128,512]{1,0:T(8,128)(2,1)S(1)} %collective-permute-done.text_ref.refs_0_, bf16[128,512]{1,0:T(8,128)(2,1)S(1)} %collective-permute-done.1.text_ref.refs_1_, ...), custom_call_target="tpu_custom_call" | custom-call | flops 268435456 | bytes 1310720 | tf_op jit(solution)/shard_map/pallas_call | solution.py:183
  12.7 2.0 %collective-permute-start.4 = (bf16[128,512]{1,0:T(8,128)(2,1)S(1)}, bf16[128,512]{1,0:T(8,128)(2,1)S(1)}, u32[]{:S(2)}, u32[]{:S(2)}) collective-permute-start(bf16[128,512]{1,0:T(8,128)(2,1)S(1)} %get-tuple-element.16), channel_id=1, source_target_pairs={{0,2},{1,3},{2,0},{3,1},{4,5},{5,4},{6,7},{7,6},{8,10},{9,11},{10,... | collective-permute-start | bytes 393224 | tf_op jit(solution)/shard_map/ppermute | solution.py:146
  14.6 0.0 collective-permute-done.6.refs_5_
  14.6 0.0 collective-permute-done.5.refs_4_
  14.6 0.7 %shard_map.74 = (f32[128,512]{1,0:T(8,128)S(1)}, bf16[128,512]{1,0:T(8,128)(2,1)S(1)}) custom-call(f32[8,128]{1,0:T(8,128)S(1)} %iota.7.after_ref.scalar_ref, f32[128,512]{1,0:T(8,128)S(1)} %get-tuple-element.13.grad_ref.after_ref, bf16[128,512]{1,0:T(8,128)(2,1)S(1)} %copy-done.1, bf16[128,512]{1,0:T(8,128)(2,1)S(1)} %collective-permute-done.3.refs_5_.refs_1_, ...), custom_call_target="tpu_custom_call" | custom-call | flops 268435456 | bytes 1310720 | tf_op jit(solution)/shard_map/pallas_call | solution.py:194
  15.3 1.6 %collective-permute-start.7 = (bf16[128,512]{1,0:T(8,128)(2,1)S(1)}, bf16[128,512]{1,0:T(8,128)(2,1)S(1)}, u32[]{:S(2)}, u32[]{:S(2)}) collective-permute-start(bf16[128,512]{1,0:T(8,128)(2,1)S(1)} %get-tuple-element.21), channel_id=1, source_target_pairs={{0,1},{1,0},{2,3},{3,2},{4,6},{5,7},{6,4},{7,5},{8,9},{9,8},{10,11... | collective-permute-start | bytes 393224 | tf_op jit(solution)/shard_map/ppermute | solution.py:146
  16.9 0.8 %collective-permute-done.4.refs_0_ = bf16[128,512]{1,0:T(8,128)(2,1)S(1)} collective-permute-done((bf16[128,512]{1,0:T(8,128)(2,1)S(1)}, bf16[128,512]{1,0:T(8,128)(2,1)S(1)}, u32[]{:S(2)}, u32[]{:S(2)}) %collective-permute-start.4) | collective-permute-done | bytes 131104 | tf_op jit(solution)/shard_map/ppermute | solution.py:146
  17.7 1.9 %shard_map.73 = (f32[128,3072]{1,0:T(8,128)}, f32[128,512]{1,0:T(8,128)S(1)}, f32[128,1]{1,0:T(8,128)S(1)}) custom-call(f32[128,512]{1,0:T(8,128)S(1)} %get-tuple-element.13.grad_ref.after_ref, f32[128,512]{1,0:T(8,128)S(1)} %get-tuple-element.14.unit_ref, f32[128,1]{1,0:T(8,128)S(1)} %get-tuple-element.15.inv_ref, bf16[3072,512]{1,0:T(8,128)(2,1)S(1)} %copy-done, ...), custom_call_target="tpu_custom_call" | custom-call | flops 402653184 | bytes 7864320 | tf_op jit(solution)/shard_map/pallas_call | solution.py:205
  19.6 0.7 %collective-permute-done.7.refs_0_ = bf16[128,512]{1,0:T(8,128)(2,1)S(1)} collective-permute-done((bf16[128,512]{1,0:T(8,128)(2,1)S(1)}, bf16[128,512]{1,0:T(8,128)(2,1)S(1)}, u32[]{:S(2)}, u32[]{:S(2)}) %collective-permute-start.7) | collective-permute-done | bytes 131104 | tf_op jit(solution)/shard_map/ppermute | solution.py:146
  20.3 0.9 %shard_map.75 = f32[128,512]{1,0:T(8,128)} custom-call(f32[128,512]{1,0:T(8,128)S(1)} %get-tuple-element.18.grad_ref, f32[128,512]{1,0:T(8,128)S(1)} %get-tuple-element.19.unit_ref, f32[128,1]{1,0:T(8,128)S(1)} %get-tuple-element.20.inv_ref, bf16[128,512]{1,0:T(8,128)(2,1)S(1)} %collective-permute-done.7.refs_0_), custom_call_target="tpu_custom_call" | custom-call | flops 524288 | bytes 786432 | tf_op jit(solution)/shard_map/pallas_call | solution.py:215
  (2 shorter events, 0.0 us)
Async XLA Ops:
  0.6 4.7 %copy-start = (bf16[3072,512]{1,0:T(8,128)(2,1)S(1)}, bf16[3072,512]{1,0:T(8,128)(2,1)}, u32[]{:S(2)}) copy-start(bf16[3072,512]{1,0:T(8,128)(2,1)} %head_ref.3) | copy-start | bytes 9437188
  0.6 4.7 %copy-start.2 = (bf16[128,3072]{1,0:T(8,128)(2,1)S(1)}, bf16[128,3072]{1,0:T(8,128)(2,1)}, u32[]{:S(2)}) copy-start(bf16[128,3072]{1,0:T(8,128)(2,1)} %img_ref.1) | copy-start | bytes 2359300
  0.6 11.3 %collective-permute-start.3 = (bf16[128,512]{1,0:T(8,128)(2,1)}, bf16[128,512]{1,0:T(8,128)(2,1)S(1)}, u32[]{:S(2)}, u32[]{:S(2)}) collective-permute-start(bf16[128,512]{1,0:T(8,128)(2,1)} %refs_0_.1), channel_id=1, source_target_pairs={{0,1},{1,0},{2,3},{3,2},{4,6},{5,7},{6,4},{7,5},{8,9},{9,8},{10,11... | collective-permute-start | bytes 393224 | tf_op jit(solution)/shard_map/ppermute | solution.py:146
  3.7 8.2 %collective-permute-start.1 = (bf16[128,512]{1,0:T(8,128)(2,1)}, bf16[128,512]{1,0:T(8,128)(2,1)S(1)}, u32[]{:S(2)}, u32[]{:S(2)}) collective-permute-start(bf16[128,512]{1,0:T(8,128)(2,1)} %refs_0_.1), channel_id=1, source_target_pairs={{0,6},{1,7},{2,4},{3,5},{4,9},{5,8},{6,11},{7,10},{8,14},{9,15},{1... | collective-permute-start | bytes 393224 | tf_op jit(solution)/shard_map/ppermute | solution.py:146
  3.7 7.3 %collective-permute-start = (bf16[128,512]{1,0:T(8,128)(2,1)}, bf16[128,512]{1,0:T(8,128)(2,1)S(1)}, u32[]{:S(2)}, u32[]{:S(2)}) collective-permute-start(bf16[128,512]{1,0:T(8,128)(2,1)} %refs_0_.1), channel_id=1, source_target_pairs={{0,4},{1,5},{2,6},{3,7},{4,8},{5,9},{6,10},{7,11},{8,12},{9,13},{1... | collective-permute-start | bytes 393224 | tf_op jit(solution)/shard_map/ppermute | solution.py:146
  5.3 6.7 %copy-start.1 = (bf16[128,512]{1,0:T(8,128)(2,1)S(1)}, bf16[128,512]{1,0:T(8,128)(2,1)}, u32[]{:S(2)}) copy-start(bf16[128,512]{1,0:T(8,128)(2,1)} %refs_0_.1) | copy-start | bytes 393220
  6.0 6.0 %collective-permute-start.2 = (bf16[128,512]{1,0:T(8,128)(2,1)S(1)}, bf16[128,512]{1,0:T(8,128)(2,1)S(1)}, u32[]{:S(2)}, u32[]{:S(2)}) collective-permute-start(bf16[128,512]{1,0:T(8,128)(2,1)S(1)} %get-tuple-element.12.refs_2_), channel_id=1, source_target_pairs={{0,2},{1,3},{2,0},{3,1},{4,5},{5,4},{6,7},{7,6},{8,10},{9,11},{10,... | collective-permute-start | bytes 393224 | tf_op jit(solution)/shard_map/ppermute | solution.py:146
  7.6 7.0 %collective-permute-start.6 = (bf16[128,512]{1,0:T(8,128)(2,1)S(1)}, bf16[128,512]{1,0:T(8,128)(2,1)S(1)}, u32[]{:S(2)}, u32[]{:S(2)}) collective-permute-start(bf16[128,512]{1,0:T(8,128)(2,1)S(1)} %get-tuple-element.12.refs_2_), channel_id=1, source_target_pairs={{0,29},{1,28},{2,31},{3,30},{4,2},{5,3},{6,0},{7,1},{8,5},{9,4},{1... | collective-permute-start | bytes 393224 | tf_op jit(solution)/shard_map/ppermute | solution.py:146
  11.0 3.6 %collective-permute-start.5 = (bf16[128,512]{1,0:T(8,128)(2,1)S(1)}, bf16[128,512]{1,0:T(8,128)(2,1)S(1)}, u32[]{:S(2)}, u32[]{:S(2)}) collective-permute-start(bf16[128,512]{1,0:T(8,128)(2,1)S(1)} %get-tuple-element.12.refs_2_), channel_id=1, source_target_pairs={{0,28},{1,29},{2,30},{3,31},{4,0},{5,1},{6,2},{7,3},{8,4},{9,5},{1... | collective-permute-start | bytes 393224 | tf_op jit(solution)/shard_map/ppermute | solution.py:146
  12.7 5.0 %collective-permute-start.4 = (bf16[128,512]{1,0:T(8,128)(2,1)S(1)}, bf16[128,512]{1,0:T(8,128)(2,1)S(1)}, u32[]{:S(2)}, u32[]{:S(2)}) collective-permute-start(bf16[128,512]{1,0:T(8,128)(2,1)S(1)} %get-tuple-element.16), channel_id=1, source_target_pairs={{0,2},{1,3},{2,0},{3,1},{4,5},{5,4},{6,7},{7,6},{8,10},{9,11},{10,... | collective-permute-start | bytes 393224 | tf_op jit(solution)/shard_map/ppermute | solution.py:146
  15.3 5.0 %collective-permute-start.7 = (bf16[128,512]{1,0:T(8,128)(2,1)S(1)}, bf16[128,512]{1,0:T(8,128)(2,1)S(1)}, u32[]{:S(2)}, u32[]{:S(2)}) collective-permute-start(bf16[128,512]{1,0:T(8,128)(2,1)S(1)} %get-tuple-element.21), channel_id=1, source_target_pairs={{0,1},{1,0},{2,3},{3,2},{4,6},{5,7},{6,4},{7,5},{8,9},{9,8},{10,11... | collective-permute-start | bytes 393224 | tf_op jit(solution)/shard_map/ppermute | solution.py:146

commit v7 on v6

--- a/solution.py
+++ b/solution.py
@@ -119,7 +119,7 @@
     n_col = next(k for k in range(math.isqrt(n_group), 0, -1) if n_group % k == 0)
     n_row = n_group // n_col
     shape = jax.ShapeDtypeStruct
-    parts = 8 if width % 1024 == 0 else 1
+    parts = 12 if width % 1536 == 0 else 1
 
     def kernel(body, flops, moved, **options):
         return pl.pallas_call(

time: 21.3 us -> 21.3 us (level)
  no operation moved by 1% of the time
where the time goes in v7:
time: 21.3 us; the launch traced here: 21.2 us
  starting transfers between devices  12 us (56%)
  Pallas kernels  5.07 us (24%)
  between operations  2.06 us (10%)
  waiting for transfers between devices  1.98 us (9%)
    ppermute x8, starting transfers between devices, send(): return lax.ppermute(piece, ('blk', 'group'), route(image_side, distance, k))  12 us
    pallas_call x1, Pallas kernels, body(): kernel(feat_kernel, 2 * rows * width * emb, 4 * width * (rows + emb), out...  2 us
    ppermute x8, waiting for transfers between devices, send(): return lax.ppermute(piece, ('blk', 'group'), route(image_side, distance, k))  1.98 us
    pallas_call x1, Pallas kernels, body(): kernel(text_out_kernel, 8 * rows * emb, 12 * rows * emb, out_shape=shape(...  0.85 us
    pallas_call x1, Pallas kernels, body(): kernel(project_kernel, 2 * rows * width * emb, 2 * width * (rows + emb),...  0.67 us
    pallas_call x1, Pallas kernels, body(): kernel(functools.partial(text_kernel, n_row, 2 * n_col), 8 * n_col * n_ro...  0.67 us
    pallas_call x1, Pallas kernels, body(): kernel(functools.partial(image_kernel, n_col, n_row), 8 * n_col * n_row *...  0.65 us
  transfers between devices with their start and end apart: 8, of which 3 were waited for; matrix products, arithmetic and copies ran while one was open for 0% of the time, Pallas kernels for 20%

profile of v7, /device:TPU:0, one launch (start us, length us, event | category | flops | bytes accessed | tf_op | source)
XLA Modules:
  0.0 21.2 jit_solution(2253672067442044970)
XLA Ops:
  0.6 0.0 copy-start
  0.6 0.0 copy-start.2
  0.6 3.0 %collective-permute-start.3 = (bf16[128,512]{1,0:T(8,128)(2,1)}, bf16[128,512]{1,0:T(8,128)(2,1)S(1)}, u32[]{:S(2)}, u32[]{:S(2)}) collective-permute-start(bf16[128,512]{1,0:T(8,128)(2,1)} %refs_0_.1), channel_id=1, source_target_pairs={{0,1},{1,0},{2,3},{3,2},{4,6},{5,7},{6,4},{7,5},{8,9},{9,8},{10,11... | collective-permute-start | bytes 393224 | tf_op jit(solution)/shard_map/ppermute | solution.py:146
  3.7 0.0 collective-permute-start.1
  3.7 1.7 %collective-permute-start = (bf16[128,512]{1,0:T(8,128)(2,1)}, bf16[128,512]{1,0:T(8,128)(2,1)S(1)}, u32[]{:S(2)}, u32[]{:S(2)}) collective-permute-start(bf16[128,512]{1,0:T(8,128)(2,1)} %refs_0_.1), channel_id=1, source_target_pairs={{0,4},{1,5},{2,6},{3,7},{4,8},{5,9},{6,10},{7,11},{8,12},{9,13},{1... | collective-permute-start | bytes 393224 | tf_op jit(solution)/shard_map/ppermute | solution.py:146
  5.3 0.0 copy-done
  5.3 0.0 copy-done.2
  5.3 0.0 copy-start.1
  5.3 0.7 %shard_map.69 = (f32[128,512]{1,0:T(8,128)S(1)}, f32[128,1]{1,0:T(8,128)S(1)}, bf16[128,512]{1,0:T(8,128)(2,1)S(1)}) custom-call(f32[8,128]{1,0:T(8,128)S(1)} %shard_map.68.after_ref, bf16[128,3072]{1,0:T(8,128)(2,1)S(1)} %copy-done.2, bf16[3072,512]{1,0:T(8,128)(2,1)S(1)} %copy-done), custom_call_target="tpu_custom_call" | custom-call | flops 402653184 | bytes 3932160 | tf_op jit(solution)/shard_map/pallas_call | solution.py:158
  6.0 1.6 %collective-permute-start.2 = (bf16[128,512]{1,0:T(8,128)(2,1)S(1)}, bf16[128,512]{1,0:T(8,128)(2,1)S(1)}, u32[]{:S(2)}, u32[]{:S(2)}) collective-permute-start(bf16[128,512]{1,0:T(8,128)(2,1)S(1)} %get-tuple-element.12.refs_2_), channel_id=1, source_target_pairs={{0,2},{1,3},{2,0},{3,1},{4,5},{5,4},{6,7},{7,6},{8,10},{9,11},{10,... | collective-permute-start | bytes 393224 | tf_op jit(solution)/shard_map/ppermute | solution.py:146
  7.6 1.5 %collective-permute-start.6 = (bf16[128,512]{1,0:T(8,128)(2,1)S(1)}, bf16[128,512]{1,0:T(8,128)(2,1)S(1)}, u32[]{:S(2)}, u32[]{:S(2)}) collective-permute-start(bf16[128,512]{1,0:T(8,128)(2,1)S(1)} %get-tuple-element.12.refs_2_), channel_id=1, source_target_pairs={{0,29},{1,28},{2,31},{3,30},{4,2},{5,3},{6,0},{7,1},{8,5},{9,4},{1... | collective-permute-start | bytes 393224 | tf_op jit(solution)/shard_map/ppermute | solution.py:146
  10.5 0.5 %collective-permute-done.text_ref.refs_0_ = bf16[128,512]{1,0:T(8,128)(2,1)S(1)} collective-permute-done((bf16[128,512]{1,0:T(8,128)(2,1)}, bf16[128,512]{1,0:T(8,128)(2,1)S(1)}, u32[]{:S(2)}, u32[]{:S(2)}) %collective-permute-start) | collective-permute-done | bytes 131104 | tf_op jit(solution)/shard_map/ppermute | solution.py:146
  11.0 0.7 %collective-permute-start.5 = (bf16[128,512]{1,0:T(8,128)(2,1)S(1)}, bf16[128,512]{1,0:T(8,128)(2,1)S(1)}, u32[]{:S(2)}, u32[]{:S(2)}) collective-permute-start(bf16[128,512]{1,0:T(8,128)(2,1)S(1)} %get-tuple-element.12.refs_2_), channel_id=1, source_target_pairs={{0,28},{1,29},{2,30},{3,31},{4,0},{5,1},{6,2},{7,3},{8,4},{9,5},{1... | collective-permute-start | bytes 393224 | tf_op jit(solution)/shard_map/ppermute | solution.py:146
  11.7 0.1 iota.7.after_ref.scalar_ref
  11.7 0.1 shard_map.70.after_ref.refs_6_
  11.8 0.0 collective-permute-done.1.text_ref.refs_1_
  11.9 0.1 shard_map.71.refs_7_
  12.0 0.0 collective-permute-done.3.refs_5_.refs_1_
  12.0 0.0 collective-permute-done.2.refs_3_
  12.0 0.0 copy-done.1
  12.0 0.7 %shard_map.72 = (f32[128,512]{1,0:T(8,128)S(1)}, bf16[128,512]{1,0:T(8,128)(2,1)S(1)}) custom-call(f32[8,128]{1,0:T(8,128)S(1)} %iota.7.after_ref.scalar_ref, bf16[128,512]{1,0:T(8,128)(2,1)S(1)} %collective-permute-done.text_ref.refs_0_, bf16[128,512]{1,0:T(8,128)(2,1)S(1)} %collective-permute-done.1.text_ref.refs_1_, ...), custom_call_target="tpu_custom_call" | custom-call | flops 268435456 | bytes 1310720 | tf_op jit(solution)/shard_map/pallas_call | solution.py:183
  12.7 2.0 %collective-permute-start.4 = (bf16[128,512]{1,0:T(8,128)(2,1)S(1)}, bf16[128,512]{1,0:T(8,128)(2,1)S(1)}, u32[]{:S(2)}, u32[]{:S(2)}) collective-permute-start(bf16[128,512]{1,0:T(8,128)(2,1)S(1)} %get-tuple-element.16), channel_id=1, source_target_pairs={{0,2},{1,3},{2,0},{3,1},{4,5},{5,4},{6,7},{7,6},{8,10},{9,11},{10,... | collective-permute-start | bytes 393224 | tf_op jit(solution)/shard_map/ppermute | solution.py:146
  14.6 0.0 collective-permute-done.6.refs_5_
  14.6 0.0 collective-permute-done.5.refs_4_
  14.6 0.7 %shard_map.74 = (f32[128,512]{1,0:T(8,128)S(1)}, bf16[128,512]{1,0:T(8,128)(2,1)S(1)}) custom-call(f32[8,128]{1,0:T(8,128)S(1)} %iota.7.after_ref.scalar_ref, f32[128,512]{1,0:T(8,128)S(1)} %get-tuple-element.13.grad_ref.after_ref, bf16[128,512]{1,0:T(8,128)(2,1)S(1)} %copy-done.1, bf16[128,512]{1,0:T(8,128)(2,1)S(1)} %collective-permute-done.3.refs_5_.refs_1_, ...), custom_call_target="tpu_custom_call" | custom-call | flops 268435456 | bytes 1310720 | tf_op jit(solution)/shard_map/pallas_call | solution.py:194
  15.3 1.6 %collective-permute-start.7 = (bf16[128,512]{1,0:T(8,128)(2,1)S(1)}, bf16[128,512]{1,0:T(8,128)(2,1)S(1)}, u32[]{:S(2)}, u32[]{:S(2)}) collective-permute-start(bf16[128,512]{1,0:T(8,128)(2,1)S(1)} %get-tuple-element.21), channel_id=1, source_target_pairs={{0,1},{1,0},{2,3},{3,2},{4,6},{5,7},{6,4},{7,5},{8,9},{9,8},{10,11... | collective-permute-start | bytes 393224 | tf_op jit(solution)/shard_map/ppermute | solution.py:146
  16.9 0.8 %collective-permute-done.4.refs_0_ = bf16[128,512]{1,0:T(8,128)(2,1)S(1)} collective-permute-done((bf16[128,512]{1,0:T(8,128)(2,1)S(1)}, bf16[128,512]{1,0:T(8,128)(2,1)S(1)}, u32[]{:S(2)}, u32[]{:S(2)}) %collective-permute-start.4) | collective-permute-done | bytes 131104 | tf_op jit(solution)/shard_map/ppermute | solution.py:146
  17.7 2.0 %shard_map.73 = (f32[128,3072]{1,0:T(8,128)}, f32[128,512]{1,0:T(8,128)S(1)}, f32[128,1]{1,0:T(8,128)S(1)}) custom-call(f32[128,512]{1,0:T(8,128)S(1)} %get-tuple-element.13.grad_ref.after_ref, f32[128,512]{1,0:T(8,128)S(1)} %get-tuple-element.14.unit_ref, f32[128,1]{1,0:T(8,128)S(1)} %get-tuple-element.15.inv_ref, bf16[3072,512]{1,0:T(8,128)(2,1)S(1)} %copy-done, ...), custom_call_target="tpu_custom_call" | custom-call | flops 402653184 | bytes 7864320 | tf_op jit(solution)/shard_map/pallas_call | solution.py:205
  19.7 0.6 %collective-permute-done.7.refs_0_ = bf16[128,512]{1,0:T(8,128)(2,1)S(1)} collective-permute-done((bf16[128,512]{1,0:T(8,128)(2,1)S(1)}, bf16[128,512]{1,0:T(8,128)(2,1)S(1)}, u32[]{:S(2)}, u32[]{:S(2)}) %collective-permute-start.7) | collective-permute-done | bytes 131104 | tf_op jit(solution)/shard_map/ppermute | solution.py:146
  20.3 0.9 %shard_map.75 = f32[128,512]{1,0:T(8,128)} custom-call(f32[128,512]{1,0:T(8,128)S(1)} %get-tuple-element.18.grad_ref, f32[128,512]{1,0:T(8,128)S(1)} %get-tuple-element.19.unit_ref, f32[128,1]{1,0:T(8,128)S(1)} %get-tuple-element.20.inv_ref, bf16[128,512]{1,0:T(8,128)(2,1)S(1)} %collective-permute-done.7.refs_0_), custom_call_target="tpu_custom_call" | custom-call | flops 524288 | bytes 786432 | tf_op jit(solution)/shard_map/pallas_call | solution.py:215
  (2 shorter events, 0.0 us)
Async XLA Ops:
  0.6 4.7 %copy-start = (bf16[3072,512]{1,0:T(8,128)(2,1)S(1)}, bf16[3072,512]{1,0:T(8,128)(2,1)}, u32[]{:S(2)}) copy-start(bf16[3072,512]{1,0:T(8,128)(2,1)} %head_ref.3) | copy-start | bytes 9437188
  0.6 4.7 %copy-start.2 = (bf16[128,3072]{1,0:T(8,128)(2,1)S(1)}, bf16[128,3072]{1,0:T(8,128)(2,1)}, u32[]{:S(2)}) copy-start(bf16[128,3072]{1,0:T(8,128)(2,1)} %img_ref.1) | copy-start | bytes 2359300
  0.6 11.3 %collective-permute-start.3 = (bf16[128,512]{1,0:T(8,128)(2,1)}, bf16[128,512]{1,0:T(8,128)(2,1)S(1)}, u32[]{:S(2)}, u32[]{:S(2)}) collective-permute-start(bf16[128,512]{1,0:T(8,128)(2,1)} %refs_0_.1), channel_id=1, source_target_pairs={{0,1},{1,0},{2,3},{3,2},{4,6},{5,7},{6,4},{7,5},{8,9},{9,8},{10,11... | collective-permute-start | bytes 393224 | tf_op jit(solution)/shard_map/ppermute | solution.py:146
  3.7 8.2 %collective-permute-start.1 = (bf16[128,512]{1,0:T(8,128)(2,1)}, bf16[128,512]{1,0:T(8,128)(2,1)S(1)}, u32[]{:S(2)}, u32[]{:S(2)}) collective-permute-start(bf16[128,512]{1,0:T(8,128)(2,1)} %refs_0_.1), channel_id=1, source_target_pairs={{0,6},{1,7},{2,4},{3,5},{4,9},{5,8},{6,11},{7,10},{8,14},{9,15},{1... | collective-permute-start | bytes 393224 | tf_op jit(solution)/shard_map/ppermute | solution.py:146
  3.7 7.3 %collective-permute-start = (bf16[128,512]{1,0:T(8,128)(2,1)}, bf16[128,512]{1,0:T(8,128)(2,1)S(1)}, u32[]{:S(2)}, u32[]{:S(2)}) collective-permute-start(bf16[128,512]{1,0:T(8,128)(2,1)} %refs_0_.1), channel_id=1, source_target_pairs={{0,4},{1,5},{2,6},{3,7},{4,8},{5,9},{6,10},{7,11},{8,12},{9,13},{1... | collective-permute-start | bytes 393224 | tf_op jit(solution)/shard_map/ppermute | solution.py:146
  5.3 6.7 %copy-start.1 = (bf16[128,512]{1,0:T(8,128)(2,1)S(1)}, bf16[128,512]{1,0:T(8,128)(2,1)}, u32[]{:S(2)}) copy-start(bf16[128,512]{1,0:T(8,128)(2,1)} %refs_0_.1) | copy-start | bytes 393220
  6.0 6.0 %collective-permute-start.2 = (bf16[128,512]{1,0:T(8,128)(2,1)S(1)}, bf16[128,512]{1,0:T(8,128)(2,1)S(1)}, u32[]{:S(2)}, u32[]{:S(2)}) collective-permute-start(bf16[128,512]{1,0:T(8,128)(2,1)S(1)} %get-tuple-element.12.refs_2_), channel_id=1, source_target_pairs={{0,2},{1,3},{2,0},{3,1},{4,5},{5,4},{6,7},{7,6},{8,10},{9,11},{10,... | collective-permute-start | bytes 393224 | tf_op jit(solution)/shard_map/ppermute | solution.py:146
  7.6 7.0 %collective-permute-start.6 = (bf16[128,512]{1,0:T(8,128)(2,1)S(1)}, bf16[128,512]{1,0:T(8,128)(2,1)S(1)}, u32[]{:S(2)}, u32[]{:S(2)}) collective-permute-start(bf16[128,512]{1,0:T(8,128)(2,1)S(1)} %get-tuple-element.12.refs_2_), channel_id=1, source_target_pairs={{0,29},{1,28},{2,31},{3,30},{4,2},{5,3},{6,0},{7,1},{8,5},{9,4},{1... | collective-permute-start | bytes 393224 | tf_op jit(solution)/shard_map/ppermute | solution.py:146
  11.0 3.6 %collective-permute-start.5 = (bf16[128,512]{1,0:T(8,128)(2,1)S(1)}, bf16[128,512]{1,0:T(8,128)(2,1)S(1)}, u32[]{:S(2)}, u32[]{:S(2)}) collective-permute-start(bf16[128,512]{1,0:T(8,128)(2,1)S(1)} %get-tuple-element.12.refs_2_), channel_id=1, source_target_pairs={{0,28},{1,29},{2,30},{3,31},{4,0},{5,1},{6,2},{7,3},{8,4},{9,5},{1... | collective-permute-start | bytes 393224 | tf_op jit(solution)/shard_map/ppermute | solution.py:146
  12.7 5.0 %collective-permute-start.4 = (bf16[128,512]{1,0:T(8,128)(2,1)S(1)}, bf16[128,512]{1,0:T(8,128)(2,1)S(1)}, u32[]{:S(2)}, u32[]{:S(2)}) collective-permute-start(bf16[128,512]{1,0:T(8,128)(2,1)S(1)} %get-tuple-element.16), channel_id=1, source_target_pairs={{0,2},{1,3},{2,0},{3,1},{4,5},{5,4},{6,7},{7,6},{8,10},{9,11},{10,... | collective-permute-start | bytes 393224 | tf_op jit(solution)/shard_map/ppermute | solution.py:146
  15.3 5.0 %collective-permute-start.7 = (bf16[128,512]{1,0:T(8,128)(2,1)S(1)}, bf16[128,512]{1,0:T(8,128)(2,1)S(1)}, u32[]{:S(2)}, u32[]{:S(2)}) collective-permute-start(bf16[128,512]{1,0:T(8,128)(2,1)S(1)} %get-tuple-element.21), channel_id=1, source_target_pairs={{0,1},{1,0},{2,3},{3,2},{4,6},{5,7},{6,4},{7,5},{8,9},{9,8},{10,11... | collective-permute-start | bytes 393224 | tf_op jit(solution)/shard_map/ppermute | solution.py:146

commit v8 on v6

--- a/solution.py
+++ b/solution.py
@@ -71,7 +71,7 @@
     meet(scalar_ref, images, texts, weight_ref, grad_ref, term_refs)
 
 
-def text_kernel(n_row, n_image, scalar_ref, after_ref, *refs):
+def text_kernel(n_row, n_image, scalar_ref, *refs):
     text_refs, refs = refs[:n_row], refs[n_row:]
     image_refs, refs = refs[:n_image], refs[n_image:]
     (grad_ref, *term_refs), weight_ref = refs[:-1], refs[-1]
@@ -196,10 +196,10 @@
         8 * n_col * n_row * rows * rows * emb,
         2 * rows * emb * (2 * n_col + 3 * n_row),
         out_shape=(grad_piece,) + (low_piece,) * (n_row - 1),
-        in_specs=[VMEM, ANY] + [VMEM] * (n_row + 2 * n_col),
+        in_specs=[VMEM] * (1 + n_row + 2 * n_col),
         out_specs=(VMEM,) * n_row,
         scratch_shapes=[pltpu.VMEM((n_row * rows, 2 * n_col * rows), BF16)],
-    )(scalars, grad_img, *texts, *images, *later_images)
+    )(scalars, *texts, *images, *later_images)
     txt_peers = [send(term, False, 0, -k) for k, term in enumerate(txt_terms, 1)]
 
     d_feat, txt_unit, txt_inv = kernel(

time: 21.3 us -> 21.4 us (level)
  no operation moved by 1% of the time
where the time goes in v8:
time: 21.4 us; the launch traced here: 21.2 us
  starting transfers between devices  12 us (56%)
  Pallas kernels  5.01 us (23%)
  between operations  2.06 us (10%)
  waiting for transfers between devices  2.05 us (10%)
    ppermute x8, starting transfers between devices, send(): return lax.ppermute(piece, ('blk', 'group'), route(image_side, distance, k))  12 us
    ppermute x8, waiting for transfers between devices, send(): return lax.ppermute(piece, ('blk', 'group'), route(image_side, distance, k))  2.05 us
    pallas_call x1, Pallas kernels, body(): kernel(feat_kernel, 2 * rows * width * emb, 4 * width * (rows + emb), out...  1.94 us
    pallas_call x1, Pallas kernels, body(): kernel(text_out_kernel, 8 * rows * emb, 12 * rows * emb, out_shape=shape(...  0.86 us
    pallas_call x1, Pallas kernels, body(): kernel(functools.partial(text_kernel, n_row, 2 * n_col), 8 * n_col * n_ro...  0.67 us
    pallas_call x1, Pallas kernels, body(): kernel(project_kernel, 2 * rows * width * emb, 2 * width * (rows + emb),...  0.67 us
    pallas_call x1, Pallas kernels, body(): kernel(functools.partial(image_kernel, n_col, n_row), 8 * n_col * n_row *...  0.65 us
  transfers between devices with their start and end apart: 8, of which 3 were waited for; matrix products, arithmetic and copies ran while one was open for 0% of the time, Pallas kernels for 20%

profile of v8, /device:TPU:0, one launch (start us, length us, event | category | flops | bytes accessed | tf_op | source)
XLA Modules:
  0.0 21.2 jit_solution(15403467291136766064)
XLA Ops:
  0.6 0.0 copy-start
  0.6 0.0 copy-start.1
  0.6 3.0 %collective-permute-start.3 = (bf16[128,512]{1,0:T(8,128)(2,1)}, bf16[128,512]{1,0:T(8,128)(2,1)S(1)}, u32[]{:S(2)}, u32[]{:S(2)}) collective-permute-start(bf16[128,512]{1,0:T(8,128)(2,1)} %refs_0_.1), channel_id=1, source_target_pairs={{0,1},{1,0},{2,3},{3,2},{4,6},{5,7},{6,4},{7,5},{8,9},{9,8},{10,11... | collective-permute-start | bytes 393224 | tf_op jit(solution)/shard_map/ppermute | solution.py:146
  3.7 0.0 collective-permute-start.1
  3.7 1.7 %collective-permute-start = (bf16[128,512]{1,0:T(8,128)(2,1)}, bf16[128,512]{1,0:T(8,128)(2,1)S(1)}, u32[]{:S(2)}, u32[]{:S(2)}) collective-permute-start(bf16[128,512]{1,0:T(8,128)(2,1)} %refs_0_.1), channel_id=1, source_target_pairs={{0,4},{1,5},{2,6},{3,7},{4,8},{5,9},{6,10},{7,11},{8,12},{9,13},{1... | collective-permute-start | bytes 393224 | tf_op jit(solution)/shard_map/ppermute | solution.py:146
  5.3 0.0 copy-done
  5.3 0.0 copy-done.1
  5.3 0.0 copy-start.2
  5.3 0.7 %shard_map.69 = (f32[128,512]{1,0:T(8,128)S(1)}, f32[128,1]{1,0:T(8,128)S(1)}, bf16[128,512]{1,0:T(8,128)(2,1)S(1)}) custom-call(f32[8,128]{1,0:T(8,128)S(1)} %shard_map.68.after_ref, bf16[128,3072]{1,0:T(8,128)(2,1)S(1)} %copy-done.1, bf16[3072,512]{1,0:T(8,128)(2,1)S(1)} %copy-done), custom_call_target="tpu_custom_call" | custom-call | flops 402653184 | bytes 3932160 | tf_op jit(solution)/shard_map/pallas_call | solution.py:158
  6.0 1.6 %collective-permute-start.2 = (bf16[128,512]{1,0:T(8,128)(2,1)S(1)}, bf16[128,512]{1,0:T(8,128)(2,1)S(1)}, u32[]{:S(2)}, u32[]{:S(2)}) collective-permute-start(bf16[128,512]{1,0:T(8,128)(2,1)S(1)} %get-tuple-element.12.refs_2_), channel_id=1, source_target_pairs={{0,2},{1,3},{2,0},{3,1},{4,5},{5,4},{6,7},{7,6},{8,10},{9,11},{10,... | collective-permute-start | bytes 393224 | tf_op jit(solution)/shard_map/ppermute | solution.py:146
  7.6 1.5 %collective-permute-start.6 = (bf16[128,512]{1,0:T(8,128)(2,1)S(1)}, bf16[128,512]{1,0:T(8,128)(2,1)S(1)}, u32[]{:S(2)}, u32[]{:S(2)}) collective-permute-start(bf16[128,512]{1,0:T(8,128)(2,1)S(1)} %get-tuple-element.12.refs_2_), channel_id=1, source_target_pairs={{0,29},{1,28},{2,31},{3,30},{4,2},{5,3},{6,0},{7,1},{8,5},{9,4},{1... | collective-permute-start | bytes 393224 | tf_op jit(solution)/shard_map/ppermute | solution.py:146
  10.5 0.5 %collective-permute-done.text_ref.refs_0_ = bf16[128,512]{1,0:T(8,128)(2,1)S(1)} collective-permute-done((bf16[128,512]{1,0:T(8,128)(2,1)}, bf16[128,512]{1,0:T(8,128)(2,1)S(1)}, u32[]{:S(2)}, u32[]{:S(2)}) %collective-permute-start) | collective-permute-done | bytes 131104 | tf_op jit(solution)/shard_map/ppermute | solution.py:146
  11.0 0.7 %collective-permute-start.5 = (bf16[128,512]{1,0:T(8,128)(2,1)S(1)}, bf16[128,512]{1,0:T(8,128)(2,1)S(1)}, u32[]{:S(2)}, u32[]{:S(2)}) collective-permute-start(bf16[128,512]{1,0:T(8,128)(2,1)S(1)} %get-tuple-element.12.refs_2_), channel_id=1, source_target_pairs={{0,28},{1,29},{2,30},{3,31},{4,0},{5,1},{6,2},{7,3},{8,4},{9,5},{1... | collective-permute-start | bytes 393224 | tf_op jit(solution)/shard_map/ppermute | solution.py:146
  11.7 0.1 iota.7.after_ref.scalar_ref
  11.7 0.1 shard_map.70.after_ref.refs_6_
  11.8 0.0 collective-permute-done.1.text_ref.refs_1_
  11.9 0.1 shard_map.71.refs_7_
  12.0 0.0 collective-permute-done.3.refs_5_.refs_1_
  12.0 0.0 collective-permute-done.2.refs_3_
  12.0 0.0 copy-done.2
  12.0 0.7 %shard_map.72 = (f32[128,512]{1,0:T(8,128)S(1)}, bf16[128,512]{1,0:T(8,128)(2,1)S(1)}) custom-call(f32[8,128]{1,0:T(8,128)S(1)} %iota.7.after_ref.scalar_ref, bf16[128,512]{1,0:T(8,128)(2,1)S(1)} %collective-permute-done.text_ref.refs_0_, bf16[128,512]{1,0:T(8,128)(2,1)S(1)} %collective-permute-done.1.text_ref.refs_1_, ...), custom_call_target="tpu_custom_call" | custom-call | flops 268435456 | bytes 1310720 | tf_op jit(solution)/shard_map/pallas_call | solution.py:183
  12.7 2.0 %collective-permute-start.4 = (bf16[128,512]{1,0:T(8,128)(2,1)S(1)}, bf16[128,512]{1,0:T(8,128)(2,1)S(1)}, u32[]{:S(2)}, u32[]{:S(2)}) collective-permute-start(bf16[128,512]{1,0:T(8,128)(2,1)S(1)} %get-tuple-element.16), channel_id=1, source_target_pairs={{0,2},{1,3},{2,0},{3,1},{4,5},{5,4},{6,7},{7,6},{8,10},{9,11},{10,... | collective-permute-start | bytes 393224 | tf_op jit(solution)/shard_map/ppermute | solution.py:146
  14.6 0.0 collective-permute-done.6.refs_5_
  14.6 0.0 collective-permute-done.5.refs_4_
  14.6 0.7 %shard_map.74 = (f32[128,512]{1,0:T(8,128)S(1)}, bf16[128,512]{1,0:T(8,128)(2,1)S(1)}) custom-call(f32[8,128]{1,0:T(8,128)S(1)} %iota.7.after_ref.scalar_ref, bf16[128,512]{1,0:T(8,128)(2,1)S(1)} %copy-done.2, bf16[128,512]{1,0:T(8,128)(2,1)S(1)} %collective-permute-done.3.refs_5_.refs_1_, bf16[128,512]{1,0:T(8,128)(2,1)S(1)} %get-tuple-element.12.refs_2_, ...), custom_call_target="tpu_custom_call" | custom-call | flops 268435456 | bytes 1310720 | tf_op jit(solution)/shard_map/pallas_call | solution.py:194
  15.3 1.6 %collective-permute-start.7 = (bf16[128,512]{1,0:T(8,128)(2,1)S(1)}, bf16[128,512]{1,0:T(8,128)(2,1)S(1)}, u32[]{:S(2)}, u32[]{:S(2)}) collective-permute-start(bf16[128,512]{1,0:T(8,128)(2,1)S(1)} %get-tuple-element.21), channel_id=1, source_target_pairs={{0,1},{1,0},{2,3},{3,2},{4,6},{5,7},{6,4},{7,5},{8,9},{9,8},{10,11... | collective-permute-start | bytes 393224 | tf_op jit(solution)/shard_map/ppermute | solution.py:146
  16.9 0.8 %collective-permute-done.4.refs_0_ = bf16[128,512]{1,0:T(8,128)(2,1)S(1)} collective-permute-done((bf16[128,512]{1,0:T(8,128)(2,1)S(1)}, bf16[128,512]{1,0:T(8,128)(2,1)S(1)}, u32[]{:S(2)}, u32[]{:S(2)}) %collective-permute-start.4) | collective-permute-done | bytes 131104 | tf_op jit(solution)/shard_map/ppermute | solution.py:146
  17.7 1.9 %shard_map.73 = (f32[128,3072]{1,0:T(8,128)}, f32[128,512]{1,0:T(8,128)S(1)}, f32[128,1]{1,0:T(8,128)S(1)}) custom-call(f32[128,512]{1,0:T(8,128)S(1)} %get-tuple-element.13.grad_ref, f32[128,512]{1,0:T(8,128)S(1)} %get-tuple-element.14.unit_ref, f32[128,1]{1,0:T(8,128)S(1)} %get-tuple-element.15.inv_ref, bf16[3072,512]{1,0:T(8,128)(2,1)S(1)} %copy-done, ...), custom_call_target="tpu_custom_call" | custom-call | flops 402653184 | bytes 7864320 | tf_op jit(solution)/shard_map/pallas_call | solution.py:205
  19.6 0.7 %collective-permute-done.7.refs_0_ = bf16[128,512]{1,0:T(8,128)(2,1)S(1)} collective-permute-done((bf16[128,512]{1,0:T(8,128)(2,1)S(1)}, bf16[128,512]{1,0:T(8,128)(2,1)S(1)}, u32[]{:S(2)}, u32[]{:S(2)}) %collective-permute-start.7) | collective-permute-done | bytes 131104 | tf_op jit(solution)/shard_map/ppermute | solution.py:146
  20.3 0.9 %shard_map.75 = f32[128,512]{1,0:T(8,128)} custom-call(f32[128,512]{1,0:T(8,128)S(1)} %get-tuple-element.18.grad_ref, f32[128,512]{1,0:T(8,128)S(1)} %get-tuple-element.19.unit_ref, f32[128,1]{1,0:T(8,128)S(1)} %get-tuple-element.20.inv_ref, bf16[128,512]{1,0:T(8,128)(2,1)S(1)} %collective-permute-done.7.refs_0_), custom_call_target="tpu_custom_call" | custom-call | flops 524288 | bytes 786432 | tf_op jit(solution)/shard_map/pallas_call | solution.py:215
  (2 shorter events, 0.0 us)
Async XLA Ops:
  0.6 4.7 %copy-start = (bf16[3072,512]{1,0:T(8,128)(2,1)S(1)}, bf16[3072,512]{1,0:T(8,128)(2,1)}, u32[]{:S(2)}) copy-start(bf16[3072,512]{1,0:T(8,128)(2,1)} %head_ref.3) | copy-start | bytes 9437188
  0.6 4.7 %copy-start.1 = (bf16[128,3072]{1,0:T(8,128)(2,1)S(1)}, bf16[128,3072]{1,0:T(8,128)(2,1)}, u32[]{:S(2)}) copy-start(bf16[128,3072]{1,0:T(8,128)(2,1)} %img_ref.1) | copy-start | bytes 2359300
  0.6 11.3 %collective-permute-start.3 = (bf16[128,512]{1,0:T(8,128)(2,1)}, bf16[128,512]{1,0:T(8,128)(2,1)S(1)}, u32[]{:S(2)}, u32[]{:S(2)}) collective-permute-start(bf16[128,512]{1,0:T(8,128)(2,1)} %refs_0_.1), channel_id=1, source_target_pairs={{0,1},{1,0},{2,3},{3,2},{4,6},{5,7},{6,4},{7,5},{8,9},{9,8},{10,11... | collective-permute-start | bytes 393224 | tf_op jit(solution)/shard_map/ppermute | solution.py:146
  3.7 8.2 %collective-permute-start.1 = (bf16[128,512]{1,0:T(8,128)(2,1)}, bf16[128,512]{1,0:T(8,128)(2,1)S(1)}, u32[]{:S(2)}, u32[]{:S(2)}) collective-permute-start(bf16[128,512]{1,0:T(8,128)(2,1)} %refs_0_.1), channel_id=1, source_target_pairs={{0,6},{1,7},{2,4},{3,5},{4,9},{5,8},{6,11},{7,10},{8,14},{9,15},{1... | collective-permute-start | bytes 393224 | tf_op jit(solution)/shard_map/ppermute | solution.py:146
  3.7 7.3 %collective-permute-start = (bf16[128,512]{1,0:T(8,128)(2,1)}, bf16[128,512]{1,0:T(8,128)(2,1)S(1)}, u32[]{:S(2)}, u32[]{:S(2)}) collective-permute-start(bf16[128,512]{1,0:T(8,128)(2,1)} %refs_0_.1), channel_id=1, source_target_pairs={{0,4},{1,5},{2,6},{3,7},{4,8},{5,9},{6,10},{7,11},{8,12},{9,13},{1... | collective-permute-start | bytes 393224 | tf_op jit(solution)/shard_map/ppermute | solution.py:146
  5.3 6.7 %copy-start.2 = (bf16[128,512]{1,0:T(8,128)(2,1)S(1)}, bf16[128,512]{1,0:T(8,128)(2,1)}, u32[]{:S(2)}) copy-start(bf16[128,512]{1,0:T(8,128)(2,1)} %refs_0_.1) | copy-start | bytes 393220
  6.0 6.0 %collective-permute-start.2 = (bf16[128,512]{1,0:T(8,128)(2,1)S(1)}, bf16[128,512]{1,0:T(8,128)(2,1)S(1)}, u32[]{:S(2)}, u32[]{:S(2)}) collective-permute-start(bf16[128,512]{1,0:T(8,128)(2,1)S(1)} %get-tuple-element.12.refs_2_), channel_id=1, source_target_pairs={{0,2},{1,3},{2,0},{3,1},{4,5},{5,4},{6,7},{7,6},{8,10},{9,11},{10,... | collective-permute-start | bytes 393224 | tf_op jit(solution)/shard_map/ppermute | solution.py:146
  7.6 7.0 %collective-permute-start.6 = (bf16[128,512]{1,0:T(8,128)(2,1)S(1)}, bf16[128,512]{1,0:T(8,128)(2,1)S(1)}, u32[]{:S(2)}, u32[]{:S(2)}) collective-permute-start(bf16[128,512]{1,0:T(8,128)(2,1)S(1)} %get-tuple-element.12.refs_2_), channel_id=1, source_target_pairs={{0,29},{1,28},{2,31},{3,30},{4,2},{5,3},{6,0},{7,1},{8,5},{9,4},{1... | collective-permute-start | bytes 393224 | tf_op jit(solution)/shard_map/ppermute | solution.py:146
  11.0 3.6 %collective-permute-start.5 = (bf16[128,512]{1,0:T(8,128)(2,1)S(1)}, bf16[128,512]{1,0:T(8,128)(2,1)S(1)}, u32[]{:S(2)}, u32[]{:S(2)}) collective-permute-start(bf16[128,512]{1,0:T(8,128)(2,1)S(1)} %get-tuple-element.12.refs_2_), channel_id=1, source_target_pairs={{0,28},{1,29},{2,30},{3,31},{4,0},{5,1},{6,2},{7,3},{8,4},{9,5},{1... | collective-permute-start | bytes 393224 | tf_op jit(solution)/shard_map/ppermute | solution.py:146
  12.7 5.0 %collective-permute-start.4 = (bf16[128,512]{1,0:T(8,128)(2,1)S(1)}, bf16[128,512]{1,0:T(8,128)(2,1)S(1)}, u32[]{:S(2)}, u32[]{:S(2)}) collective-permute-start(bf16[128,512]{1,0:T(8,128)(2,1)S(1)} %get-tuple-element.16), channel_id=1, source_target_pairs={{0,2},{1,3},{2,0},{3,1},{4,5},{5,4},{6,7},{7,6},{8,10},{9,11},{10,... | collective-permute-start | bytes 393224 | tf_op jit(solution)/shard_map/ppermute | solution.py:146
  15.3 5.0 %collective-permute-start.7 = (bf16[128,512]{1,0:T(8,128)(2,1)S(1)}, bf16[128,512]{1,0:T(8,128)(2,1)S(1)}, u32[]{:S(2)}, u32[]{:S(2)}) collective-permute-start(bf16[128,512]{1,0:T(8,128)(2,1)S(1)} %get-tuple-element.21), channel_id=1, source_target_pairs={{0,1},{1,0},{2,3},{3,2},{4,6},{5,7},{6,4},{7,5},{8,9},{9,8},{10,11... | collective-permute-start | bytes 393224 | tf_op jit(solution)/shard_map/ppermute | solution.py:146
